TPU v7x, 32 devices: a whole 2x2x4 slice. The times are simulated.
32 devices in a mesh: blk: 8 (over z, x), col: 4 (over y, core).
Axes of the slice: x: 2, y: 2, z: 4, core: 2. Of those that a mesh axis runs over, the one named last changes fastest.
Arguments:
- upper_row: float32 [512, 8, 512], P(None, 'blk', 'col'), may hold values from -0.17 to 4.17, as said below
- lower_row: float32 [512, 8, 512], P(None, 'blk', 'col'), may hold values from -0.1 to 0.1
Outputs:
- new_upper: float32 [512, 8, 512], P(None, 'blk', 'col')
- new_lower: float32 [512, 8, 512], P(None, 'blk', 'col')
Inputs may be any that keep to these rules, and one draw needn't show every extreme that they name: Block 0 of upper_row is 4 times the identity plus entries within 0.16 of it; the other blocks hold entries within 0.1.
All inputs are finite; a program needn't handle non-finite values.
Results may differ from a plain program's by a relative error of at most 0.00023.
Values sent between devices are 32-bit elements; how exact they have to be, the bound alone decides.
No kernel may reach another device: no remote copies, remote signals or barrier semaphores. Data moves between devices by JAX's collectives and lax.ppermute only.
A program may use at most 64 MiB of HBM per device.

v0:
```python
import jax
import jax.numpy as jnp
from jax import lax
from jax.sharding import PartitionSpec as P

HIGHEST_PREC = lax.Precision.HIGHEST


def shifted(value, axis, steps):
    count = lax.axis_size(axis)
    initial, last = (max(0, -steps), min(count, count - steps))
    return lax.ppermute(value, axis, [(source, source + steps) for source in range(initial, last)])


def broadcast(block, axis, holder):
    block = jnp.where(lax.axis_index(axis) == holder, block, jnp.zeros_like(block))
    return lax.psum(block, axis)


def product(left_mat, right_mat):
    return jnp.dot(left_mat, right_mat, precision=HIGHEST_PREC, preferred_element_type=jnp.float32)


def apply_rows(matrix, blocks):
    return jnp.einsum(
        "ij,jkc->ikc", matrix, blocks, precision=HIGHEST_PREC, preferred_element_type=jnp.float32
    )


def apply_transposed(matrix, blocks):
    return jnp.einsum(
        "ri,rkc->ikc", matrix, blocks, precision=HIGHEST_PREC, preferred_element_type=jnp.float32
    )


def gram_of(reflect):
    return jnp.einsum(
        "ri,rj->ij", reflect, reflect, precision=HIGHEST_PREC, preferred_element_type=jnp.float32
    )


def slide_upper(upper_row):
    incoming = shifted(upper_row, "blk", 1)
    return jnp.concatenate([incoming, upper_row[:, :-1, :]], axis=1)


def first_inverse(head_upper, identity):
    norm_scale = jnp.sqrt(jnp.sum(head_upper * head_upper) / head_upper.shape[0] + 1e-06)
    return (2.0 * identity - head_upper / norm_scale) / norm_scale


def transform_whole(head_upper, head_lower):
    identity = jnp.eye(head_upper.shape[0], dtype=jnp.float32)
    inverse_one = first_inverse(head_upper, identity)
    inverse_two = product(inverse_one, 2.0 * identity - product(head_upper, inverse_one))
    reflect = product(head_lower, inverse_two)
    gram_matrix = gram_of(reflect)
    power_two = product(gram_matrix, gram_matrix)
    power_three = product(gram_matrix, power_two)
    power_four = product(gram_matrix, power_three)
    left_root = (
        identity
        + 0.5 * gram_matrix
        + 0.375 * power_two
        + 0.3125 * power_three
        + 0.0625 * power_four
    )
    inner_poly = 0.5 * identity + 0.375 * gram_matrix + 0.3125 * power_two + 0.0625 * power_three
    return (reflect, left_root, inner_poly)


def shards(upper_row, lower_row):
    blocks_here = upper_row.shape[1]
    root_index = 1 // blocks_here
    local_index = 1 % blocks_here
    upper_row = slide_upper(upper_row)
    lead_upper = broadcast(upper_row[:, local_index, :], "blk", root_index)
    lead_lower = broadcast(lower_row[:, local_index, :], "blk", root_index)
    head_upper = lax.all_gather(lead_upper, "col", axis=1, tiled=True)
    head_lower = lax.all_gather(lead_lower, "col", axis=1, tiled=True)
    reflect, left_root, inner_poly = transform_whole(head_upper, head_lower)
    mixed_rows = upper_row - apply_transposed(reflect, lower_row)
    residue = lower_row - apply_rows(reflect, upper_row)
    pulled = apply_transposed(reflect, residue)
    upper_row = apply_rows(left_root, mixed_rows)
    lower_row = residue + apply_rows(reflect, apply_rows(inner_poly, pulled))
    return (upper_row, lower_row)


def solution(mesh):
    return jax.shard_map(
        shards,
        mesh=mesh,
        in_specs=(P(None, "blk", "col"), P(None, "blk", "col")),
        out_specs=(P(None, "blk", "col"), P(None, "blk", "col")),
        check_vma=False,
    )
```

profile of v0, /device:TPU:0, one launch (start us, length us, event | category | flops | bytes accessed | tf_op | source)
XLA Modules:
  0.0 156.4 jit_solution(6102680298517803959)
XLA Ops:
  7.2 0.0 all-reduce.3.cloned.1.call-start
  7.2 4.9 %collective-permute-start = (f32[512,1,128]{2,0,1:T(8,128)}, f32[512,1,128]{2,0,1:T(8,128)S(1)}, u32[]{:S(2)}, u32[]{:S(2)}) collective-permute-start(f32[512,1,128]{2,0,1:T(8,128)} %bitcast.56), channel_id=1, source_target_pairs={{0,4},{4,8},{8,12},{12,16},{16,20},{20,24},{24,28},{1,5},{5,9},{9,... | collective-permute-start | bytes 786440 | tf_op jit(solution)/shard_map/ppermute | solution.py:12
  12.1 0.7 broadcast_select_fusion
  12.8 5.1 %collective-permute-done = f32[512,1,128]{2,0,1:T(8,128)S(1)} collective-permute-done((f32[512,1,128]{2,0,1:T(8,128)}, f32[512,1,128]{2,0,1:T(8,128)S(1)}, u32[]{:S(2)}, u32[]{:S(2)}) %collective-permute-start) | collective-permute-done | bytes 262176 | tf_op jit(solution)/shard_map/ppermute | solution.py:12
  17.9 0.7 bitcast_select_fusion
  18.6 0.0 all-reduce.3.cloned.1.call-update
  18.7 0.0 all-gather.5.cloned.1.call-start
  18.7 74.9 %all-reduce.3.cloned.1.call-done = (f32[512,128]{1,0:T(8,128)}, f32[512,128]{1,0:T(8,128)}) async-done(((f32[512,128]{1,0:T(8,128)}, f32[512,128]{1,0:T(8,128)}), (f32[512,128]{1,0:T(8,128)}, f32[512,128]{1,0:T(8,128)})) %all-reduce.3.cloned.1.call-update) | async-done | bytes 524304 | tf_op jit(solution)/shard_map/psum | solution.py:17
  93.6 0.0 all-gather.5.cloned.1.call-update
  93.6 0.0 all-gather.3.cloned.1.call-start
  93.6 0.7 all-gather.3.cloned.1.call-update
  94.3 16.9 %all-gather.5.cloned.1.call-done = f32[512,512]{1,0:T(8,128)} async-done(((f32[512,128]{1,0:T(8,128)}), f32[512,512]{1,0:T(8,128)}) %all-gather.5.cloned.1.call-update) | async-done | bytes 1048592 | tf_op jit(solution)/shard_map/all_gather | solution.py:79
  111.3 0.0 copy-start.1
  111.3 2.2 %multiply_reduce_fusion = f32[]{:T(128)} fusion(f32[512,512]{1,0:T(8,128)} %all-gather.5.cloned.1.call-done), kind=kLoop, calls=%fused_computation.20 | loop fusion | flops 524287 | bytes 1048580 | tf_op jit(solution)/shard_map/reduce_sum | solution.py:48
  114.2 0.0 copy-done.1
  114.2 1.9 %select_subtract_fusion = f32[512,512]{1,0:T(8,128)S(1)} fusion(f32[512,512]{1,0:T(8,128)S(1)} %copy-done.1, f32[]{:T(128)S(6)} %sqrt.3), kind=kOutput, calls=%fused_computation | convolution fusion | flops 1612709888 | bytes 2097156 | tf_op jit(solution)/shard_map/dot_general | solution.py:21
  116.1 2.0 %fusion.22 = f32[512,512]{1,0:T(8,128)S(1)} fusion(f32[512,512]{1,0:T(8,128)S(1)} %select_subtract_fusion, f32[512,512]{1,0:T(8,128)S(1)} %copy-done.1, f32[]{:T(128)S(6)} %sqrt.3), kind=kOutput, calls=%fused_computation.31 | convolution fusion | flops 1611923456 | bytes 3145732 | tf_op jit(solution)/shard_map/dot_general | solution.py:21
  118.1 11.7 %all-gather.3.cloned.1.call-done = f32[512,512]{1,0:T(8,128)} async-done(((f32[512,128]{1,0:T(8,128)}), f32[512,512]{1,0:T(8,128)}) %all-gather.3.cloned.1.call-update) | async-done | bytes 1048592 | tf_op jit(solution)/shard_map/all_gather | solution.py:80
  129.8 3.1 %fusion.34 = f32[512,512]{1,0:T(8,128)S(1)} fusion(f32[512,512]{1,0:T(8,128)} %all-gather.3.cloned.1.call-done, f32[512,512]{1,0:T(8,128)S(1)} %fusion.22), kind=kOutput, calls=%fused_computation.42 | convolution fusion | flops 1610612736 | bytes 3145728 | tf_op jit(solution)/shard_map/dot_general | solution.py:21
  132.9 0.0 copy-start
  132.9 1.9 %fusion.35 = f32[512,512]{1,0:T(8,128)S(1)} fusion(f32[512,512]{1,0:T(8,128)S(1)} %fusion.34), kind=kOutput, calls=%fused_computation.43 | convolution fusion | flops 1610612736 | bytes 2097152 | tf_op jit(solution)/shard_map/ri,rj->ij/dot_general | solution.py:37
  134.8 0.0 copy-done
  134.8 1.0 fusion.3
  135.8 1.8 %fusion.19 = f32[512,128]{1,0:T(8,128)S(1)} fusion(f32[512,512]{1,0:T(8,128)S(1)} %fusion.34, f32[512,1,128]{2,0,1:T(8,128)S(1)} %fusion.3), kind=kOutput, calls=%fused_computation.27 | convolution fusion | flops 402653184 | bytes 1572864 | tf_op jit(solution)/shard_map/ri,rkc->ikc/dot_general | solution.py:31
  137.6 1.9 %fusion.36 = f32[512,512]{1,0:T(8,128)S(1)} fusion(f32[512,512]{1,0:T(8,128)S(1)} %fusion.35), kind=kOutput, calls=%fused_computation.44 | convolution fusion | flops 1610612736 | bytes 2097152 | tf_op jit(solution)/shard_map/dot_general | solution.py:21
  139.5 2.0 %fusion.37 = f32[512,512]{1,0:T(8,128)S(1)} fusion(f32[512,512]{1,0:T(8,128)S(1)} %fusion.35, f32[512,512]{1,0:T(8,128)S(1)} %fusion.36), kind=kOutput, calls=%fused_computation.45 | convolution fusion | flops 1610612736 | bytes 3145728 | tf_op jit(solution)/shard_map/dot_general | solution.py:21
  141.6 2.0 %fusion = f32[512,512]{1,0:T(8,128)S(1)} fusion(f32[512,512]{1,0:T(8,128)S(1)} %fusion.35, f32[512,512]{1,0:T(8,128)S(1)} %fusion.37, f32[512,512]{1,0:T(8,128)S(1)} %fusion.36), kind=kOutput, calls=%fused_computation.3 | convolution fusion | flops 1613234176 | bytes 4194304 | tf_op jit(solution)/shard_map/dot_general | solution.py:21
  143.6 1.1 fusion.6
  144.7 1.7 %fusion.4 = f32[512,1,128]{2,0,1:T(8,128)} fusion(f32[512,1,128]{2,0,1:T(8,128)S(1)} %fusion.3, f32[512,512]{1,0:T(8,128)S(1)} %fusion.34, f32[512,128]{1,0:T(8,128)S(1)} %fusion.6), kind=kOutput, calls=%fused_computation.10 | convolution fusion | flops 402718720 | bytes 1835008 | tf_op jit(solution)/shard_map/ij,jkc->ikc/dot_general | solution.py:25
  146.4 1.8 %fusion.2 = f32[512,128]{1,0:T(8,128)S(1)} fusion(f32[512,1,128]{2,0,1:T(8,128)S(1)} %collective-permute-done, f32[512,512]{1,0:T(8,128)S(1)} %fusion.34, f32[512,128]{1,0:T(8,128)S(1)} %bitcast.53), kind=kOutput, calls=%fused_computation.8 | convolution fusion | flops 402718720 | bytes 1835008 | tf_op jit(solution)/shard_map/ri,rkc->ikc/dot_general | solution.py:31
  148.2 1.7 %fusion.38 = f32[512,128]{1,0:T(8,128)} fusion(f32[512,512]{1,0:T(8,128)S(1)} %fusion, f32[512,128]{1,0:T(8,128)S(1)} %fusion.2), kind=kOutput, calls=%fused_computation.46 | convolution fusion | flops 402653184 | bytes 1572864 | tf_op jit(solution)/shard_map/ij,jkc->ikc/dot_general | solution.py:25
Async XLA Ops:
  7.2 86.4 %all-reduce.3.cloned.1.call-start = ((), (), s32[]{:S(2)}) async-start(), calls=%async_computation.2 | async-start | bytes 1048576 | tf_op jit(solution)/shard_map/psum | solution.py:17
  7.2 10.7 %collective-permute-start = (f32[512,1,128]{2,0,1:T(8,128)}, f32[512,1,128]{2,0,1:T(8,128)S(1)}, u32[]{:S(2)}, u32[]{:S(2)}) collective-permute-start(f32[512,1,128]{2,0,1:T(8,128)} %bitcast.56), channel_id=1, source_target_pairs={{0,4},{4,8},{8,12},{12,16},{16,20},{20,24},{24,28},{1,5},{5,9},{9,... | collective-permute-start | bytes 786440 | tf_op jit(solution)/shard_map/ppermute | solution.py:12
  18.7 92.6 %all-gather.5.cloned.1.call-start = ((), (), s32[]{:S(2)}) async-start(), calls=%async_computation.1 | async-start | bytes 1310720 | tf_op jit(solution)/shard_map/all_gather | solution.py:79
  93.6 36.2 %all-gather.3.cloned.1.call-start = ((), (), s32[]{:S(2)}) async-start(), calls=%async_computation | async-start | bytes 1310720 | tf_op jit(solution)/shard_map/all_gather | solution.py:80
  111.3 2.9 %copy-start.1 = (f32[512,512]{1,0:T(8,128)S(1)}, f32[512,512]{1,0:T(8,128)}, u32[]{:S(2)}) copy-start(f32[512,512]{1,0:T(8,128)} %all-gather.5.cloned.1.call-done) | copy-start | bytes 3145732
  132.9 1.9 %copy-start = (f32[512,1,128]{2,1,0:T(1,128)S(1)}, f32[512,1,128]{2,1,0:T(1,128)}, u32[]{:S(2)}) copy-start(f32[512,1,128]{2,1,0:T(1,128)} %param.3) | copy-start | bytes 786436
Sparse Core Ops, SparseCore 0:
  18.8 74.7 all-reduce.2
  95.2 16.0 all-gather.4
  112.9 16.8 all-gather.2
where the time goes:
time: 157 us; the launch traced here: 156 us
  waiting for transfers between devices  109 us (69%)
  matrix products  23.9 us (15%)
  between operations  14.6 us (9%)
  starting transfers between devices  4.98 us (3%)
  other arithmetic  3.64 us (2%)
    psum x1, waiting for transfers between devices, broadcast(): return lax.psum(block, axis)  74.9 us
    all_gather x1, waiting for transfers between devices, shards(): head_upper = lax.all_gather(lead_upper, 'col', axis=1, tiled=True)  16.9 us
    dot_general x6, matrix products, product(): jnp.dot(left_mat, right_mat, precision=HIGHEST_PREC, preferred_element_ty...  12.9 us
    all_gather x1, waiting for transfers between devices, shards(): head_lower = lax.all_gather(lead_lower, 'col', axis=1, tiled=True)  11.7 us
    dot_general x4, matrix products, apply_rows(): jnp.einsum('ij,jkc->ikc', matrix, blocks, precision=HIGHEST_PREC, preferr...  5.48 us
    ppermute x1, waiting for transfers between devices, shifted(): lax.ppermute(value, axis, [(source, source + steps) for source in range(i...  5.11 us
    ppermute x1, starting transfers between devices, shifted(): lax.ppermute(value, axis, [(source, source + steps) for source in range(i...  4.86 us
    dot_general x2, matrix products, apply_transposed(): jnp.einsum('ri,rkc->ikc', matrix, blocks, precision=HIGHEST_PREC, preferr...  3.66 us
  transfers between devices with their start and end apart: 4, of which 4 were waited for; matrix products, arithmetic and copies ran while one was open for 4% of the time, Pallas kernels for 0%

commit v1 on v0

v1 whole, which is shorter than its diff:
```python
import functools

import jax
import jax.numpy as jnp
from jax import lax
from jax.experimental import pallas as pl
from jax.experimental.pallas import tpu as pltpu
from jax.sharding import PartitionSpec as P

PAIR = 2


def halves(value):
    high = value.astype(jnp.bfloat16)
    return high, (value - high.astype(jnp.float32)).astype(jnp.bfloat16)


def product(left, right, contract=(1, 0)):
    (left_high, left_low), (right_high, right_low) = left, right
    return lax.dot_general(
        jnp.concatenate([left_high, left_high, left_low], axis=contract[0]),
        jnp.concatenate([right_high, right_low, right_high], axis=contract[1]),
        (((contract[0],), (contract[1],)), ((), ())),
        preferred_element_type=jnp.float32,
    )


def step_kernel(groups, place_ref, *refs):
    count = groups * PAIR
    shares = refs[: PAIR * count]
    upper_ref, lower_ref, new_upper_ref, new_lower_ref = refs[PAIR * count : PAIR * count + 4]
    head_ref, rest_high, rest_low, low_high, low_low = refs[PAIR * count + 4 :]
    order, width = upper_ref.shape
    on_upper = place_ref[0] == 0
    total = jnp.zeros((8, width), jnp.float32)
    for step in range(groups):
        for side in range(PAIR):
            group = lax.rem(place_ref[1] + step, groups)
            column = group * PAIR + lax.rem(place_ref[2] + side, PAIR)
            same = shares[step * PAIR + side][...]
            other = shares[count + step * PAIR + side][...]
            head = jnp.where(on_upper, same, other)
            head_ref[column] = head
            total = total + jnp.sum((head * head).reshape(-1, 8, width), axis=0)
            low_high[column], low_low[column] = halves(jnp.where(on_upper, other, same))
    scale = lax.rsqrt(jnp.sum(total) / order + 1e-06)
    rows = lax.broadcasted_iota(jnp.int32, (order, width), 0)
    lanes = lax.broadcasted_iota(jnp.int32, (order, width), 1)
    for column in range(count):
        identity = jnp.where(rows == lanes + column * width, 1.0, 0.0)
        rest_high[column], rest_low[column] = halves(identity - head_ref[column] * scale)

    def joined(ref):
        return jnp.concatenate([ref[column] for column in range(count)], axis=1)

    rest = (joined(rest_high), joined(rest_low))
    low = (joined(low_high), joined(low_low))
    square = halves(product(rest, rest))
    middle = low[0].astype(jnp.float32) + low[1].astype(jnp.float32) + product(low, rest)
    reflect = halves((middle + product(halves(middle), square)) * scale)
    upper = upper_ref[...]
    lower = lower_ref[...]
    gram = halves(product(reflect, reflect, (1, 1)))
    mixed = upper - product(reflect, halves(lower), (0, 0))
    residue = lower - product(reflect, halves(upper))
    both = jnp.concatenate([product(reflect, halves(mixed)), product(gram, halves(residue))], axis=1)
    inner = 0.3125 * both + 0.0625 * product(gram, halves(both))
    inner = 0.375 * both + product(gram, halves(inner))
    inner = 0.5 * both + product(gram, halves(inner))
    new_upper_ref[...] = mixed + product(reflect, halves(inner[:, :width]), (0, 0))
    new_lower_ref[...] = residue + inner[:, width:]


def step_call(place, shares, upper, lower, groups):
    order, width = upper.shape
    count = groups * PAIR
    whole = pl.BlockSpec(memory_space=pltpu.VMEM)
    return pl.pallas_call(
        functools.partial(step_kernel, groups),
        out_shape=(jax.ShapeDtypeStruct(upper.shape, jnp.float32),) * 2,
        in_specs=[pl.BlockSpec(memory_space=pltpu.SMEM)] + [whole] * (len(shares) + 2),
        out_specs=(whole, whole),
        scratch_shapes=[pltpu.VMEM((count, order, width), jnp.float32)]
        + [pltpu.VMEM((count, order, width), jnp.bfloat16)] * 4,
        compiler_params=pltpu.CompilerParams(vmem_limit_bytes=48 * 1024 * 1024),
    )(place, *shares, upper, lower)


def spread(share, rows, row):
    stride = 1
    while stride < rows:
        stride *= 2
    while stride > 1:
        stride //= 2
        pairs = [(first, first + stride) for first in range(0, rows - stride, 2 * stride)]
        sends = [(PAIR * a + x, PAIR * b + x) for a, b in pairs for x in range(PAIR)]
        received = lax.ppermute(share, "blk", sends)
        share = jnp.where(lax.rem(row, 2 * stride) == stride, received, share)
    return share


def exchange(share, rows, groups):
    size = groups * PAIR
    shares = []
    for flip in range(PAIR):
        for step in range(groups):
            sends = [
                (
                    (PAIR * row + (x ^ flip)) * size + (y + step) % groups * PAIR + core,
                    (PAIR * row + x) * size + y * PAIR + core,
                )
                for row in range(rows)
                for x in range(PAIR)
                for y in range(groups)
                for core in range(PAIR)
            ]
            mine = lax.ppermute(share, ("blk", "col"), sends) if flip or step else share
            swap = [(column, column ^ 1) for column in range(size)]
            shares += [mine, lax.ppermute(mine, "col", swap)]
    return shares


def shards(upper_row, lower_row):
    blocks, size = lax.axis_size("blk"), lax.axis_size("col")
    assert upper_row.shape[1] == 1 and blocks % PAIR == 0 and size % PAIR == 0
    rows, groups = blocks // PAIR, size // PAIR
    block, column = lax.axis_index("blk"), lax.axis_index("col")
    upper, lower = upper_row[:, 0, :], lower_row[:, 0, :]
    shifted = lax.ppermute(upper, "blk", [(source, source + 1) for source in range(blocks - 1)])
    side = lax.rem(block, PAIR)
    share = spread(jnp.where(side == 0, upper, lower), rows, block // PAIR)
    shares = exchange(share, rows, groups)
    place = jnp.stack([side, column // PAIR, lax.rem(column, PAIR)]).astype(jnp.int32)
    new_upper, new_lower = step_call(place, shares, shifted, lower, groups)
    return new_upper[:, None, :], new_lower[:, None, :]


def solution(mesh):
    placement = P(None, "blk", "col")
    return jax.shard_map(
        shards,
        mesh=mesh,
        in_specs=(placement, placement),
        out_specs=(placement, placement),
        check_vma=False,
    )
```

time: 157 us -> 51.5 us (0.33)
  the two profiles are of different devices: /device:TPU:0 before, /device:TPU:25 now
where the time goes in v1:
time: 51.5 us; the launch traced here: 51.3 us
  starting transfers between devices  23 us (45%)
  waiting for transfers between devices  15.9 us (31%)
  Pallas kernels  10.5 us (20%)
  other arithmetic  1.12 us (2%)
  between operations  0.75 us (1%)
    ppermute x4, starting transfers between devices, exchange(): shares += [mine, lax.ppermute(mine, 'col', swap)]  15.2 us
    ppermute x2, waiting for transfers between devices, spread(): received = lax.ppermute(share, 'blk', sends)  14.4 us
    pallas_call x1, Pallas kernels, step_call(): pl.pallas_call(functools.partial(step_kernel, groups), out_shape=(jax.Sha...  10.5 us
    ppermute x1, starting transfers between devices, shards(): lax.ppermute(upper, 'blk', [(source, source + 1) for source in range(bloc...  3.11 us
    ppermute x3, starting transfers between devices, exchange(): mine = lax.ppermute(share, ('blk', 'col'), sends) if flip or step else share  2.71 us
    ppermute x2, starting transfers between devices, spread(): received = lax.ppermute(share, 'blk', sends)  1.97 us
    ppermute x4, waiting for transfers between devices, exchange(): shares += [mine, lax.ppermute(mine, 'col', swap)]  1.45 us
  transfers between devices with their start and end apart: 10, of which 3 were waited for; matrix products, arithmetic and copies ran while one was open for 0% of the time, Pallas kernels for 0%

profile of v1, /device:TPU:25, one launch (start us, length us, event | category | flops | bytes accessed | tf_op | source)
XLA Modules:
  0.0 51.3 jit_solution(5096461496353241806)
XLA Ops:
  0.6 1.0 %broadcast_select_fusion = f32[512,128]{1,0:T(8,128)S(1)} fusion(f32[512,128]{1,0:T(8,128)} %bitcast.13, f32[512,128]{1,0:T(8,128)} %bitcast.11, pred[]{:T(512)S(6)} %eq.11), kind=kLoop, calls=%fused_computation | loop fusion | flops 65536 | bytes 786433 | tf_op jit(solution)/shard_map/jit(_where)/select_n | solution.py:131
  1.6 0.7 %collective-permute-start = (f32[512,128]{1,0:T(8,128)S(1)}, f32[512,128]{1,0:T(8,128)S(1)}, u32[]{:S(2)}, u32[]{:S(2)}) collective-permute-start(f32[512,128]{1,0:T(8,128)S(1)} %broadcast_select_fusion), channel_id=1, source_target_pairs={{0,16},{4,20},{1,17},{5,21},{2,18},{6,22},{3,19},{7,23}} | collective-permute-start | bytes 786440 | tf_op jit(solution)/shard_map/ppermute | solution.py:97
  2.3 0.0 collective-permute-done
  2.4 1.3 %collective-permute-start.1 = (f32[512,128]{1,0:T(8,128)S(1)}, f32[512,128]{1,0:T(8,128)S(1)}, u32[]{:S(2)}, u32[]{:S(2)}) collective-permute-start(f32[512,128]{1,0:T(8,128)S(1)} %broadcast_select_fusion.1), channel_id=1, source_target_pairs={{0,8},{4,12},{16,24},{20,28},{1,9},{5,13},{17,25},{21,29},{2,10},{... | collective-permute-start | bytes 786440 | tf_op jit(solution)/shard_map/ppermute | solution.py:97
  3.7 0.0 copy-start.1
  3.7 0.0 copy-start
  3.7 14.4 %collective-permute-done.1 = f32[512,128]{1,0:T(8,128)S(1)} collective-permute-done((f32[512,128]{1,0:T(8,128)S(1)}, f32[512,128]{1,0:T(8,128)S(1)}, u32[]{:S(2)}, u32[]{:S(2)}) %collective-permute-start.1) | collective-permute-done | bytes 262176 | tf_op jit(solution)/shard_map/ppermute | solution.py:97
  18.2 2.2 %collective-permute-start.7 = (f32[512,128]{1,0:T(8,128)S(1)}, f32[512,128]{1,0:T(8,128)S(1)}, u32[]{:S(2)}, u32[]{:S(2)}) collective-permute-start(f32[512,128]{1,0:T(8,128)S(1)} %broadcast_select_fusion.2.refs_0_), channel_id=1, source_target_pairs={{6,0},{7,1},{4,2},{5,3},{2,4},{3,5},{0,6},{1,7},{14,8},{15,9},{12,... | collective-permute-start | bytes 786440 | tf_op jit(solution)/shard_map/ppermute | solution.py:117
  20.4 0.3 collective-permute-start.5
  20.7 0.2 collective-permute-start.3
  20.9 0.0 copy-done.1
  20.9 3.1 %collective-permute-start.9 = (f32[512,128]{1,0:T(8,128)S(1)}, f32[512,128]{1,0:T(8,128)S(1)}, u32[]{:S(2)}, u32[]{:S(2)}) collective-permute-start(f32[512,128]{1,0:T(8,128)S(1)} %bitcast.14), channel_id=1, source_target_pairs={{0,4},{4,8},{8,12},{12,16},{16,20},{20,24},{24,28},{1,5},{5,9},{9,... | collective-permute-start | bytes 786440 | tf_op jit(solution)/shard_map/ppermute | solution.py:129
  24.0 3.4 %collective-permute-start.2 = (f32[512,128]{1,0:T(8,128)S(1)}, f32[512,128]{1,0:T(8,128)S(1)}, u32[]{:S(2)}, u32[]{:S(2)}) collective-permute-start(f32[512,128]{1,0:T(8,128)S(1)} %broadcast_select_fusion.2.refs_0_), channel_id=1, source_target_pairs={{0,1},{1,0},{2,3},{3,2},{4,5},{5,4},{6,7},{7,6},{8,9},{9,8},{10,11... | collective-permute-start | bytes 786440 | tf_op jit(solution)/shard_map/ppermute | solution.py:119
  27.4 0.0 collective-permute-done.7.refs_6_
  27.4 8.8 %collective-permute-start.8 = (f32[512,128]{1,0:T(8,128)S(1)}, f32[512,128]{1,0:T(8,128)S(1)}, u32[]{:S(2)}, u32[]{:S(2)}) collective-permute-start(f32[512,128]{1,0:T(8,128)S(1)} %collective-permute-done.7.refs_6_), channel_id=1, source_target_pairs={{0,1},{1,0},{2,3},{3,2},{4,5},{5,4},{6,7},{7,6},{8,9},{9,8},{10,11... | collective-permute-start | bytes 786440 | tf_op jit(solution)/shard_map/ppermute | solution.py:119
  36.2 0.0 collective-permute-done.5.refs_4_
  36.2 3.0 %collective-permute-start.6 = (f32[512,128]{1,0:T(8,128)S(1)}, f32[512,128]{1,0:T(8,128)S(1)}, u32[]{:S(2)}, u32[]{:S(2)}) collective-permute-start(f32[512,128]{1,0:T(8,128)S(1)} %collective-permute-done.5.refs_4_), channel_id=1, source_target_pairs={{0,1},{1,0},{2,3},{3,2},{4,5},{5,4},{6,7},{7,6},{8,9},{9,8},{10,11... | collective-permute-start | bytes 786440 | tf_op jit(solution)/shard_map/ppermute | solution.py:119
  39.2 0.0 collective-permute-done.3.refs_2_
  39.2 0.0 collective-permute-start.4
  39.2 0.1 pad_add_fusion.place_ref
  39.3 0.0 collective-permute-done.9.refs_8_
  39.3 0.0 collective-permute-done.2.refs_1_
  39.3 0.0 collective-permute-done.8.refs_7_
  39.3 1.1 %collective-permute-done.6.refs_5_ = f32[512,128]{1,0:T(8,128)S(1)} collective-permute-done((f32[512,128]{1,0:T(8,128)S(1)}, f32[512,128]{1,0:T(8,128)S(1)}, u32[]{:S(2)}, u32[]{:S(2)}) %collective-permute-start.6) | collective-permute-done | bytes 262176 | tf_op jit(solution)/shard_map/ppermute | solution.py:119
  40.4 0.4 collective-permute-done.4.refs_3_
  40.7 0.0 copy-done
  40.7 10.5 %shard_map.41 = (f32[512,128]{1,0:T(8,128)}, f32[512,128]{1,0:T(8,128)}) custom-call(s32[3]{0:T(128)S(1)} %pad_add_fusion.place_ref, f32[512,128]{1,0:T(8,128)S(1)} %broadcast_select_fusion.2.refs_0_, f32[512,128]{1,0:T(8,128)S(1)} %collective-permute-done.2.refs_1_, f32[512,128]{1,0:T(8,128)S(1)} %collective-permute-done.3.refs_2_, ...), custom_call_target="tpu_custom_call" | custom-call | tf_op jit(solution)/shard_map/pallas_call | solution.py:78
  (2 shorter events, 0.1 us)
Async XLA Ops:
  1.6 0.7 %collective-permute-start = (f32[512,128]{1,0:T(8,128)S(1)}, f32[512,128]{1,0:T(8,128)S(1)}, u32[]{:S(2)}, u32[]{:S(2)}) collective-permute-start(f32[512,128]{1,0:T(8,128)S(1)} %broadcast_select_fusion), channel_id=1, source_target_pairs={{0,16},{4,20},{1,17},{5,21},{2,18},{6,22},{3,19},{7,23}} | collective-permute-start | bytes 786440 | tf_op jit(solution)/shard_map/ppermute | solution.py:97
  2.4 15.8 %collective-permute-start.1 = (f32[512,128]{1,0:T(8,128)S(1)}, f32[512,128]{1,0:T(8,128)S(1)}, u32[]{:S(2)}, u32[]{:S(2)}) collective-permute-start(f32[512,128]{1,0:T(8,128)S(1)} %broadcast_select_fusion.1), channel_id=1, source_target_pairs={{0,8},{4,12},{16,24},{20,28},{1,9},{5,13},{17,25},{21,29},{2,10},{... | collective-permute-start | bytes 786440 | tf_op jit(solution)/shard_map/ppermute | solution.py:97
  3.7 17.2 %copy-start.1 = (f32[512,1,128]{2,1,0:T(1,128)S(1)}, f32[512,1,128]{2,1,0:T(1,128)}, u32[]{:S(2)}) copy-start(f32[512,1,128]{2,1,0:T(1,128)} %param.2) | copy-start | bytes 786436
  3.7 37.0 %copy-start = (f32[512,1,128]{2,1,0:T(1,128)S(1)}, f32[512,1,128]{2,1,0:T(1,128)}, u32[]{:S(2)}) copy-start(f32[512,1,128]{2,1,0:T(1,128)} %param.3) | copy-start | bytes 786436
  18.2 9.2 %collective-permute-start.7 = (f32[512,128]{1,0:T(8,128)S(1)}, f32[512,128]{1,0:T(8,128)S(1)}, u32[]{:S(2)}, u32[]{:S(2)}) collective-permute-start(f32[512,128]{1,0:T(8,128)S(1)} %broadcast_select_fusion.2.refs_0_), channel_id=1, source_target_pairs={{6,0},{7,1},{4,2},{5,3},{2,4},{3,5},{0,6},{1,7},{14,8},{15,9},{12,... | collective-permute-start | bytes 786440 | tf_op jit(solution)/shard_map/ppermute | solution.py:117
  20.4 15.8 %collective-permute-start.5 = (f32[512,128]{1,0:T(8,128)S(1)}, f32[512,128]{1,0:T(8,128)S(1)}, u32[]{:S(2)}, u32[]{:S(2)}) collective-permute-start(f32[512,128]{1,0:T(8,128)S(1)} %broadcast_select_fusion.2.refs_0_), channel_id=1, source_target_pairs={{4,0},{5,1},{6,2},{7,3},{0,4},{1,5},{2,6},{3,7},{12,8},{13,9},{14,... | collective-permute-start | bytes 786440 | tf_op jit(solution)/shard_map/ppermute | solution.py:117
  20.7 18.5 %collective-permute-start.3 = (f32[512,128]{1,0:T(8,128)S(1)}, f32[512,128]{1,0:T(8,128)S(1)}, u32[]{:S(2)}, u32[]{:S(2)}) collective-permute-start(f32[512,128]{1,0:T(8,128)S(1)} %broadcast_select_fusion.2.refs_0_), channel_id=1, source_target_pairs={{2,0},{3,1},{0,2},{1,3},{6,4},{7,5},{4,6},{5,7},{10,8},{11,9},{8,1... | collective-permute-start | bytes 786440 | tf_op jit(solution)/shard_map/ppermute | solution.py:117
  20.9 18.4 %collective-permute-start.9 = (f32[512,128]{1,0:T(8,128)S(1)}, f32[512,128]{1,0:T(8,128)S(1)}, u32[]{:S(2)}, u32[]{:S(2)}) collective-permute-start(f32[512,128]{1,0:T(8,128)S(1)} %bitcast.14), channel_id=1, source_target_pairs={{0,4},{4,8},{8,12},{12,16},{16,20},{20,24},{24,28},{1,5},{5,9},{9,... | collective-permute-start | bytes 786440 | tf_op jit(solution)/shard_map/ppermute | solution.py:129
  24.0 15.3 %collective-permute-start.2 = (f32[512,128]{1,0:T(8,128)S(1)}, f32[512,128]{1,0:T(8,128)S(1)}, u32[]{:S(2)}, u32[]{:S(2)}) collective-permute-start(f32[512,128]{1,0:T(8,128)S(1)} %broadcast_select_fusion.2.refs_0_), channel_id=1, source_target_pairs={{0,1},{1,0},{2,3},{3,2},{4,5},{5,4},{6,7},{7,6},{8,9},{9,8},{10,11... | collective-permute-start | bytes 786440 | tf_op jit(solution)/shard_map/ppermute | solution.py:119
  27.4 11.9 %collective-permute-start.8 = (f32[512,128]{1,0:T(8,128)S(1)}, f32[512,128]{1,0:T(8,128)S(1)}, u32[]{:S(2)}, u32[]{:S(2)}) collective-permute-start(f32[512,128]{1,0:T(8,128)S(1)} %collective-permute-done.7.refs_6_), channel_id=1, source_target_pairs={{0,1},{1,0},{2,3},{3,2},{4,5},{5,4},{6,7},{7,6},{8,9},{9,8},{10,11... | collective-permute-start | bytes 786440 | tf_op jit(solution)/shard_map/ppermute | solution.py:119
  36.2 4.2 %collective-permute-start.6 = (f32[512,128]{1,0:T(8,128)S(1)}, f32[512,128]{1,0:T(8,128)S(1)}, u32[]{:S(2)}, u32[]{:S(2)}) collective-permute-start(f32[512,128]{1,0:T(8,128)S(1)} %collective-permute-done.5.refs_4_), channel_id=1, source_target_pairs={{0,1},{1,0},{2,3},{3,2},{4,5},{5,4},{6,7},{7,6},{8,9},{9,8},{10,11... | collective-permute-start | bytes 786440 | tf_op jit(solution)/shard_map/ppermute | solution.py:119
  39.2 1.5 %collective-permute-start.4 = (f32[512,128]{1,0:T(8,128)S(1)}, f32[512,128]{1,0:T(8,128)S(1)}, u32[]{:S(2)}, u32[]{:S(2)}) collective-permute-start(f32[512,128]{1,0:T(8,128)S(1)} %collective-permute-done.3.refs_2_), channel_id=1, source_target_pairs={{0,1},{1,0},{2,3},{3,2},{4,5},{5,4},{6,7},{7,6},{8,9},{9,8},{10,11... | collective-permute-start | bytes 786440 | tf_op jit(solution)/shard_map/ppermute | solution.py:119

commit v2 on v1

v2 whole, which is shorter than its diff:
```python
import functools

import jax
import jax.numpy as jnp
from jax import lax
from jax.experimental import pallas as pl
from jax.experimental.pallas import tpu as pltpu
from jax.sharding import PartitionSpec as P

PAIR = 2
LEAD = 4.0


def halves(value):
    high = value.astype(jnp.bfloat16)
    return high, (value - high.astype(jnp.float32)).astype(jnp.bfloat16)


def whole(parts):
    return parts[0].astype(jnp.float32) + parts[1].astype(jnp.float32)


def product(left, right, side=0):
    (left_high, left_low), (right_high, right_low) = left, right
    return lax.dot_general(
        jnp.concatenate([left_high, left_high, left_low], axis=1),
        jnp.concatenate([right_high, right_low, right_high], axis=side),
        (((1,), (side,)), ((), ())),
        preferred_element_type=jnp.float32,
    )


def add_diagonal(matrix, block):
    width = block.shape[0]
    count = matrix.shape[0] // width
    return jnp.concatenate(
        [
            jnp.concatenate(
                [
                    matrix[i * width : (i + 1) * width, j * width : (j + 1) * width] + (block if i == j else 0.0)
                    for j in range(count)
                ],
                axis=1,
            )
            for i in range(count)
        ],
        axis=0,
    )


def step_kernel(groups, place_ref, *refs):
    count = groups * PAIR
    shares = refs[: PAIR * count]
    upper_ref, lower_ref, new_upper_ref, new_lower_ref = refs[PAIR * count : PAIR * count + 4]
    rest_high, rest_low, low_high, low_low = refs[PAIR * count + 4 :]
    order, width = upper_ref.shape
    on_upper = place_ref[0] == 0
    square_shape = (width, width)
    unit = jnp.where(
        lax.broadcasted_iota(jnp.int32, square_shape, 0) == lax.broadcasted_iota(jnp.int32, square_shape, 1), 1.0, 0.0
    )
    total = jnp.zeros((8, width), jnp.float32)
    for step in range(groups):
        for side in range(PAIR):
            group = lax.rem(place_ref[1] + step, groups)
            column = group * PAIR + lax.rem(place_ref[2] + side, PAIR)
            same_ref = shares[step * PAIR + side]
            other_ref = shares[count + step * PAIR + side]
            same, other = same_ref[...], other_ref[...]
            head = jnp.where(on_upper, same, other)
            total = total + jnp.sum((head * head).reshape(-1, 8, width), axis=0)
            rest_high[column], rest_low[column] = halves(head)
            near = pl.ds(pl.multiple_of(column * width, width), width)
            diagonal = jnp.where(on_upper, same_ref[near, :], other_ref[near, :]) - LEAD * unit
            rest_high[column, near, :], rest_low[column, near, :] = halves(diagonal)
            low_high[column], low_low[column] = halves(jnp.where(on_upper, other, same))
    scale = lax.rsqrt(jnp.full((1, 1), jnp.sum(total)) / order + 1e-06)
    shift = 1.0 - LEAD * scale

    def joined(ref):
        return jnp.concatenate([ref[column] for column in range(count)], axis=1)

    rest = (joined(rest_high), joined(rest_low))
    low = (joined(low_high), joined(low_low))
    square = (scale * scale) * product(rest, rest) - (2.0 * shift * scale) * whole(rest)
    square = halves(add_diagonal(square, shift * shift * unit))
    middle = (1.0 + shift) * whole(low) - scale * product(low, rest)
    reflect = halves((middle + product(halves(middle), square)) * scale)
    upper = upper_ref[...].T
    lower = lower_ref[...].T
    gram = halves(product(reflect, reflect, 1))
    bent = product(halves(upper), reflect, 1)
    pulled = product(halves(jnp.concatenate([lower, bent], axis=0)), gram)
    both = jnp.concatenate([bent - pulled[:width], pulled[:width] - pulled[width:]], axis=0)
    inner = 0.3125 * both + 0.0625 * product(halves(both), gram)
    inner = 0.375 * both + product(halves(inner), gram)
    inner = 0.5 * both + product(halves(inner), gram)
    new_upper_ref[...] = (upper - product(halves(lower - inner[:width]), reflect)).T
    new_lower_ref[...] = (lower - bent + inner[width:]).T


def step_call(place, shares, upper, lower, groups):
    order, width = upper.shape
    count = groups * PAIR
    in_vmem = pl.BlockSpec(memory_space=pltpu.VMEM)
    return pl.pallas_call(
        functools.partial(step_kernel, groups),
        out_shape=(jax.ShapeDtypeStruct(upper.shape, jnp.float32),) * 2,
        in_specs=[pl.BlockSpec(memory_space=pltpu.SMEM)] + [in_vmem] * (len(shares) + 2),
        out_specs=(in_vmem, in_vmem),
        scratch_shapes=[pltpu.VMEM((count, order, width), jnp.bfloat16)] * 4,
        compiler_params=pltpu.CompilerParams(vmem_limit_bytes=48 * 1024 * 1024),
    )(place, *shares, upper, lower)


def spread(share, rows, row):
    stride = 1
    while stride < rows:
        stride *= 2
    while stride > 1:
        stride //= 2
        pairs = [(first, first + stride) for first in range(0, rows - stride, 2 * stride)]
        sends = [(PAIR * a + x, PAIR * b + x) for a, b in pairs for x in range(PAIR)]
        received = lax.ppermute(share, "blk", sends)
        share = jnp.where(lax.rem(row, 2 * stride) == stride, received, share)
    return share


def exchange(share, rows, groups):
    size = groups * PAIR
    shares = []
    for flip in range(PAIR):
        for step in range(groups):
            sends = [
                (
                    (PAIR * row + (x ^ flip)) * size + (y + step) % groups * PAIR + core,
                    (PAIR * row + x) * size + y * PAIR + core,
                )
                for row in range(rows)
                for x in range(PAIR)
                for y in range(groups)
                for core in range(PAIR)
            ]
            mine = lax.ppermute(share, ("blk", "col"), sends) if flip or step else share
            swap = [(column, column ^ 1) for column in range(size)]
            shares += [mine, lax.ppermute(mine, "col", swap)]
    return shares


def shards(upper_row, lower_row):
    blocks, size = lax.axis_size("blk"), lax.axis_size("col")
    assert upper_row.shape[1] == 1 and blocks % PAIR == 0 and size % PAIR == 0
    rows, groups = blocks // PAIR, size // PAIR
    block, column = lax.axis_index("blk"), lax.axis_index("col")
    upper, lower = upper_row[:, 0, :], lower_row[:, 0, :]
    side = lax.rem(block, PAIR)
    swapped = lax.ppermute(upper, "blk", [(source, source ^ 1) for source in range(blocks)])
    ahead = [(source, source + PAIR) for source in range(0, blocks - PAIR, PAIR)]
    shifted = jnp.where(side == 1, swapped, lax.ppermute(swapped, "blk", ahead))
    share = spread(jnp.where(side == 0, upper, lower), rows, block // PAIR)
    shares = exchange(share, rows, groups)
    place = jnp.stack([side, column // PAIR, lax.rem(column, PAIR)]).astype(jnp.int32)
    new_upper, new_lower = step_call(place, shares, shifted, lower, groups)
    return new_upper[:, None, :], new_lower[:, None, :]


def solution(mesh):
    placement = P(None, "blk", "col")
    return jax.shard_map(
        shards,
        mesh=mesh,
        in_specs=(placement, placement),
        out_specs=(placement, placement),
        check_vma=False,
    )
```

time: 51.5 us -> 43.4 us (0.84)
  the two profiles are of different devices: /device:TPU:25 before, /device:TPU:0 now
where the time goes in v2:
time: 43.4 us; the launch traced here: 43 us
  starting transfers between devices  17 us (39%)
  waiting for transfers between devices  16 us (37%)
  Pallas kernels  8.1 us (19%)
  other arithmetic  1.15 us (3%)
  between operations  0.77 us (2%)
    ppermute x2, waiting for transfers between devices, spread(): received = lax.ppermute(share, 'blk', sends)  8.86 us
    pallas_call x1, Pallas kernels, step_call(): pl.pallas_call(functools.partial(step_kernel, groups), out_shape=(jax.Sha...  8.1 us
    ppermute x2, starting transfers between devices, spread(): received = lax.ppermute(share, 'blk', sends)  7.26 us
    ppermute x3, waiting for transfers between devices, exchange(): mine = lax.ppermute(share, ('blk', 'col'), sends) if flip or step else share  5.85 us
    ppermute x1, starting transfers between devices, shards(): shifted = jnp.where(side == 1, swapped, lax.ppermute(swapped, 'blk', ahead))  4.39 us
    ppermute x3, starting transfers between devices, exchange(): mine = lax.ppermute(share, ('blk', 'col'), sends) if flip or step else share  3.55 us
    ppermute x1, starting transfers between devices, shards(): lax.ppermute(upper, 'blk', [(source, source ^ 1) for source in range(bloc...  1.56 us
    ppermute x4, waiting for transfers between devices, exchange(): shares += [mine, lax.ppermute(mine, 'col', swap)]  1.26 us
  transfers between devices with their start and end apart: 11, of which 7 were waited for; matrix products, arithmetic and copies ran while one was open for 0% of the time, Pallas kernels for 0%

profile of v2, /device:TPU:0, one launch (start us, length us, event | category | flops | bytes accessed | tf_op | source)
XLA Modules:
  0.0 43.0 jit_solution(13543955172250771116)
XLA Ops:
  0.6 1.0 %broadcast_select_fusion.1 = f32[512,128]{1,0:T(8,128)S(1)} fusion(f32[512,128]{1,0:T(8,128)} %bitcast.13, f32[512,128]{1,0:T(8,128)} %bitcast.11, pred[]{:T(512)S(6)} %eq.14), kind=kLoop, calls=%fused_computation.1 | loop fusion | flops 65536 | bytes 786433 | tf_op jit(solution)/shard_map/jit(_where)/select_n | solution.py:160
  1.6 6.0 %collective-permute-start = (f32[512,128]{1,0:T(8,128)S(1)}, f32[512,128]{1,0:T(8,128)S(1)}, u32[]{:S(2)}, u32[]{:S(2)}) collective-permute-start(f32[512,128]{1,0:T(8,128)S(1)} %broadcast_select_fusion.1), channel_id=1, source_target_pairs={{0,16},{4,20},{1,17},{5,21},{2,18},{6,22},{3,19},{7,23}} | collective-permute-start | bytes 786440 | tf_op jit(solution)/shard_map/ppermute | solution.py:124
  7.6 0.0 copy-start.1
  7.6 5.5 %collective-permute-done = f32[512,128]{1,0:T(8,128)S(1)} collective-permute-done((f32[512,128]{1,0:T(8,128)S(1)}, f32[512,128]{1,0:T(8,128)S(1)}, u32[]{:S(2)}, u32[]{:S(2)}) %collective-permute-start) | collective-permute-done | bytes 262176 | tf_op jit(solution)/shard_map/ppermute | solution.py:124
  13.2 1.3 %collective-permute-start.1 = (f32[512,128]{1,0:T(8,128)S(1)}, f32[512,128]{1,0:T(8,128)S(1)}, u32[]{:S(2)}, u32[]{:S(2)}) collective-permute-start(f32[512,128]{1,0:T(8,128)S(1)} %broadcast_select_fusion.2), channel_id=1, source_target_pairs={{0,8},{4,12},{16,24},{20,28},{1,9},{5,13},{17,25},{21,29},{2,10},{... | collective-permute-start | bytes 786440 | tf_op jit(solution)/shard_map/ppermute | solution.py:124
  14.5 0.0 copy-done.1
  14.5 1.6 %collective-permute-start.9 = (f32[512,128]{1,0:T(8,128)S(1)}, f32[512,128]{1,0:T(8,128)S(1)}, u32[]{:S(2)}, u32[]{:S(2)}) collective-permute-start(f32[512,128]{1,0:T(8,128)S(1)} %bitcast.14), channel_id=1, source_target_pairs={{0,4},{4,0},{8,12},{12,8},{16,20},{20,16},{24,28},{28,24},{1,5},{5... | collective-permute-start | bytes 786440 | tf_op jit(solution)/shard_map/ppermute | solution.py:157
  16.0 3.4 %collective-permute-done.1 = f32[512,128]{1,0:T(8,128)S(1)} collective-permute-done((f32[512,128]{1,0:T(8,128)S(1)}, f32[512,128]{1,0:T(8,128)S(1)}, u32[]{:S(2)}, u32[]{:S(2)}) %collective-permute-start.1) | collective-permute-done | bytes 262176 | tf_op jit(solution)/shard_map/ppermute | solution.py:124
  19.4 2.5 %collective-permute-start.7 = (f32[512,128]{1,0:T(8,128)S(1)}, f32[512,128]{1,0:T(8,128)S(1)}, u32[]{:S(2)}, u32[]{:S(2)}) collective-permute-start(f32[512,128]{1,0:T(8,128)S(1)} %broadcast_select_fusion.3.refs_0_), channel_id=1, source_target_pairs={{6,0},{7,1},{4,2},{5,3},{2,4},{3,5},{0,6},{1,7},{14,8},{15,9},{12,... | collective-permute-start | bytes 786440 | tf_op jit(solution)/shard_map/ppermute | solution.py:144
  22.0 0.5 %collective-permute-start.5 = (f32[512,128]{1,0:T(8,128)S(1)}, f32[512,128]{1,0:T(8,128)S(1)}, u32[]{:S(2)}, u32[]{:S(2)}) collective-permute-start(f32[512,128]{1,0:T(8,128)S(1)} %broadcast_select_fusion.3.refs_0_), channel_id=1, source_target_pairs={{4,0},{5,1},{6,2},{7,3},{0,4},{1,5},{2,6},{3,7},{12,8},{13,9},{14,... | collective-permute-start | bytes 786440 | tf_op jit(solution)/shard_map/ppermute | solution.py:144
  22.5 0.5 %collective-permute-start.3 = (f32[512,128]{1,0:T(8,128)S(1)}, f32[512,128]{1,0:T(8,128)S(1)}, u32[]{:S(2)}, u32[]{:S(2)}) collective-permute-start(f32[512,128]{1,0:T(8,128)S(1)} %broadcast_select_fusion.3.refs_0_), channel_id=1, source_target_pairs={{2,0},{3,1},{0,2},{1,3},{6,4},{7,5},{4,6},{5,7},{10,8},{11,9},{8,1... | collective-permute-start | bytes 786440 | tf_op jit(solution)/shard_map/ppermute | solution.py:144
  23.0 0.0 collective-permute-done.9
  23.0 4.4 %collective-permute-start.10 = (f32[512,128]{1,0:T(8,128)S(1)}, f32[512,128]{1,0:T(8,128)S(1)}, u32[]{:S(2)}, u32[]{:S(2)}) collective-permute-start(f32[512,128]{1,0:T(8,128)S(1)} %collective-permute-done.9), channel_id=1, source_target_pairs={{0,8},{8,16},{16,24},{1,9},{9,17},{17,25},{2,10},{10,18},{18,26},{... | collective-permute-start | bytes 786440 | tf_op jit(solution)/shard_map/ppermute | solution.py:159
  27.4 0.1 collective-permute-start.2
  27.5 2.2 %collective-permute-done.7.refs_6_ = f32[512,128]{1,0:T(8,128)S(1)} collective-permute-done((f32[512,128]{1,0:T(8,128)S(1)}, f32[512,128]{1,0:T(8,128)S(1)}, u32[]{:S(2)}, u32[]{:S(2)}) %collective-permute-start.7) | collective-permute-done | bytes 262176 | tf_op jit(solution)/shard_map/ppermute | solution.py:144
  29.7 0.0 collective-permute-start.8
  29.7 3.3 %collective-permute-done.5.refs_4_ = f32[512,128]{1,0:T(8,128)S(1)} collective-permute-done((f32[512,128]{1,0:T(8,128)S(1)}, f32[512,128]{1,0:T(8,128)S(1)}, u32[]{:S(2)}, u32[]{:S(2)}) %collective-permute-start.5) | collective-permute-done | bytes 262176 | tf_op jit(solution)/shard_map/ppermute | solution.py:144
  33.0 0.0 collective-permute-start.6
  33.0 0.3 collective-permute-done.3.refs_2_
  33.4 0.2 collective-permute-start.4
  33.5 0.1 pad_add_fusion.place_ref
  33.6 0.0 copy-start
  33.6 0.0 collective-permute-done.10
  33.6 0.0 collective-permute-done.2.refs_1_
  33.6 0.0 collective-permute-done.8.refs_7_
  33.7 0.9 %collective-permute-done.6.refs_5_ = f32[512,128]{1,0:T(8,128)S(1)} collective-permute-done((f32[512,128]{1,0:T(8,128)S(1)}, f32[512,128]{1,0:T(8,128)S(1)}, u32[]{:S(2)}, u32[]{:S(2)}) %collective-permute-start.6) | collective-permute-done | bytes 262176 | tf_op jit(solution)/shard_map/ppermute | solution.py:146
  34.5 0.4 collective-permute-done.4.refs_3_
  34.9 0.0 copy-done
  34.9 8.1 %shard_map.41 = (f32[512,128]{1,0:T(8,128)}, f32[512,128]{1,0:T(8,128)}) custom-call(s32[3]{0:T(128)S(1)} %pad_add_fusion.place_ref, f32[512,128]{1,0:T(8,128)S(1)} %broadcast_select_fusion.3.refs_0_, f32[512,128]{1,0:T(8,128)S(1)} %collective-permute-done.2.refs_1_, f32[512,128]{1,0:T(8,128)S(1)} %collective-permute-done.3.refs_2_, ...), custom_call_target="tpu_custom_call" | custom-call | tf_op jit(solution)/shard_map/pallas_call | solution.py:106
  (3 shorter events, 0.1 us)
Async XLA Ops:
  1.6 11.5 %collective-permute-start = (f32[512,128]{1,0:T(8,128)S(1)}, f32[512,128]{1,0:T(8,128)S(1)}, u32[]{:S(2)}, u32[]{:S(2)}) collective-permute-start(f32[512,128]{1,0:T(8,128)S(1)} %broadcast_select_fusion.1), channel_id=1, source_target_pairs={{0,16},{4,20},{1,17},{5,21},{2,18},{6,22},{3,19},{7,23}} | collective-permute-start | bytes 786440 | tf_op jit(solution)/shard_map/ppermute | solution.py:124
  7.6 6.9 %copy-start.1 = (f32[512,1,128]{2,1,0:T(1,128)S(1)}, f32[512,1,128]{2,1,0:T(1,128)}, u32[]{:S(2)}) copy-start(f32[512,1,128]{2,1,0:T(1,128)} %param.2) | copy-start | bytes 786436
  13.2 6.3 %collective-permute-start.1 = (f32[512,128]{1,0:T(8,128)S(1)}, f32[512,128]{1,0:T(8,128)S(1)}, u32[]{:S(2)}, u32[]{:S(2)}) collective-permute-start(f32[512,128]{1,0:T(8,128)S(1)} %broadcast_select_fusion.2), channel_id=1, source_target_pairs={{0,8},{4,12},{16,24},{20,28},{1,9},{5,13},{17,25},{21,29},{2,10},{... | collective-permute-start | bytes 786440 | tf_op jit(solution)/shard_map/ppermute | solution.py:124
  14.5 8.5 %collective-permute-start.9 = (f32[512,128]{1,0:T(8,128)S(1)}, f32[512,128]{1,0:T(8,128)S(1)}, u32[]{:S(2)}, u32[]{:S(2)}) collective-permute-start(f32[512,128]{1,0:T(8,128)S(1)} %bitcast.14), channel_id=1, source_target_pairs={{0,4},{4,0},{8,12},{12,8},{16,20},{20,16},{24,28},{28,24},{1,5},{5... | collective-permute-start | bytes 786440 | tf_op jit(solution)/shard_map/ppermute | solution.py:157
  19.4 10.3 %collective-permute-start.7 = (f32[512,128]{1,0:T(8,128)S(1)}, f32[512,128]{1,0:T(8,128)S(1)}, u32[]{:S(2)}, u32[]{:S(2)}) collective-permute-start(f32[512,128]{1,0:T(8,128)S(1)} %broadcast_select_fusion.3.refs_0_), channel_id=1, source_target_pairs={{6,0},{7,1},{4,2},{5,3},{2,4},{3,5},{0,6},{1,7},{14,8},{15,9},{12,... | collective-permute-start | bytes 786440 | tf_op jit(solution)/shard_map/ppermute | solution.py:144
  22.0 11.0 %collective-permute-start.5 = (f32[512,128]{1,0:T(8,128)S(1)}, f32[512,128]{1,0:T(8,128)S(1)}, u32[]{:S(2)}, u32[]{:S(2)}) collective-permute-start(f32[512,128]{1,0:T(8,128)S(1)} %broadcast_select_fusion.3.refs_0_), channel_id=1, source_target_pairs={{4,0},{5,1},{6,2},{7,3},{0,4},{1,5},{2,6},{3,7},{12,8},{13,9},{14,... | collective-permute-start | bytes 786440 | tf_op jit(solution)/shard_map/ppermute | solution.py:144
  22.5 10.9 %collective-permute-start.3 = (f32[512,128]{1,0:T(8,128)S(1)}, f32[512,128]{1,0:T(8,128)S(1)}, u32[]{:S(2)}, u32[]{:S(2)}) collective-permute-start(f32[512,128]{1,0:T(8,128)S(1)} %broadcast_select_fusion.3.refs_0_), channel_id=1, source_target_pairs={{2,0},{3,1},{0,2},{1,3},{6,4},{7,5},{4,6},{5,7},{10,8},{11,9},{8,1... | collective-permute-start | bytes 786440 | tf_op jit(solution)/shard_map/ppermute | solution.py:144
  23.0 10.6 %collective-permute-start.10 = (f32[512,128]{1,0:T(8,128)S(1)}, f32[512,128]{1,0:T(8,128)S(1)}, u32[]{:S(2)}, u32[]{:S(2)}) collective-permute-start(f32[512,128]{1,0:T(8,128)S(1)} %collective-permute-done.9), channel_id=1, source_target_pairs={{0,8},{8,16},{16,24},{1,9},{9,17},{17,25},{2,10},{10,18},{18,26},{... | collective-permute-start | bytes 786440 | tf_op jit(solution)/shard_map/ppermute | solution.py:159
  27.4 6.2 %collective-permute-start.2 = (f32[512,128]{1,0:T(8,128)S(1)}, f32[512,128]{1,0:T(8,128)S(1)}, u32[]{:S(2)}, u32[]{:S(2)}) collective-permute-start(f32[512,128]{1,0:T(8,128)S(1)} %broadcast_select_fusion.3.refs_0_), channel_id=1, source_target_pairs={{0,1},{1,0},{2,3},{3,2},{4,5},{5,4},{6,7},{7,6},{8,9},{9,8},{10,11... | collective-permute-start | bytes 786440 | tf_op jit(solution)/shard_map/ppermute | solution.py:146
  29.7 4.0 %collective-permute-start.8 = (f32[512,128]{1,0:T(8,128)S(1)}, f32[512,128]{1,0:T(8,128)S(1)}, u32[]{:S(2)}, u32[]{:S(2)}) collective-permute-start(f32[512,128]{1,0:T(8,128)S(1)} %collective-permute-done.7.refs_6_), channel_id=1, source_target_pairs={{0,1},{1,0},{2,3},{3,2},{4,5},{5,4},{6,7},{7,6},{8,9},{9,8},{10,11... | collective-permute-start | bytes 786440 | tf_op jit(solution)/shard_map/ppermute | solution.py:146
  33.0 1.5 %collective-permute-start.6 = (f32[512,128]{1,0:T(8,128)S(1)}, f32[512,128]{1,0:T(8,128)S(1)}, u32[]{:S(2)}, u32[]{:S(2)}) collective-permute-start(f32[512,128]{1,0:T(8,128)S(1)} %collective-permute-done.5.refs_4_), channel_id=1, source_target_pairs={{0,1},{1,0},{2,3},{3,2},{4,5},{5,4},{6,7},{7,6},{8,9},{9,8},{10,11... | collective-permute-start | bytes 786440 | tf_op jit(solution)/shard_map/ppermute | solution.py:146
  33.4 1.6 %collective-permute-start.4 = (f32[512,128]{1,0:T(8,128)S(1)}, f32[512,128]{1,0:T(8,128)S(1)}, u32[]{:S(2)}, u32[]{:S(2)}) collective-permute-start(f32[512,128]{1,0:T(8,128)S(1)} %collective-permute-done.3.refs_2_), channel_id=1, source_target_pairs={{0,1},{1,0},{2,3},{3,2},{4,5},{5,4},{6,7},{7,6},{8,9},{9,8},{10,11... | collective-permute-start | bytes 786440 | tf_op jit(solution)/shard_map/ppermute | solution.py:146
  33.6 1.3 %copy-start = (f32[512,1,128]{2,1,0:T(1,128)S(1)}, f32[512,1,128]{2,1,0:T(1,128)}, u32[]{:S(2)}) copy-start(f32[512,1,128]{2,1,0:T(1,128)} %param.3) | copy-start | bytes 786436

commit v3 on v2

--- a/solution.py
+++ b/solution.py
@@ -20,14 +20,29 @@
     return parts[0].astype(jnp.float32) + parts[1].astype(jnp.float32)
 
 
+def dot(left, right, side):
+    return lax.dot_general(left, right, (((1,), (side,)), ((), ())), preferred_element_type=jnp.float32)
+
+
 def product(left, right, side=0):
     (left_high, left_low), (right_high, right_low) = left, right
-    return lax.dot_general(
+    return dot(
         jnp.concatenate([left_high, left_high, left_low], axis=1),
         jnp.concatenate([right_high, right_low, right_high], axis=side),
-        (((1,), (side,)), ((), ())),
-        preferred_element_type=jnp.float32,
-    )
+        side,
+    )
+
+
+def thin_product(left, right, side=0):
+    (left_high, left_low), (right_high, right_low) = halves(left), right
+    both = dot(jnp.concatenate([left_high, left_low], axis=0), right_high, side)
+    return both[: left.shape[0]] + both[left.shape[0] :] + dot(left_high, right_low, side)
+
+
+def inner_product(left, gram):
+    inner = 0.3125 * left + 0.0625 * thin_product(left, gram)
+    inner = 0.375 * left + thin_product(inner, gram)
+    return 0.5 * left + thin_product(inner, gram)
 
 
 def add_diagonal(matrix, block):
@@ -48,13 +63,14 @@
     )
 
 
-def step_kernel(groups, place_ref, *refs):
+def step_kernel(groups, *refs):
     count = groups * PAIR
+    block, here = lax.axis_index("blk"), lax.axis_index("col")
     shares = refs[: PAIR * count]
     upper_ref, lower_ref, new_upper_ref, new_lower_ref = refs[PAIR * count : PAIR * count + 4]
-    rest_high, rest_low, low_high, low_low = refs[PAIR * count + 4 :]
+    rest_high, rest_low, low_high, low_low, made_upper, made_lower, sent = refs[PAIR * count + 4 :]
     order, width = upper_ref.shape
-    on_upper = place_ref[0] == 0
+    on_upper = lax.rem(block, PAIR) == 0
     square_shape = (width, width)
     unit = jnp.where(
         lax.broadcasted_iota(jnp.int32, square_shape, 0) == lax.broadcasted_iota(jnp.int32, square_shape, 1), 1.0, 0.0
@@ -62,8 +78,8 @@
     total = jnp.zeros((8, width), jnp.float32)
     for step in range(groups):
         for side in range(PAIR):
-            group = lax.rem(place_ref[1] + step, groups)
-            column = group * PAIR + lax.rem(place_ref[2] + side, PAIR)
+            group = lax.rem(here // PAIR + step, groups)
+            column = group * PAIR + lax.rem(here + side, PAIR)
             same_ref = shares[step * PAIR + side]
             other_ref = shares[count + step * PAIR + side]
             same, other = same_ref[...], other_ref[...]
@@ -89,39 +105,51 @@
     upper = upper_ref[...].T
     lower = lower_ref[...].T
     gram = halves(product(reflect, reflect, 1))
-    bent = product(halves(upper), reflect, 1)
-    pulled = product(halves(jnp.concatenate([lower, bent], axis=0)), gram)
-    both = jnp.concatenate([bent - pulled[:width], pulled[:width] - pulled[width:]], axis=0)
-    inner = 0.3125 * both + 0.0625 * product(halves(both), gram)
-    inner = 0.375 * both + product(halves(inner), gram)
-    inner = 0.5 * both + product(halves(inner), gram)
-    new_upper_ref[...] = (upper - product(halves(lower - inner[:width]), reflect)).T
-    new_lower_ref[...] = (lower - bent + inner[width:]).T
-
-
-def step_call(place, shares, upper, lower, groups):
+    bent = thin_product(upper, reflect, 1)
+    pulled = thin_product(lower, gram)
+    inner_upper = inner_product(bent - pulled, gram)
+    inner_lower = inner_product(pulled - thin_product(bent, gram), gram)
+    made_lower[...] = (lower - bent + inner_lower).T
+    lower_copy = pltpu.make_async_copy(made_lower, new_lower_ref, sent.at[0])
+    lower_copy.start()
+    made_upper[...] = (upper - thin_product(lower - inner_upper, reflect)).T
+    upper_copy = pltpu.make_async_copy(made_upper, new_upper_ref, sent.at[1])
+    upper_copy.start()
+    lower_copy.wait()
+    upper_copy.wait()
+
+
+def step_call(shares, upper, lower, groups):
     order, width = upper.shape
     count = groups * PAIR
     in_vmem = pl.BlockSpec(memory_space=pltpu.VMEM)
     return pl.pallas_call(
         functools.partial(step_kernel, groups),
         out_shape=(jax.ShapeDtypeStruct(upper.shape, jnp.float32),) * 2,
-        in_specs=[pl.BlockSpec(memory_space=pltpu.SMEM)] + [in_vmem] * (len(shares) + 2),
-        out_specs=(in_vmem, in_vmem),
-        scratch_shapes=[pltpu.VMEM((count, order, width), jnp.bfloat16)] * 4,
+        in_specs=[in_vmem] * (len(shares) + 2),
+        out_specs=(pl.BlockSpec(memory_space=pl.ANY),) * 2,
+        scratch_shapes=[pltpu.VMEM((count, order, width), jnp.bfloat16)] * 4
+        + [pltpu.VMEM((order, width), jnp.float32)] * 2
+        + [pltpu.SemaphoreType.DMA((2,))],
         compiler_params=pltpu.CompilerParams(vmem_limit_bytes=48 * 1024 * 1024),
-    )(place, *shares, upper, lower)
-
-
-def spread(share, rows, row):
+    )(*shares, upper, lower)
+
+
+def spread(upper, lower, rows, row, flip):
     stride = 1
     while stride < rows:
         stride *= 2
+    share = lax.optimization_barrier(jnp.where(flip == 0, upper, lower))
     while stride > 1:
         stride //= 2
         pairs = [(first, first + stride) for first in range(0, rows - stride, 2 * stride)]
-        sends = [(PAIR * a + x, PAIR * b + x) for a, b in pairs for x in range(PAIR)]
-        received = lax.ppermute(share, "blk", sends)
+        sends = [[(PAIR * a + x, PAIR * b + x) for a, b in pairs] for x in range(PAIR)]
+        if 2 * stride >= rows:
+            received = jnp.where(
+                flip == 0, lax.ppermute(upper, "blk", sends[0]), lax.ppermute(lower, "blk", sends[1])
+            )
+        else:
+            received = lax.ppermute(share, "blk", sends[0] + sends[1])
         share = jnp.where(lax.rem(row, 2 * stride) == stride, received, share)
     return share
 
@@ -151,16 +179,15 @@
     blocks, size = lax.axis_size("blk"), lax.axis_size("col")
     assert upper_row.shape[1] == 1 and blocks % PAIR == 0 and size % PAIR == 0
     rows, groups = blocks // PAIR, size // PAIR
-    block, column = lax.axis_index("blk"), lax.axis_index("col")
+    block = lax.axis_index("blk")
     upper, lower = upper_row[:, 0, :], lower_row[:, 0, :]
     side = lax.rem(block, PAIR)
     swapped = lax.ppermute(upper, "blk", [(source, source ^ 1) for source in range(blocks)])
     ahead = [(source, source + PAIR) for source in range(0, blocks - PAIR, PAIR)]
     shifted = jnp.where(side == 1, swapped, lax.ppermute(swapped, "blk", ahead))
-    share = spread(jnp.where(side == 0, upper, lower), rows, block // PAIR)
+    share = spread(upper, lower, rows, block // PAIR, side)
     shares = exchange(share, rows, groups)
-    place = jnp.stack([side, column // PAIR, lax.rem(column, PAIR)]).astype(jnp.int32)
-    new_upper, new_lower = step_call(place, shares, shifted, lower, groups)
+    new_upper, new_lower = step_call(shares, shifted, lower, groups)
     return new_upper[:, None, :], new_lower[:, None, :]
 
 

time: 43.4 us -> 42.8 us (0.986)
  waiting for transfers between devices: 16 us -> 14.2 us
  starting transfers between devices: 17 us -> 18.6 us
  Pallas kernels: 8.1 us -> 7.57 us
    ppermute x2 -> x3, waiting for transfers between devices: 8.86 us -> 6.82 us  [the longest x1 4.12 us: spread(): lax.ppermute(upper, 'blk', sends[0])]
    ppermute x2 -> x3, starting transfers between devices: 7.26 us -> 7.94 us  [the longest x1 5.96 us: spread(): lax.ppermute(upper, 'blk', sends[0])]
    ppermute x1, starting transfers between devices: 1.56 us -> 2.24 us  [shards(): lax.ppermute(upper, 'blk', [(source, source ^ 1) for source in range(bloc...]
    pallas_call x1, Pallas kernels: 8.1 us -> 7.57 us  [step_call(): pl.pallas_call(functools.partial(step_kernel, groups), out_shape=(jax.Sha...]
  transfers between devices with their start and end apart: 11 -> 12, of which waited for: 7 -> 7; matrix products, arithmetic and copies ran while one was open for 0% -> 2% of each run, Pallas kernels for 0% -> 0%
where the time goes in v3:
time: 42.8 us; the launch traced here: 42.3 us
  starting transfers between devices  18.6 us (43%)
  waiting for transfers between devices  14.2 us (33%)
  Pallas kernels  7.57 us (18%)
  other arithmetic  1.08 us (3%)
  between operations  0.76 us (2%)
    pallas_call x1, Pallas kernels, step_call(): pl.pallas_call(functools.partial(step_kernel, groups), out_shape=(jax.Sha...  7.57 us
    ppermute x3, waiting for transfers between devices, exchange(): mine = lax.ppermute(share, ('blk', 'col'), sends) if flip or step else share  6.04 us
    ppermute x1, starting transfers between devices, spread(): lax.ppermute(upper, 'blk', sends[0])  5.96 us
    ppermute x1, starting transfers between devices, shards(): shifted = jnp.where(side == 1, swapped, lax.ppermute(swapped, 'blk', ahead))  4.39 us
    ppermute x1, waiting for transfers between devices, spread(): lax.ppermute(upper, 'blk', sends[0])  4.12 us
    ppermute x3, starting transfers between devices, exchange(): mine = lax.ppermute(share, ('blk', 'col'), sends) if flip or step else share  3.84 us
    ppermute x1, waiting for transfers between devices, spread(): received = lax.ppermute(share, 'blk', sends[0] + sends[1])  2.69 us
    ppermute x1, starting transfers between devices, shards(): lax.ppermute(upper, 'blk', [(source, source ^ 1) for source in range(bloc...  2.24 us
  transfers between devices with their start and end apart: 12, of which 7 were waited for; matrix products, arithmetic and copies ran while one was open for 2% of the time, Pallas kernels for 0%

profile of v3, /device:TPU:0, one launch (start us, length us, event | category | flops | bytes accessed | tf_op | source)
XLA Modules:
  0.0 42.3 jit_solution(10412290120900847947)
XLA Ops:
  0.6 6.0 %collective-permute-start = (f32[512,128]{1,0:T(8,128)}, f32[512,128]{1,0:T(8,128)S(1)}, u32[]{:S(2)}, u32[]{:S(2)}) collective-permute-start(f32[512,128]{1,0:T(8,128)} %bitcast.11), channel_id=1, source_target_pairs={{0,16},{1,17},{2,18},{3,19}} | collective-permute-start | bytes 786440 | tf_op jit(solution)/shard_map/ppermute | solution.py:149
  6.6 0.7 %collective-permute-start.1 = (f32[512,128]{1,0:T(8,128)}, f32[512,128]{1,0:T(8,128)S(1)}, u32[]{:S(2)}, u32[]{:S(2)}) collective-permute-start(f32[512,128]{1,0:T(8,128)} %bitcast.8), channel_id=1, source_target_pairs={{4,20},{5,21},{6,22},{7,23}} | collective-permute-start | bytes 786440 | tf_op jit(solution)/shard_map/ppermute | solution.py:149
  7.3 1.0 %broadcast_select_fusion.1 = f32[512,128]{1,0:T(8,128)S(1)} fusion(f32[512,128]{1,0:T(8,128)} %bitcast.12, f32[512,128]{1,0:T(8,128)} %bitcast.9, pred[]{:T(512)S(6)} %eq.15), kind=kLoop, calls=%fused_computation.2 | loop fusion | flops 65536 | bytes 786433 | tf_op jit(solution)/shard_map/jit(_where)/select_n | solution.py:142
  8.3 0.0 copy-start.1
  8.3 4.1 %collective-permute-done = f32[512,128]{1,0:T(8,128)S(1)} collective-permute-done((f32[512,128]{1,0:T(8,128)}, f32[512,128]{1,0:T(8,128)S(1)}, u32[]{:S(2)}, u32[]{:S(2)}) %collective-permute-start) | collective-permute-done | bytes 262176 | tf_op jit(solution)/shard_map/ppermute | solution.py:149
  12.4 0.0 collective-permute-done.1
  12.5 1.3 %collective-permute-start.2 = (f32[512,128]{1,0:T(8,128)S(1)}, f32[512,128]{1,0:T(8,128)S(1)}, u32[]{:S(2)}, u32[]{:S(2)}) collective-permute-start(f32[512,128]{1,0:T(8,128)S(1)} %select_select_fusion), channel_id=1, source_target_pairs={{0,8},{16,24},{4,12},{20,28},{1,9},{17,25},{5,13},{21,29},{2,10},{... | collective-permute-start | bytes 786440 | tf_op jit(solution)/shard_map/ppermute | solution.py:152
  13.8 0.0 copy-done.1
  13.8 2.2 %collective-permute-start.10 = (f32[512,128]{1,0:T(8,128)S(1)}, f32[512,128]{1,0:T(8,128)S(1)}, u32[]{:S(2)}, u32[]{:S(2)}) collective-permute-start(f32[512,128]{1,0:T(8,128)S(1)} %bitcast.13), channel_id=1, source_target_pairs={{0,4},{4,0},{8,12},{12,8},{16,20},{20,16},{24,28},{28,24},{1,5},{5... | collective-permute-start | bytes 786440 | tf_op jit(solution)/shard_map/ppermute | solution.py:185
  16.0 2.7 %collective-permute-done.2 = f32[512,128]{1,0:T(8,128)S(1)} collective-permute-done((f32[512,128]{1,0:T(8,128)S(1)}, f32[512,128]{1,0:T(8,128)S(1)}, u32[]{:S(2)}, u32[]{:S(2)}) %collective-permute-start.2) | collective-permute-done | bytes 262176 | tf_op jit(solution)/shard_map/ppermute | solution.py:152
  18.8 3.2 %collective-permute-start.8 = (f32[512,128]{1,0:T(8,128)S(1)}, f32[512,128]{1,0:T(8,128)S(1)}, u32[]{:S(2)}, u32[]{:S(2)}) collective-permute-start(f32[512,128]{1,0:T(8,128)S(1)} %broadcast_select_fusion.2.refs_0_), channel_id=1, source_target_pairs={{6,0},{7,1},{4,2},{5,3},{2,4},{3,5},{0,6},{1,7},{14,8},{15,9},{12,... | collective-permute-start | bytes 786440 | tf_op jit(solution)/shard_map/ppermute | solution.py:172
  22.0 0.0 collective-permute-start.6
  22.0 0.6 %collective-permute-start.4 = (f32[512,128]{1,0:T(8,128)S(1)}, f32[512,128]{1,0:T(8,128)S(1)}, u32[]{:S(2)}, u32[]{:S(2)}) collective-permute-start(f32[512,128]{1,0:T(8,128)S(1)} %broadcast_select_fusion.2.refs_0_), channel_id=1, source_target_pairs={{2,0},{3,1},{0,2},{1,3},{6,4},{7,5},{4,6},{5,7},{10,8},{11,9},{8,1... | collective-permute-start | bytes 786440 | tf_op jit(solution)/shard_map/ppermute | solution.py:172
  22.6 0.0 collective-permute-done.10
  22.6 4.4 %collective-permute-start.11 = (f32[512,128]{1,0:T(8,128)S(1)}, f32[512,128]{1,0:T(8,128)S(1)}, u32[]{:S(2)}, u32[]{:S(2)}) collective-permute-start(f32[512,128]{1,0:T(8,128)S(1)} %collective-permute-done.10), channel_id=1, source_target_pairs={{0,8},{8,16},{16,24},{1,9},{9,17},{17,25},{2,10},{10,18},{18,26},{... | collective-permute-start | bytes 786440 | tf_op jit(solution)/shard_map/ppermute | solution.py:187
  27.0 0.1 collective-permute-start.3
  27.1 2.2 %collective-permute-done.8.refs_6_ = f32[512,128]{1,0:T(8,128)S(1)} collective-permute-done((f32[512,128]{1,0:T(8,128)S(1)}, f32[512,128]{1,0:T(8,128)S(1)}, u32[]{:S(2)}, u32[]{:S(2)}) %collective-permute-start.8) | collective-permute-done | bytes 262176 | tf_op jit(solution)/shard_map/ppermute | solution.py:172
  29.3 0.0 collective-permute-start.9
  29.3 3.4 %collective-permute-done.6.refs_4_ = f32[512,128]{1,0:T(8,128)S(1)} collective-permute-done((f32[512,128]{1,0:T(8,128)S(1)}, f32[512,128]{1,0:T(8,128)S(1)}, u32[]{:S(2)}, u32[]{:S(2)}) %collective-permute-start.6) | collective-permute-done | bytes 262176 | tf_op jit(solution)/shard_map/ppermute | solution.py:172
  32.8 0.0 collective-permute-start.7
  32.8 0.4 collective-permute-done.4.refs_2_
  33.1 0.1 collective-permute-start.5
  33.3 0.0 copy-start
  33.3 0.0 collective-permute-done.11
  33.3 0.0 collective-permute-done.3.refs_1_
  33.3 0.0 collective-permute-done.9.refs_7_
  33.3 1.0 %collective-permute-done.7.refs_5_ = f32[512,128]{1,0:T(8,128)S(1)} collective-permute-done((f32[512,128]{1,0:T(8,128)S(1)}, f32[512,128]{1,0:T(8,128)S(1)}, u32[]{:S(2)}, u32[]{:S(2)}) %collective-permute-start.7) | collective-permute-done | bytes 262176 | tf_op jit(solution)/shard_map/ppermute | solution.py:174
  34.3 0.4 collective-permute-done.5.refs_3_
  34.7 0.0 copy-done
  34.7 7.6 %shard_map.41 = (f32[512,128]{1,0:T(8,128)}, f32[512,128]{1,0:T(8,128)}) custom-call(f32[512,128]{1,0:T(8,128)S(1)} %broadcast_select_fusion.2.refs_0_, f32[512,128]{1,0:T(8,128)S(1)} %collective-permute-done.3.refs_1_, f32[512,128]{1,0:T(8,128)S(1)} %collective-permute-done.4.refs_2_, f32[512,128]{1,0:T(8,128)S(1)} %collective-permute-done.5.refs_3_, ...), custom_call_target="tpu_custom_call" | custom-call | tf_op jit(solution)/shard_map/pallas_call | solution.py:126
  (3 shorter events, 0.1 us)
Async XLA Ops:
  0.6 11.8 %collective-permute-start = (f32[512,128]{1,0:T(8,128)}, f32[512,128]{1,0:T(8,128)S(1)}, u32[]{:S(2)}, u32[]{:S(2)}) collective-permute-start(f32[512,128]{1,0:T(8,128)} %bitcast.11), channel_id=1, source_target_pairs={{0,16},{1,17},{2,18},{3,19}} | collective-permute-start | bytes 786440 | tf_op jit(solution)/shard_map/ppermute | solution.py:149
  6.6 5.8 %collective-permute-start.1 = (f32[512,128]{1,0:T(8,128)}, f32[512,128]{1,0:T(8,128)S(1)}, u32[]{:S(2)}, u32[]{:S(2)}) collective-permute-start(f32[512,128]{1,0:T(8,128)} %bitcast.8), channel_id=1, source_target_pairs={{4,20},{5,21},{6,22},{7,23}} | collective-permute-start | bytes 786440 | tf_op jit(solution)/shard_map/ppermute | solution.py:149
  8.3 5.5 %copy-start.1 = (f32[512,1,128]{2,1,0:T(1,128)S(1)}, f32[512,1,128]{2,1,0:T(1,128)}, u32[]{:S(2)}) copy-start(f32[512,1,128]{2,1,0:T(1,128)} %param.2) | copy-start | bytes 786436
  12.5 6.3 %collective-permute-start.2 = (f32[512,128]{1,0:T(8,128)S(1)}, f32[512,128]{1,0:T(8,128)S(1)}, u32[]{:S(2)}, u32[]{:S(2)}) collective-permute-start(f32[512,128]{1,0:T(8,128)S(1)} %select_select_fusion), channel_id=1, source_target_pairs={{0,8},{16,24},{4,12},{20,28},{1,9},{17,25},{5,13},{21,29},{2,10},{... | collective-permute-start | bytes 786440 | tf_op jit(solution)/shard_map/ppermute | solution.py:152
  13.8 8.8 %collective-permute-start.10 = (f32[512,128]{1,0:T(8,128)S(1)}, f32[512,128]{1,0:T(8,128)S(1)}, u32[]{:S(2)}, u32[]{:S(2)}) collective-permute-start(f32[512,128]{1,0:T(8,128)S(1)} %bitcast.13), channel_id=1, source_target_pairs={{0,4},{4,0},{8,12},{12,8},{16,20},{20,16},{24,28},{28,24},{1,5},{5... | collective-permute-start | bytes 786440 | tf_op jit(solution)/shard_map/ppermute | solution.py:185
  18.8 10.6 %collective-permute-start.8 = (f32[512,128]{1,0:T(8,128)S(1)}, f32[512,128]{1,0:T(8,128)S(1)}, u32[]{:S(2)}, u32[]{:S(2)}) collective-permute-start(f32[512,128]{1,0:T(8,128)S(1)} %broadcast_select_fusion.2.refs_0_), channel_id=1, source_target_pairs={{6,0},{7,1},{4,2},{5,3},{2,4},{3,5},{0,6},{1,7},{14,8},{15,9},{12,... | collective-permute-start | bytes 786440 | tf_op jit(solution)/shard_map/ppermute | solution.py:172
  22.0 10.8 %collective-permute-start.6 = (f32[512,128]{1,0:T(8,128)S(1)}, f32[512,128]{1,0:T(8,128)S(1)}, u32[]{:S(2)}, u32[]{:S(2)}) collective-permute-start(f32[512,128]{1,0:T(8,128)S(1)} %broadcast_select_fusion.2.refs_0_), channel_id=1, source_target_pairs={{4,0},{5,1},{6,2},{7,3},{0,4},{1,5},{2,6},{3,7},{12,8},{13,9},{14,... | collective-permute-start | bytes 786440 | tf_op jit(solution)/shard_map/ppermute | solution.py:172
  22.0 11.2 %collective-permute-start.4 = (f32[512,128]{1,0:T(8,128)S(1)}, f32[512,128]{1,0:T(8,128)S(1)}, u32[]{:S(2)}, u32[]{:S(2)}) collective-permute-start(f32[512,128]{1,0:T(8,128)S(1)} %broadcast_select_fusion.2.refs_0_), channel_id=1, source_target_pairs={{2,0},{3,1},{0,2},{1,3},{6,4},{7,5},{4,6},{5,7},{10,8},{11,9},{8,1... | collective-permute-start | bytes 786440 | tf_op jit(solution)/shard_map/ppermute | solution.py:172
  22.6 10.7 %collective-permute-start.11 = (f32[512,128]{1,0:T(8,128)S(1)}, f32[512,128]{1,0:T(8,128)S(1)}, u32[]{:S(2)}, u32[]{:S(2)}) collective-permute-start(f32[512,128]{1,0:T(8,128)S(1)} %collective-permute-done.10), channel_id=1, source_target_pairs={{0,8},{8,16},{16,24},{1,9},{9,17},{17,25},{2,10},{10,18},{18,26},{... | collective-permute-start | bytes 786440 | tf_op jit(solution)/shard_map/ppermute | solution.py:187
  27.0 6.3 %collective-permute-start.3 = (f32[512,128]{1,0:T(8,128)S(1)}, f32[512,128]{1,0:T(8,128)S(1)}, u32[]{:S(2)}, u32[]{:S(2)}) collective-permute-start(f32[512,128]{1,0:T(8,128)S(1)} %broadcast_select_fusion.2.refs_0_), channel_id=1, source_target_pairs={{0,1},{1,0},{2,3},{3,2},{4,5},{5,4},{6,7},{7,6},{8,9},{9,8},{10,11... | collective-permute-start | bytes 786440 | tf_op jit(solution)/shard_map/ppermute | solution.py:174
  29.3 4.0 %collective-permute-start.9 = (f32[512,128]{1,0:T(8,128)S(1)}, f32[512,128]{1,0:T(8,128)S(1)}, u32[]{:S(2)}, u32[]{:S(2)}) collective-permute-start(f32[512,128]{1,0:T(8,128)S(1)} %collective-permute-done.8.refs_6_), channel_id=1, source_target_pairs={{0,1},{1,0},{2,3},{3,2},{4,5},{5,4},{6,7},{7,6},{8,9},{9,8},{10,11... | collective-permute-start | bytes 786440 | tf_op jit(solution)/shard_map/ppermute | solution.py:174
  32.8 1.5 %collective-permute-start.7 = (f32[512,128]{1,0:T(8,128)S(1)}, f32[512,128]{1,0:T(8,128)S(1)}, u32[]{:S(2)}, u32[]{:S(2)}) collective-permute-start(f32[512,128]{1,0:T(8,128)S(1)} %collective-permute-done.6.refs_4_), channel_id=1, source_target_pairs={{0,1},{1,0},{2,3},{3,2},{4,5},{5,4},{6,7},{7,6},{8,9},{9,8},{10,11... | collective-permute-start | bytes 786440 | tf_op jit(solution)/shard_map/ppermute | solution.py:174
  33.1 1.5 %collective-permute-start.5 = (f32[512,128]{1,0:T(8,128)S(1)}, f32[512,128]{1,0:T(8,128)S(1)}, u32[]{:S(2)}, u32[]{:S(2)}) collective-permute-start(f32[512,128]{1,0:T(8,128)S(1)} %collective-permute-done.4.refs_2_), channel_id=1, source_target_pairs={{0,1},{1,0},{2,3},{3,2},{4,5},{5,4},{6,7},{7,6},{8,9},{9,8},{10,11... | collective-permute-start | bytes 786440 | tf_op jit(solution)/shard_map/ppermute | solution.py:174
  33.3 1.4 %copy-start = (f32[512,1,128]{2,1,0:T(1,128)S(1)}, f32[512,1,128]{2,1,0:T(1,128)}, u32[]{:S(2)}) copy-start(f32[512,1,128]{2,1,0:T(1,128)} %param.3) | copy-start | bytes 786436

commit v4 on v3

--- a/solution.py
+++ b/solution.py
@@ -39,12 +39,6 @@
     return both[: left.shape[0]] + both[left.shape[0] :] + dot(left_high, right_low, side)
 
 
-def inner_product(left, gram):
-    inner = 0.3125 * left + 0.0625 * thin_product(left, gram)
-    inner = 0.375 * left + thin_product(inner, gram)
-    return 0.5 * left + thin_product(inner, gram)
-
-
 def add_diagonal(matrix, block):
     width = block.shape[0]
     count = matrix.shape[0] // width
@@ -65,54 +59,53 @@
 
 def step_kernel(groups, *refs):
     count = groups * PAIR
-    block, here = lax.axis_index("blk"), lax.axis_index("col")
     shares = refs[: PAIR * count]
     upper_ref, lower_ref, new_upper_ref, new_lower_ref = refs[PAIR * count : PAIR * count + 4]
     rest_high, rest_low, low_high, low_low, made_upper, made_lower, sent = refs[PAIR * count + 4 :]
     order, width = upper_ref.shape
+    block, here = lax.axis_index("blk"), lax.axis_index("col")
     on_upper = lax.rem(block, PAIR) == 0
     square_shape = (width, width)
     unit = jnp.where(
         lax.broadcasted_iota(jnp.int32, square_shape, 0) == lax.broadcasted_iota(jnp.int32, square_shape, 1), 1.0, 0.0
     )
-    total = jnp.zeros((8, width), jnp.float32)
+    rows = []
     for step in range(groups):
         for side in range(PAIR):
-            group = lax.rem(here // PAIR + step, groups)
-            column = group * PAIR + lax.rem(here + side, PAIR)
-            same_ref = shares[step * PAIR + side]
-            other_ref = shares[count + step * PAIR + side]
-            same, other = same_ref[...], other_ref[...]
-            head = jnp.where(on_upper, same, other)
+            column = lax.rem(here // PAIR + step, groups) * PAIR + lax.rem(here + side, PAIR)
+            rows.append(pl.ds(pl.multiple_of(column * width, width), width))
+    total = jnp.zeros((8, width), jnp.float32)
+    for i in range(count):
+        columns = slice(i * width, (i + 1) * width)
+        for j in range(count):
+            head = jnp.where(on_upper, shares[i][rows[j], :], shares[count + i][rows[j], :])
             total = total + jnp.sum((head * head).reshape(-1, 8, width), axis=0)
-            rest_high[column], rest_low[column] = halves(head)
-            near = pl.ds(pl.multiple_of(column * width, width), width)
-            diagonal = jnp.where(on_upper, same_ref[near, :], other_ref[near, :]) - LEAD * unit
-            rest_high[column, near, :], rest_low[column, near, :] = halves(diagonal)
-            low_high[column], low_low[column] = halves(jnp.where(on_upper, other, same))
+            to = slice(j * width, (j + 1) * width)
+            rest_high[to, columns], rest_low[to, columns] = halves(head - LEAD * unit if i == j else head)
+        low_high[:, columns], low_low[:, columns] = halves(jnp.where(on_upper, shares[count + i][...], shares[i][...]))
     scale = lax.rsqrt(jnp.full((1, 1), jnp.sum(total)) / order + 1e-06)
     shift = 1.0 - LEAD * scale
-
-    def joined(ref):
-        return jnp.concatenate([ref[column] for column in range(count)], axis=1)
-
-    rest = (joined(rest_high), joined(rest_low))
-    low = (joined(low_high), joined(low_low))
+    rest = (rest_high[...], rest_low[...])
+    low = (low_high[...], low_low[...])
     square = (scale * scale) * product(rest, rest) - (2.0 * shift * scale) * whole(rest)
     square = halves(add_diagonal(square, shift * shift * unit))
     middle = (1.0 + shift) * whole(low) - scale * product(low, rest)
     reflect = halves((middle + product(halves(middle), square)) * scale)
-    upper = upper_ref[...].T
+    upper = jnp.concatenate([upper_ref[part, :].T for part in rows], axis=1)
     lower = lower_ref[...].T
     gram = halves(product(reflect, reflect, 1))
     bent = thin_product(upper, reflect, 1)
     pulled = thin_product(lower, gram)
-    inner_upper = inner_product(bent - pulled, gram)
-    inner_lower = inner_product(pulled - thin_product(bent, gram), gram)
+    bases = [bent - pulled, pulled - thin_product(bent, gram)]
+    inners = [0.3125 * base + 0.0625 * thin_product(base, gram) for base in bases]
+    inners = [0.375 * base + thin_product(inner, gram) for base, inner in zip(bases, inners)]
+    inner_upper, inner_lower = [0.5 * base + thin_product(inner, gram) for base, inner in zip(bases, inners)]
     made_lower[...] = (lower - bent + inner_lower).T
     lower_copy = pltpu.make_async_copy(made_lower, new_lower_ref, sent.at[0])
     lower_copy.start()
-    made_upper[...] = (upper - thin_product(lower - inner_upper, reflect)).T
+    upper = upper - thin_product(lower - inner_upper, reflect)
+    for i, part in enumerate(rows):
+        made_upper[part, :] = upper[:, i * width : (i + 1) * width].T
     upper_copy = pltpu.make_async_copy(made_upper, new_upper_ref, sent.at[1])
     upper_copy.start()
     lower_copy.wait()
@@ -128,7 +121,7 @@
         out_shape=(jax.ShapeDtypeStruct(upper.shape, jnp.float32),) * 2,
         in_specs=[in_vmem] * (len(shares) + 2),
         out_specs=(pl.BlockSpec(memory_space=pl.ANY),) * 2,
-        scratch_shapes=[pltpu.VMEM((count, order, width), jnp.bfloat16)] * 4
+        scratch_shapes=[pltpu.VMEM((order, order), jnp.bfloat16)] * 4
         + [pltpu.VMEM((order, width), jnp.float32)] * 2
         + [pltpu.SemaphoreType.DMA((2,))],
         compiler_params=pltpu.CompilerParams(vmem_limit_bytes=48 * 1024 * 1024),

time: 42.8 us -> 42 us (0.981)
  Pallas kernels: 7.57 us -> 6.8 us
    pallas_call x1, Pallas kernels: 7.57 us -> 6.8 us  [step_call(): pl.pallas_call(functools.partial(step_kernel, groups), out_shape=(jax.Sha...]
  transfers between devices with their start and end apart: 12 -> 12, of which waited for: 7 -> 7; matrix products, arithmetic and copies ran while one was open for 2% -> 3% of each run, Pallas kernels for 0% -> 0%
where the time goes in v4:
time: 42 us; the launch traced here: 41.5 us
  starting transfers between devices  18.6 us (44%)
  waiting for transfers between devices  14.2 us (34%)
  Pallas kernels  6.8 us (16%)
  other arithmetic  1.08 us (3%)
  between operations  0.76 us (2%)
    pallas_call x1, Pallas kernels, step_call(): pl.pallas_call(functools.partial(step_kernel, groups), out_shape=(jax.Sha...  6.8 us
    ppermute x3, waiting for transfers between devices, exchange(): mine = lax.ppermute(share, ('blk', 'col'), sends) if flip or step else share  6.04 us
    ppermute x1, starting transfers between devices, spread(): lax.ppermute(upper, 'blk', sends[0])  5.96 us
    ppermute x1, starting transfers between devices, shards(): shifted = jnp.where(side == 1, swapped, lax.ppermute(swapped, 'blk', ahead))  4.39 us
    ppermute x1, waiting for transfers between devices, spread(): lax.ppermute(upper, 'blk', sends[0])  4.12 us
    ppermute x3, starting transfers between devices, exchange(): mine = lax.ppermute(share, ('blk', 'col'), sends) if flip or step else share  3.84 us
    ppermute x1, waiting for transfers between devices, spread(): received = lax.ppermute(share, 'blk', sends[0] + sends[1])  2.69 us
    ppermute x1, starting transfers between devices, shards(): lax.ppermute(upper, 'blk', [(source, source ^ 1) for source in range(bloc...  2.24 us
  transfers between devices with their start and end apart: 12, of which 7 were waited for; matrix products, arithmetic and copies ran while one was open for 3% of the time, Pallas kernels for 0%

profile of v4, /device:TPU:0, one launch (start us, length us, event | category | flops | bytes accessed | tf_op | source)
XLA Modules:
  0.0 41.5 jit_solution(10040821300983068143)
XLA Ops:
  0.6 6.0 %collective-permute-start = (f32[512,128]{1,0:T(8,128)}, f32[512,128]{1,0:T(8,128)S(1)}, u32[]{:S(2)}, u32[]{:S(2)}) collective-permute-start(f32[512,128]{1,0:T(8,128)} %bitcast.11), channel_id=1, source_target_pairs={{0,16},{1,17},{2,18},{3,19}} | collective-permute-start | bytes 786440 | tf_op jit(solution)/shard_map/ppermute | solution.py:142
  6.6 0.7 %collective-permute-start.1 = (f32[512,128]{1,0:T(8,128)}, f32[512,128]{1,0:T(8,128)S(1)}, u32[]{:S(2)}, u32[]{:S(2)}) collective-permute-start(f32[512,128]{1,0:T(8,128)} %bitcast.8), channel_id=1, source_target_pairs={{4,20},{5,21},{6,22},{7,23}} | collective-permute-start | bytes 786440 | tf_op jit(solution)/shard_map/ppermute | solution.py:142
  7.3 1.0 %broadcast_select_fusion.1 = f32[512,128]{1,0:T(8,128)S(1)} fusion(f32[512,128]{1,0:T(8,128)} %bitcast.12, f32[512,128]{1,0:T(8,128)} %bitcast.9, pred[]{:T(512)S(6)} %eq.15), kind=kLoop, calls=%fused_computation.2 | loop fusion | flops 65536 | bytes 786433 | tf_op jit(solution)/shard_map/jit(_where)/select_n | solution.py:135
  8.3 0.0 copy-start.1
  8.3 4.1 %collective-permute-done = f32[512,128]{1,0:T(8,128)S(1)} collective-permute-done((f32[512,128]{1,0:T(8,128)}, f32[512,128]{1,0:T(8,128)S(1)}, u32[]{:S(2)}, u32[]{:S(2)}) %collective-permute-start) | collective-permute-done | bytes 262176 | tf_op jit(solution)/shard_map/ppermute | solution.py:142
  12.4 0.0 collective-permute-done.1
  12.5 1.3 %collective-permute-start.2 = (f32[512,128]{1,0:T(8,128)S(1)}, f32[512,128]{1,0:T(8,128)S(1)}, u32[]{:S(2)}, u32[]{:S(2)}) collective-permute-start(f32[512,128]{1,0:T(8,128)S(1)} %select_select_fusion), channel_id=1, source_target_pairs={{0,8},{16,24},{4,12},{20,28},{1,9},{17,25},{5,13},{21,29},{2,10},{... | collective-permute-start | bytes 786440 | tf_op jit(solution)/shard_map/ppermute | solution.py:145
  13.8 0.0 copy-done.1
  13.8 2.2 %collective-permute-start.10 = (f32[512,128]{1,0:T(8,128)S(1)}, f32[512,128]{1,0:T(8,128)S(1)}, u32[]{:S(2)}, u32[]{:S(2)}) collective-permute-start(f32[512,128]{1,0:T(8,128)S(1)} %bitcast.13), channel_id=1, source_target_pairs={{0,4},{4,0},{8,12},{12,8},{16,20},{20,16},{24,28},{28,24},{1,5},{5... | collective-permute-start | bytes 786440 | tf_op jit(solution)/shard_map/ppermute | solution.py:178
  16.0 2.7 %collective-permute-done.2 = f32[512,128]{1,0:T(8,128)S(1)} collective-permute-done((f32[512,128]{1,0:T(8,128)S(1)}, f32[512,128]{1,0:T(8,128)S(1)}, u32[]{:S(2)}, u32[]{:S(2)}) %collective-permute-start.2) | collective-permute-done | bytes 262176 | tf_op jit(solution)/shard_map/ppermute | solution.py:145
  18.8 3.2 %collective-permute-start.8 = (f32[512,128]{1,0:T(8,128)S(1)}, f32[512,128]{1,0:T(8,128)S(1)}, u32[]{:S(2)}, u32[]{:S(2)}) collective-permute-start(f32[512,128]{1,0:T(8,128)S(1)} %broadcast_select_fusion.2.refs_0_), channel_id=1, source_target_pairs={{6,0},{7,1},{4,2},{5,3},{2,4},{3,5},{0,6},{1,7},{14,8},{15,9},{12,... | collective-permute-start | bytes 786440 | tf_op jit(solution)/shard_map/ppermute | solution.py:165
  22.0 0.0 collective-permute-start.6
  22.0 0.6 %collective-permute-start.4 = (f32[512,128]{1,0:T(8,128)S(1)}, f32[512,128]{1,0:T(8,128)S(1)}, u32[]{:S(2)}, u32[]{:S(2)}) collective-permute-start(f32[512,128]{1,0:T(8,128)S(1)} %broadcast_select_fusion.2.refs_0_), channel_id=1, source_target_pairs={{2,0},{3,1},{0,2},{1,3},{6,4},{7,5},{4,6},{5,7},{10,8},{11,9},{8,1... | collective-permute-start | bytes 786440 | tf_op jit(solution)/shard_map/ppermute | solution.py:165
  22.6 0.0 collective-permute-done.10
  22.6 4.4 %collective-permute-start.11 = (f32[512,128]{1,0:T(8,128)S(1)}, f32[512,128]{1,0:T(8,128)S(1)}, u32[]{:S(2)}, u32[]{:S(2)}) collective-permute-start(f32[512,128]{1,0:T(8,128)S(1)} %collective-permute-done.10), channel_id=1, source_target_pairs={{0,8},{8,16},{16,24},{1,9},{9,17},{17,25},{2,10},{10,18},{18,26},{... | collective-permute-start | bytes 786440 | tf_op jit(solution)/shard_map/ppermute | solution.py:180
  27.0 0.1 collective-permute-start.3
  27.1 2.2 %collective-permute-done.8.refs_6_ = f32[512,128]{1,0:T(8,128)S(1)} collective-permute-done((f32[512,128]{1,0:T(8,128)S(1)}, f32[512,128]{1,0:T(8,128)S(1)}, u32[]{:S(2)}, u32[]{:S(2)}) %collective-permute-start.8) | collective-permute-done | bytes 262176 | tf_op jit(solution)/shard_map/ppermute | solution.py:165
  29.3 0.0 collective-permute-start.9
  29.3 3.4 %collective-permute-done.6.refs_4_ = f32[512,128]{1,0:T(8,128)S(1)} collective-permute-done((f32[512,128]{1,0:T(8,128)S(1)}, f32[512,128]{1,0:T(8,128)S(1)}, u32[]{:S(2)}, u32[]{:S(2)}) %collective-permute-start.6) | collective-permute-done | bytes 262176 | tf_op jit(solution)/shard_map/ppermute | solution.py:165
  32.8 0.0 collective-permute-start.7
  32.8 0.4 collective-permute-done.4.refs_2_
  33.1 0.1 collective-permute-start.5
  33.3 0.0 copy-start
  33.3 0.0 collective-permute-done.11
  33.3 0.0 collective-permute-done.3.refs_1_
  33.3 0.0 collective-permute-done.9.refs_7_
  33.3 1.0 %collective-permute-done.7.refs_5_ = f32[512,128]{1,0:T(8,128)S(1)} collective-permute-done((f32[512,128]{1,0:T(8,128)S(1)}, f32[512,128]{1,0:T(8,128)S(1)}, u32[]{:S(2)}, u32[]{:S(2)}) %collective-permute-start.7) | collective-permute-done | bytes 262176 | tf_op jit(solution)/shard_map/ppermute | solution.py:167
  34.3 0.4 collective-permute-done.5.refs_3_
  34.7 0.0 copy-done
  34.7 6.8 %shard_map.41 = (f32[512,128]{1,0:T(8,128)}, f32[512,128]{1,0:T(8,128)}) custom-call(f32[512,128]{1,0:T(8,128)S(1)} %broadcast_select_fusion.2.refs_0_, f32[512,128]{1,0:T(8,128)S(1)} %collective-permute-done.3.refs_1_, f32[512,128]{1,0:T(8,128)S(1)} %collective-permute-done.4.refs_2_, f32[512,128]{1,0:T(8,128)S(1)} %collective-permute-done.5.refs_3_, ...), custom_call_target="tpu_custom_call" | custom-call | tf_op jit(solution)/shard_map/pallas_call | solution.py:119
  (3 shorter events, 0.1 us)
Async XLA Ops:
  0.6 11.8 %collective-permute-start = (f32[512,128]{1,0:T(8,128)}, f32[512,128]{1,0:T(8,128)S(1)}, u32[]{:S(2)}, u32[]{:S(2)}) collective-permute-start(f32[512,128]{1,0:T(8,128)} %bitcast.11), channel_id=1, source_target_pairs={{0,16},{1,17},{2,18},{3,19}} | collective-permute-start | bytes 786440 | tf_op jit(solution)/shard_map/ppermute | solution.py:142
  6.6 5.8 %collective-permute-start.1 = (f32[512,128]{1,0:T(8,128)}, f32[512,128]{1,0:T(8,128)S(1)}, u32[]{:S(2)}, u32[]{:S(2)}) collective-permute-start(f32[512,128]{1,0:T(8,128)} %bitcast.8), channel_id=1, source_target_pairs={{4,20},{5,21},{6,22},{7,23}} | collective-permute-start | bytes 786440 | tf_op jit(solution)/shard_map/ppermute | solution.py:142
  8.3 5.5 %copy-start.1 = (f32[512,1,128]{2,1,0:T(1,128)S(1)}, f32[512,1,128]{2,1,0:T(1,128)}, u32[]{:S(2)}) copy-start(f32[512,1,128]{2,1,0:T(1,128)} %param.2) | copy-start | bytes 786436
  12.5 6.3 %collective-permute-start.2 = (f32[512,128]{1,0:T(8,128)S(1)}, f32[512,128]{1,0:T(8,128)S(1)}, u32[]{:S(2)}, u32[]{:S(2)}) collective-permute-start(f32[512,128]{1,0:T(8,128)S(1)} %select_select_fusion), channel_id=1, source_target_pairs={{0,8},{16,24},{4,12},{20,28},{1,9},{17,25},{5,13},{21,29},{2,10},{... | collective-permute-start | bytes 786440 | tf_op jit(solution)/shard_map/ppermute | solution.py:145
  13.8 8.8 %collective-permute-start.10 = (f32[512,128]{1,0:T(8,128)S(1)}, f32[512,128]{1,0:T(8,128)S(1)}, u32[]{:S(2)}, u32[]{:S(2)}) collective-permute-start(f32[512,128]{1,0:T(8,128)S(1)} %bitcast.13), channel_id=1, source_target_pairs={{0,4},{4,0},{8,12},{12,8},{16,20},{20,16},{24,28},{28,24},{1,5},{5... | collective-permute-start | bytes 786440 | tf_op jit(solution)/shard_map/ppermute | solution.py:178
  18.8 10.6 %collective-permute-start.8 = (f32[512,128]{1,0:T(8,128)S(1)}, f32[512,128]{1,0:T(8,128)S(1)}, u32[]{:S(2)}, u32[]{:S(2)}) collective-permute-start(f32[512,128]{1,0:T(8,128)S(1)} %broadcast_select_fusion.2.refs_0_), channel_id=1, source_target_pairs={{6,0},{7,1},{4,2},{5,3},{2,4},{3,5},{0,6},{1,7},{14,8},{15,9},{12,... | collective-permute-start | bytes 786440 | tf_op jit(solution)/shard_map/ppermute | solution.py:165
  22.0 10.8 %collective-permute-start.6 = (f32[512,128]{1,0:T(8,128)S(1)}, f32[512,128]{1,0:T(8,128)S(1)}, u32[]{:S(2)}, u32[]{:S(2)}) collective-permute-start(f32[512,128]{1,0:T(8,128)S(1)} %broadcast_select_fusion.2.refs_0_), channel_id=1, source_target_pairs={{4,0},{5,1},{6,2},{7,3},{0,4},{1,5},{2,6},{3,7},{12,8},{13,9},{14,... | collective-permute-start | bytes 786440 | tf_op jit(solution)/shard_map/ppermute | solution.py:165
  22.0 11.2 %collective-permute-start.4 = (f32[512,128]{1,0:T(8,128)S(1)}, f32[512,128]{1,0:T(8,128)S(1)}, u32[]{:S(2)}, u32[]{:S(2)}) collective-permute-start(f32[512,128]{1,0:T(8,128)S(1)} %broadcast_select_fusion.2.refs_0_), channel_id=1, source_target_pairs={{2,0},{3,1},{0,2},{1,3},{6,4},{7,5},{4,6},{5,7},{10,8},{11,9},{8,1... | collective-permute-start | bytes 786440 | tf_op jit(solution)/shard_map/ppermute | solution.py:165
  22.6 10.7 %collective-permute-start.11 = (f32[512,128]{1,0:T(8,128)S(1)}, f32[512,128]{1,0:T(8,128)S(1)}, u32[]{:S(2)}, u32[]{:S(2)}) collective-permute-start(f32[512,128]{1,0:T(8,128)S(1)} %collective-permute-done.10), channel_id=1, source_target_pairs={{0,8},{8,16},{16,24},{1,9},{9,17},{17,25},{2,10},{10,18},{18,26},{... | collective-permute-start | bytes 786440 | tf_op jit(solution)/shard_map/ppermute | solution.py:180
  27.0 6.3 %collective-permute-start.3 = (f32[512,128]{1,0:T(8,128)S(1)}, f32[512,128]{1,0:T(8,128)S(1)}, u32[]{:S(2)}, u32[]{:S(2)}) collective-permute-start(f32[512,128]{1,0:T(8,128)S(1)} %broadcast_select_fusion.2.refs_0_), channel_id=1, source_target_pairs={{0,1},{1,0},{2,3},{3,2},{4,5},{5,4},{6,7},{7,6},{8,9},{9,8},{10,11... | collective-permute-start | bytes 786440 | tf_op jit(solution)/shard_map/ppermute | solution.py:167
  29.3 4.0 %collective-permute-start.9 = (f32[512,128]{1,0:T(8,128)S(1)}, f32[512,128]{1,0:T(8,128)S(1)}, u32[]{:S(2)}, u32[]{:S(2)}) collective-permute-start(f32[512,128]{1,0:T(8,128)S(1)} %collective-permute-done.8.refs_6_), channel_id=1, source_target_pairs={{0,1},{1,0},{2,3},{3,2},{4,5},{5,4},{6,7},{7,6},{8,9},{9,8},{10,11... | collective-permute-start | bytes 786440 | tf_op jit(solution)/shard_map/ppermute | solution.py:167
  32.8 1.5 %collective-permute-start.7 = (f32[512,128]{1,0:T(8,128)S(1)}, f32[512,128]{1,0:T(8,128)S(1)}, u32[]{:S(2)}, u32[]{:S(2)}) collective-permute-start(f32[512,128]{1,0:T(8,128)S(1)} %collective-permute-done.6.refs_4_), channel_id=1, source_target_pairs={{0,1},{1,0},{2,3},{3,2},{4,5},{5,4},{6,7},{7,6},{8,9},{9,8},{10,11... | collective-permute-start | bytes 786440 | tf_op jit(solution)/shard_map/ppermute | solution.py:167
  33.1 1.5 %collective-permute-start.5 = (f32[512,128]{1,0:T(8,128)S(1)}, f32[512,128]{1,0:T(8,128)S(1)}, u32[]{:S(2)}, u32[]{:S(2)}) collective-permute-start(f32[512,128]{1,0:T(8,128)S(1)} %collective-permute-done.4.refs_2_), channel_id=1, source_target_pairs={{0,1},{1,0},{2,3},{3,2},{4,5},{5,4},{6,7},{7,6},{8,9},{9,8},{10,11... | collective-permute-start | bytes 786440 | tf_op jit(solution)/shard_map/ppermute | solution.py:167
  33.3 1.4 %copy-start = (f32[512,1,128]{2,1,0:T(1,128)S(1)}, f32[512,1,128]{2,1,0:T(1,128)}, u32[]{:S(2)}) copy-start(f32[512,1,128]{2,1,0:T(1,128)} %param.3) | copy-start | bytes 786436

commit v5 on v4

--- a/solution.py
+++ b/solution.py
@@ -8,16 +8,13 @@
 from jax.sharding import PartitionSpec as P
 
 PAIR = 2
+QUARTET = 4
 LEAD = 4.0
 
 
 def halves(value):
     high = value.astype(jnp.bfloat16)
     return high, (value - high.astype(jnp.float32)).astype(jnp.bfloat16)
-
-
-def whole(parts):
-    return parts[0].astype(jnp.float32) + parts[1].astype(jnp.float32)
 
 
 def dot(left, right, side):
@@ -39,29 +36,11 @@
     return both[: left.shape[0]] + both[left.shape[0] :] + dot(left_high, right_low, side)
 
 
-def add_diagonal(matrix, block):
-    width = block.shape[0]
-    count = matrix.shape[0] // width
-    return jnp.concatenate(
-        [
-            jnp.concatenate(
-                [
-                    matrix[i * width : (i + 1) * width, j * width : (j + 1) * width] + (block if i == j else 0.0)
-                    for j in range(count)
-                ],
-                axis=1,
-            )
-            for i in range(count)
-        ],
-        axis=0,
-    )
-
-
 def step_kernel(groups, *refs):
     count = groups * PAIR
     shares = refs[: PAIR * count]
     upper_ref, lower_ref, new_upper_ref, new_lower_ref = refs[PAIR * count : PAIR * count + 4]
-    rest_high, rest_low, low_high, low_low, made_upper, made_lower, sent = refs[PAIR * count + 4 :]
+    rest_high, rest_low, made_upper, made_lower, sent = refs[PAIR * count + 4 :]
     order, width = upper_ref.shape
     block, here = lax.axis_index("blk"), lax.axis_index("col")
     on_upper = lax.rem(block, PAIR) == 0
@@ -82,15 +61,20 @@
             total = total + jnp.sum((head * head).reshape(-1, 8, width), axis=0)
             to = slice(j * width, (j + 1) * width)
             rest_high[to, columns], rest_low[to, columns] = halves(head - LEAD * unit if i == j else head)
-        low_high[:, columns], low_low[:, columns] = halves(jnp.where(on_upper, shares[count + i][...], shares[i][...]))
     scale = lax.rsqrt(jnp.full((1, 1), jnp.sum(total)) / order + 1e-06)
     shift = 1.0 - LEAD * scale
     rest = (rest_high[...], rest_low[...])
-    low = (low_high[...], low_low[...])
-    square = (scale * scale) * product(rest, rest) - (2.0 * shift * scale) * whole(rest)
-    square = halves(add_diagonal(square, shift * shift * unit))
-    middle = (1.0 + shift) * whole(low) - scale * product(low, rest)
-    reflect = halves((middle + product(halves(middle), square)) * scale)
+    strips = []
+    for first in range(0, order, order // 2):
+        strip = slice(first, first + order // 2)
+        parts = [jnp.where(on_upper, shares[count + i][strip, :], shares[i][strip, :]) for i in range(count)]
+        strips.append(jnp.concatenate(parts, axis=1))
+    powers, sums = strips, strips
+    for _ in range(3):
+        powers = [shift * power - scale * thin_product(power, rest) for power in powers]
+        sums = [total + power for total, power in zip(sums, powers)]
+    reflects = [halves(total * scale) for total in sums]
+    reflect = tuple(jnp.concatenate(parts, axis=0) for parts in zip(*reflects))
     upper = jnp.concatenate([upper_ref[part, :].T for part in rows], axis=1)
     lower = lower_ref[...].T
     gram = halves(product(reflect, reflect, 1))
@@ -121,30 +105,46 @@
         out_shape=(jax.ShapeDtypeStruct(upper.shape, jnp.float32),) * 2,
         in_specs=[in_vmem] * (len(shares) + 2),
         out_specs=(pl.BlockSpec(memory_space=pl.ANY),) * 2,
-        scratch_shapes=[pltpu.VMEM((order, order), jnp.bfloat16)] * 4
+        scratch_shapes=[pltpu.VMEM((order, order), jnp.bfloat16)] * 2
         + [pltpu.VMEM((order, width), jnp.float32)] * 2
         + [pltpu.SemaphoreType.DMA((2,))],
         compiler_params=pltpu.CompilerParams(vmem_limit_bytes=48 * 1024 * 1024),
     )(*shares, upper, lower)
 
 
-def spread(upper, lower, rows, row, flip):
-    stride = 1
+def spread(share, moved, rows, row):
+    def send(value, moves):
+        pairs = []
+        for first in range(0, rows, QUARTET):
+            pairs += [(PAIR * (first + a) + x, PAIR * (first + b) + x) for a, b in moves for x in range(PAIR)]
+        return lax.ppermute(value, "blk", pairs)
+
+    assert rows % QUARTET == 0
+    stride = QUARTET
     while stride < rows:
         stride *= 2
-    share = lax.optimization_barrier(jnp.where(flip == 0, upper, lower))
-    while stride > 1:
+    while stride > QUARTET:
         stride //= 2
-        pairs = [(first, first + stride) for first in range(0, rows - stride, 2 * stride)]
-        sends = [[(PAIR * a + x, PAIR * b + x) for a, b in pairs] for x in range(PAIR)]
-        if 2 * stride >= rows:
-            received = jnp.where(
-                flip == 0, lax.ppermute(upper, "blk", sends[0]), lax.ppermute(lower, "blk", sends[1])
-            )
-        else:
-            received = lax.ppermute(share, "blk", sends[0] + sends[1])
+        heads = range(0, rows - stride, 2 * stride)
+        pairs = [(PAIR * a + x, PAIR * (a + stride) + x) for a in heads for x in range(PAIR)]
+        received = lax.ppermute(share, "blk", pairs)
         share = jnp.where(lax.rem(row, 2 * stride) == stride, received, share)
-    return share
+    place = lax.rem(row, QUARTET)
+    cut = share.shape[0] // 2 - 8
+    top, bottom = share[:cut], share[cut:]
+    top_one = send(top, [(0, 1)])
+    bottom_two = send(bottom, [(0, 2)])
+    bottom_one = send(bottom, [(0, 1)])
+    top_one, bottom_two = lax.optimization_barrier((top_one, bottom_two))
+    top_three = send(top_one, [(1, 3)])
+    top_two = send(top_one, [(1, 2)])
+    bottom_three = send(bottom_two, [(2, 3)])
+    bottom_one, moved = lax.optimization_barrier((bottom_one, moved))
+    top = jnp.where(place == 0, top, jnp.where(place == 1, top_one, jnp.where(place == 2, top_two, top_three)))
+    bottom = jnp.where(
+        place == 0, bottom, jnp.where(place == 1, bottom_one, jnp.where(place == 2, bottom_two, bottom_three))
+    )
+    return jnp.concatenate([top, bottom], axis=0), moved
 
 
 def exchange(share, rows, groups):
@@ -176,9 +176,11 @@
     upper, lower = upper_row[:, 0, :], lower_row[:, 0, :]
     side = lax.rem(block, PAIR)
     swapped = lax.ppermute(upper, "blk", [(source, source ^ 1) for source in range(blocks)])
-    ahead = [(source, source + PAIR) for source in range(0, blocks - PAIR, PAIR)]
-    shifted = jnp.where(side == 1, swapped, lax.ppermute(swapped, "blk", ahead))
-    share = spread(upper, lower, rows, block // PAIR, side)
+    share = jnp.where(side == 0, upper, lower)
+    share, swapped = spread(share, swapped, rows, block // PAIR)
+    forward = [(source, (source + PAIR) % blocks) for source in range(blocks)]
+    onward = lax.ppermute(swapped, "blk", forward)
+    shifted = jnp.where(side == 1, swapped, jnp.where(block == 0, 0.0, onward))
     shares = exchange(share, rows, groups)
     new_upper, new_lower = step_call(shares, shifted, lower, groups)
     return new_upper[:, None, :], new_lower[:, None, :]

time: 42 us -> 41.1 us (0.979)
  the two profiles are of different devices: /device:TPU:0 before, /device:TPU:19 now
where the time goes in v5:
time: 41.1 us; the launch traced here: 40.9 us
  starting transfers between devices  21.8 us (53%)
  waiting for transfers between devices  10.4 us (25%)
  Pallas kernels  6.71 us (16%)
  other arithmetic  1.13 us (3%)
  between operations  0.83 us (2%)
    ppermute x4, starting transfers between devices, exchange(): shares += [mine, lax.ppermute(mine, 'col', swap)]  12.3 us
    ppermute x6, waiting for transfers between devices, send(): return lax.ppermute(value, 'blk', pairs)  8.91 us
    pallas_call x1, Pallas kernels, step_call(): pl.pallas_call(functools.partial(step_kernel, groups), out_shape=(jax.Sha...  6.71 us
    ppermute x6, starting transfers between devices, send(): return lax.ppermute(value, 'blk', pairs)  6.01 us
    ppermute x3, starting transfers between devices, exchange(): mine = lax.ppermute(share, ('blk', 'col'), sends) if flip or step else share  2.71 us
    ppermute x4, waiting for transfers between devices, exchange(): shares += [mine, lax.ppermute(mine, 'col', swap)]  1.46 us
    select_n x1, other arithmetic, shards(): share = jnp.where(side == 0, upper, lower)  0.99 us
  transfers between devices with their start and end apart: 15, of which 4 were waited for; matrix products, arithmetic and copies ran while one was open for 0% of the time, Pallas kernels for 0%

profile of v5, /device:TPU:19, one launch (start us, length us, event | category | flops | bytes accessed | tf_op | source)
XLA Modules:
  0.0 40.9 jit_solution(17837725370096824687)
XLA Ops:
  0.6 1.0 %broadcast_select_fusion = f32[512,128]{1,0:T(8,128)S(1)} fusion(f32[512,128]{1,0:T(8,128)} %bitcast.10, f32[512,128]{1,0:T(8,128)} %bitcast.8, pred[]{:T(512)S(6)} %eq.22), kind=kLoop, calls=%fused_computation.3 | loop fusion | flops 65536 | bytes 786433 | tf_op jit(solution)/shard_map/jit(_where)/select_n | solution.py:179
  1.6 0.0 copy-start.1
  1.7 1.4 %collective-permute-start.1 = (f32[264,128]{1,0:T(8,128)S(1)}, f32[264,128]{1,0:T(8,128)S(1)}, u32[]{:S(2)}, u32[]{:S(2)}) collective-permute-start(f32[264,128]{1,0:T(8,128)S(1)} %slice.9), channel_id=1, source_target_pairs={{0,16},{4,20},{1,17},{5,21},{2,18},{6,22},{3,19},{7,23}} | collective-permute-start | bytes 405512 | tf_op jit(solution)/shard_map/ppermute | solution.py:120
  3.1 0.3 collective-permute-start.5
  3.4 0.7 %collective-permute-start = (f32[248,128]{1,0:T(8,128)S(1)}, f32[248,128]{1,0:T(8,128)S(1)}, u32[]{:S(2)}, u32[]{:S(2)}) collective-permute-start(f32[248,128]{1,0:T(8,128)S(1)} %slice.8), channel_id=1, source_target_pairs={{0,8},{4,12},{1,9},{5,13},{2,10},{6,14},{3,11},{7,15}} | collective-permute-start | bytes 380936 | tf_op jit(solution)/shard_map/ppermute | solution.py:120
  4.1 0.7 %collective-permute-start.4 = (f32[264,128]{1,0:T(8,128)S(1)}, f32[264,128]{1,0:T(8,128)S(1)}, u32[]{:S(2)}, u32[]{:S(2)}) collective-permute-start(f32[264,128]{1,0:T(8,128)S(1)} %slice.9), channel_id=1, source_target_pairs={{0,8},{4,12},{1,9},{5,13},{2,10},{6,14},{3,11},{7,15}} | collective-permute-start | bytes 405512 | tf_op jit(solution)/shard_map/ppermute | solution.py:120
  4.8 0.0 collective-permute-done
  4.8 4.2 %collective-permute-done.1 = f32[264,128]{1,0:T(8,128)S(1)} collective-permute-done((f32[264,128]{1,0:T(8,128)S(1)}, f32[264,128]{1,0:T(8,128)S(1)}, u32[]{:S(2)}, u32[]{:S(2)}) %collective-permute-start.1) | collective-permute-done | bytes 135200 | tf_op jit(solution)/shard_map/ppermute | solution.py:120
  9.0 0.7 %collective-permute-start.3 = (f32[248,128]{1,0:T(8,128)S(1)}, f32[248,128]{1,0:T(8,128)S(1)}, u32[]{:S(2)}, u32[]{:S(2)}) collective-permute-start(f32[248,128]{1,0:T(8,128)S(1)} %collective-permute-done), channel_id=1, source_target_pairs={{8,24},{12,28},{9,25},{13,29},{10,26},{14,30},{11,27},{15,31}} | collective-permute-start | bytes 380936 | tf_op jit(solution)/shard_map/ppermute | solution.py:120
  9.7 1.3 %collective-permute-start.2 = (f32[248,128]{1,0:T(8,128)S(1)}, f32[248,128]{1,0:T(8,128)S(1)}, u32[]{:S(2)}, u32[]{:S(2)}) collective-permute-start(f32[248,128]{1,0:T(8,128)S(1)} %collective-permute-done), channel_id=1, source_target_pairs={{8,16},{12,20},{9,17},{13,21},{10,18},{14,22},{11,19},{15,23}} | collective-permute-start | bytes 380936 | tf_op jit(solution)/shard_map/ppermute | solution.py:120
  11.0 1.3 %collective-permute-start.6 = (f32[264,128]{1,0:T(8,128)S(1)}, f32[264,128]{1,0:T(8,128)S(1)}, u32[]{:S(2)}, u32[]{:S(2)}) collective-permute-start(f32[264,128]{1,0:T(8,128)S(1)} %collective-permute-done.1), channel_id=1, source_target_pairs={{16,24},{20,28},{17,25},{21,29},{18,26},{22,30},{19,27},{23,31}} | collective-permute-start | bytes 405512 | tf_op jit(solution)/shard_map/ppermute | solution.py:120
  12.3 0.0 collective-permute-done.4
  12.4 0.0 collective-permute-done.5
  12.4 0.0 collective-permute-done.3
  12.4 4.7 %collective-permute-done.2 = f32[248,128]{1,0:T(8,128)S(1)} collective-permute-done((f32[248,128]{1,0:T(8,128)S(1)}, f32[248,128]{1,0:T(8,128)S(1)}, u32[]{:S(2)}, u32[]{:S(2)}) %collective-permute-start.2) | collective-permute-done | bytes 127008 | tf_op jit(solution)/shard_map/ppermute | solution.py:120
  17.1 0.0 collective-permute-done.6
  17.2 1.2 %collective-permute-start.12 = (f32[512,128]{1,0:T(8,128)S(1)}, f32[512,128]{1,0:T(8,128)S(1)}, u32[]{:S(2)}, u32[]{:S(2)}) collective-permute-start(f32[512,128]{1,0:T(8,128)S(1)} %pad_maximum_fusion.refs_0_), channel_id=1, source_target_pairs={{6,0},{7,1},{4,2},{5,3},{2,4},{3,5},{0,6},{1,7},{14,8},{15,9},{12,... | collective-permute-start | bytes 786440 | tf_op jit(solution)/shard_map/ppermute | solution.py:165
  18.4 1.2 %collective-permute-start.10 = (f32[512,128]{1,0:T(8,128)S(1)}, f32[512,128]{1,0:T(8,128)S(1)}, u32[]{:S(2)}, u32[]{:S(2)}) collective-permute-start(f32[512,128]{1,0:T(8,128)S(1)} %pad_maximum_fusion.refs_0_), channel_id=1, source_target_pairs={{4,0},{5,1},{6,2},{7,3},{0,4},{1,5},{2,6},{3,7},{12,8},{13,9},{14,... | collective-permute-start | bytes 786440 | tf_op jit(solution)/shard_map/ppermute | solution.py:165
  19.6 0.2 collective-permute-start.8
  19.9 0.4 %collective-permute-start.14 = (f32[512,128]{1,0:T(8,128)S(1)}, f32[512,128]{1,0:T(8,128)S(1)}, u32[]{:S(2)}, u32[]{:S(2)}) collective-permute-start(f32[512,128]{1,0:T(8,128)S(1)} %collective-permute-done.5), channel_id=1, source_target_pairs={{0,8},{4,12},{8,16},{12,20},{16,24},{20,28},{24,0},{28,4},{1,9},{5... | collective-permute-start | bytes 786440 | tf_op jit(solution)/shard_map/ppermute | solution.py:182
  20.3 4.7 %collective-permute-start.7 = (f32[512,128]{1,0:T(8,128)S(1)}, f32[512,128]{1,0:T(8,128)S(1)}, u32[]{:S(2)}, u32[]{:S(2)}) collective-permute-start(f32[512,128]{1,0:T(8,128)S(1)} %pad_maximum_fusion.refs_0_), channel_id=1, source_target_pairs={{0,1},{1,0},{2,3},{3,2},{4,5},{5,4},{6,7},{7,6},{8,9},{9,8},{10,11... | collective-permute-start | bytes 786440 | tf_op jit(solution)/shard_map/ppermute | solution.py:167
  25.0 0.0 collective-permute-done.12.refs_6_
  25.0 4.8 %collective-permute-start.13 = (f32[512,128]{1,0:T(8,128)S(1)}, f32[512,128]{1,0:T(8,128)S(1)}, u32[]{:S(2)}, u32[]{:S(2)}) collective-permute-start(f32[512,128]{1,0:T(8,128)S(1)} %collective-permute-done.12.refs_6_), channel_id=1, source_target_pairs={{0,1},{1,0},{2,3},{3,2},{4,5},{5,4},{6,7},{7,6},{8,9},{9,8},{10,11... | collective-permute-start | bytes 786440 | tf_op jit(solution)/shard_map/ppermute | solution.py:167
  29.8 0.0 collective-permute-done.10.refs_4_
  29.8 2.8 %collective-permute-start.11 = (f32[512,128]{1,0:T(8,128)S(1)}, f32[512,128]{1,0:T(8,128)S(1)}, u32[]{:S(2)}, u32[]{:S(2)}) collective-permute-start(f32[512,128]{1,0:T(8,128)S(1)} %collective-permute-done.10.refs_4_), channel_id=1, source_target_pairs={{0,1},{1,0},{2,3},{3,2},{4,5},{5,4},{6,7},{7,6},{8,9},{9,8},{10,11... | collective-permute-start | bytes 786440 | tf_op jit(solution)/shard_map/ppermute | solution.py:167
  32.6 0.0 collective-permute-done.8.refs_2_
  32.6 0.0 collective-permute-start.9
  32.6 0.0 collective-permute-done.14
  32.7 0.0 collective-permute-done.7.refs_1_
  32.7 1.1 %collective-permute-done.11.refs_5_ = f32[512,128]{1,0:T(8,128)S(1)} collective-permute-done((f32[512,128]{1,0:T(8,128)S(1)}, f32[512,128]{1,0:T(8,128)S(1)}, u32[]{:S(2)}, u32[]{:S(2)}) %collective-permute-start.11) | collective-permute-done | bytes 262176 | tf_op jit(solution)/shard_map/ppermute | solution.py:167
  33.8 0.4 collective-permute-done.9.refs_3_
  34.1 6.7 %shard_map.41 = (f32[512,128]{1,0:T(8,128)}, f32[512,128]{1,0:T(8,128)}) custom-call(f32[512,128]{1,0:T(8,128)S(1)} %pad_maximum_fusion.refs_0_, f32[512,128]{1,0:T(8,128)S(1)} %collective-permute-done.7.refs_1_, f32[512,128]{1,0:T(8,128)S(1)} %collective-permute-done.8.refs_2_, f32[512,128]{1,0:T(8,128)S(1)} %collective-permute-done.9.refs_3_, ...), custom_call_target="tpu_custom_call" | custom-call | tf_op jit(solution)/shard_map/pallas_call | solution.py:103
  (10 shorter events, 0.2 us)
Async XLA Ops:
  1.6 1.5 %copy-start.1 = (f32[512,1,128]{2,1,0:T(1,128)S(1)}, f32[512,1,128]{2,1,0:T(1,128)}, u32[]{:S(2)}) copy-start(f32[512,1,128]{2,1,0:T(1,128)} %param.2) | copy-start | bytes 786436
  1.7 7.4 %collective-permute-start.1 = (f32[264,128]{1,0:T(8,128)S(1)}, f32[264,128]{1,0:T(8,128)S(1)}, u32[]{:S(2)}, u32[]{:S(2)}) collective-permute-start(f32[264,128]{1,0:T(8,128)S(1)} %slice.9), channel_id=1, source_target_pairs={{0,16},{4,20},{1,17},{5,21},{2,18},{6,22},{3,19},{7,23}} | collective-permute-start | bytes 405512 | tf_op jit(solution)/shard_map/ppermute | solution.py:120
  3.1 9.2 %collective-permute-start.5 = (f32[512,128]{1,0:T(8,128)S(1)}, f32[512,128]{1,0:T(8,128)S(1)}, u32[]{:S(2)}, u32[]{:S(2)}) collective-permute-start(f32[512,128]{1,0:T(8,128)S(1)} %bitcast.11), channel_id=1, source_target_pairs={{0,4},{4,0},{8,12},{12,8},{16,20},{20,16},{24,28},{28,24},{1,5},{5... | collective-permute-start | bytes 786440 | tf_op jit(solution)/shard_map/ppermute | solution.py:178
  3.4 1.4 %collective-permute-start = (f32[248,128]{1,0:T(8,128)S(1)}, f32[248,128]{1,0:T(8,128)S(1)}, u32[]{:S(2)}, u32[]{:S(2)}) collective-permute-start(f32[248,128]{1,0:T(8,128)S(1)} %slice.8), channel_id=1, source_target_pairs={{0,8},{4,12},{1,9},{5,13},{2,10},{6,14},{3,11},{7,15}} | collective-permute-start | bytes 380936 | tf_op jit(solution)/shard_map/ppermute | solution.py:120
  4.1 8.2 %collective-permute-start.4 = (f32[264,128]{1,0:T(8,128)S(1)}, f32[264,128]{1,0:T(8,128)S(1)}, u32[]{:S(2)}, u32[]{:S(2)}) collective-permute-start(f32[264,128]{1,0:T(8,128)S(1)} %slice.9), channel_id=1, source_target_pairs={{0,8},{4,12},{1,9},{5,13},{2,10},{6,14},{3,11},{7,15}} | collective-permute-start | bytes 405512 | tf_op jit(solution)/shard_map/ppermute | solution.py:120
  9.0 3.3 %collective-permute-start.3 = (f32[248,128]{1,0:T(8,128)S(1)}, f32[248,128]{1,0:T(8,128)S(1)}, u32[]{:S(2)}, u32[]{:S(2)}) collective-permute-start(f32[248,128]{1,0:T(8,128)S(1)} %collective-permute-done), channel_id=1, source_target_pairs={{8,24},{12,28},{9,25},{13,29},{10,26},{14,30},{11,27},{15,31}} | collective-permute-start | bytes 380936 | tf_op jit(solution)/shard_map/ppermute | solution.py:120
  9.7 7.3 %collective-permute-start.2 = (f32[248,128]{1,0:T(8,128)S(1)}, f32[248,128]{1,0:T(8,128)S(1)}, u32[]{:S(2)}, u32[]{:S(2)}) collective-permute-start(f32[248,128]{1,0:T(8,128)S(1)} %collective-permute-done), channel_id=1, source_target_pairs={{8,16},{12,20},{9,17},{13,21},{10,18},{14,22},{11,19},{15,23}} | collective-permute-start | bytes 380936 | tf_op jit(solution)/shard_map/ppermute | solution.py:120
  11.0 6.0 %collective-permute-start.6 = (f32[264,128]{1,0:T(8,128)S(1)}, f32[264,128]{1,0:T(8,128)S(1)}, u32[]{:S(2)}, u32[]{:S(2)}) collective-permute-start(f32[264,128]{1,0:T(8,128)S(1)} %collective-permute-done.1), channel_id=1, source_target_pairs={{16,24},{20,28},{17,25},{21,29},{18,26},{22,30},{19,27},{23,31}} | collective-permute-start | bytes 405512 | tf_op jit(solution)/shard_map/ppermute | solution.py:120
  17.2 7.8 %collective-permute-start.12 = (f32[512,128]{1,0:T(8,128)S(1)}, f32[512,128]{1,0:T(8,128)S(1)}, u32[]{:S(2)}, u32[]{:S(2)}) collective-permute-start(f32[512,128]{1,0:T(8,128)S(1)} %pad_maximum_fusion.refs_0_), channel_id=1, source_target_pairs={{6,0},{7,1},{4,2},{5,3},{2,4},{3,5},{0,6},{1,7},{14,8},{15,9},{12,... | collective-permute-start | bytes 786440 | tf_op jit(solution)/shard_map/ppermute | solution.py:165
  18.4 11.4 %collective-permute-start.10 = (f32[512,128]{1,0:T(8,128)S(1)}, f32[512,128]{1,0:T(8,128)S(1)}, u32[]{:S(2)}, u32[]{:S(2)}) collective-permute-start(f32[512,128]{1,0:T(8,128)S(1)} %pad_maximum_fusion.refs_0_), channel_id=1, source_target_pairs={{4,0},{5,1},{6,2},{7,3},{0,4},{1,5},{2,6},{3,7},{12,8},{13,9},{14,... | collective-permute-start | bytes 786440 | tf_op jit(solution)/shard_map/ppermute | solution.py:165
  19.6 13.0 %collective-permute-start.8 = (f32[512,128]{1,0:T(8,128)S(1)}, f32[512,128]{1,0:T(8,128)S(1)}, u32[]{:S(2)}, u32[]{:S(2)}) collective-permute-start(f32[512,128]{1,0:T(8,128)S(1)} %pad_maximum_fusion.refs_0_), channel_id=1, source_target_pairs={{2,0},{3,1},{0,2},{1,3},{6,4},{7,5},{4,6},{5,7},{10,8},{11,9},{8,1... | collective-permute-start | bytes 786440 | tf_op jit(solution)/shard_map/ppermute | solution.py:165
  19.9 12.7 %collective-permute-start.14 = (f32[512,128]{1,0:T(8,128)S(1)}, f32[512,128]{1,0:T(8,128)S(1)}, u32[]{:S(2)}, u32[]{:S(2)}) collective-permute-start(f32[512,128]{1,0:T(8,128)S(1)} %collective-permute-done.5), channel_id=1, source_target_pairs={{0,8},{4,12},{8,16},{12,20},{16,24},{20,28},{24,0},{28,4},{1,9},{5... | collective-permute-start | bytes 786440 | tf_op jit(solution)/shard_map/ppermute | solution.py:182
  20.3 12.3 %collective-permute-start.7 = (f32[512,128]{1,0:T(8,128)S(1)}, f32[512,128]{1,0:T(8,128)S(1)}, u32[]{:S(2)}, u32[]{:S(2)}) collective-permute-start(f32[512,128]{1,0:T(8,128)S(1)} %pad_maximum_fusion.refs_0_), channel_id=1, source_target_pairs={{0,1},{1,0},{2,3},{3,2},{4,5},{5,4},{6,7},{7,6},{8,9},{9,8},{10,11... | collective-permute-start | bytes 786440 | tf_op jit(solution)/shard_map/ppermute | solution.py:167
  25.0 7.7 %collective-permute-start.13 = (f32[512,128]{1,0:T(8,128)S(1)}, f32[512,128]{1,0:T(8,128)S(1)}, u32[]{:S(2)}, u32[]{:S(2)}) collective-permute-start(f32[512,128]{1,0:T(8,128)S(1)} %collective-permute-done.12.refs_6_), channel_id=1, source_target_pairs={{0,1},{1,0},{2,3},{3,2},{4,5},{5,4},{6,7},{7,6},{8,9},{9,8},{10,11... | collective-permute-start | bytes 786440 | tf_op jit(solution)/shard_map/ppermute | solution.py:167
  29.8 4.0 %collective-permute-start.11 = (f32[512,128]{1,0:T(8,128)S(1)}, f32[512,128]{1,0:T(8,128)S(1)}, u32[]{:S(2)}, u32[]{:S(2)}) collective-permute-start(f32[512,128]{1,0:T(8,128)S(1)} %collective-permute-done.10.refs_4_), channel_id=1, source_target_pairs={{0,1},{1,0},{2,3},{3,2},{4,5},{5,4},{6,7},{7,6},{8,9},{9,8},{10,11... | collective-permute-start | bytes 786440 | tf_op jit(solution)/shard_map/ppermute | solution.py:167
  32.6 1.5 %collective-permute-start.9 = (f32[512,128]{1,0:T(8,128)S(1)}, f32[512,128]{1,0:T(8,128)S(1)}, u32[]{:S(2)}, u32[]{:S(2)}) collective-permute-start(f32[512,128]{1,0:T(8,128)S(1)} %collective-permute-done.8.refs_2_), channel_id=1, source_target_pairs={{0,1},{1,0},{2,3},{3,2},{4,5},{5,4},{6,7},{7,6},{8,9},{9,8},{10,11... | collective-permute-start | bytes 786440 | tf_op jit(solution)/shard_map/ppermute | solution.py:167
  32.6 1.5 %copy-start = (f32[512,1,128]{2,1,0:T(1,128)S(1)}, f32[512,1,128]{2,1,0:T(1,128)}, u32[]{:S(2)}) copy-start(f32[512,1,128]{2,1,0:T(1,128)} %param.3) | copy-start | bytes 786436

commit v6 on v5

--- a/solution.py
+++ b/solution.py
@@ -130,20 +130,15 @@
         received = lax.ppermute(share, "blk", pairs)
         share = jnp.where(lax.rem(row, 2 * stride) == stride, received, share)
     place = lax.rem(row, QUARTET)
-    cut = share.shape[0] // 2 - 8
-    top, bottom = share[:cut], share[cut:]
-    top_one = send(top, [(0, 1)])
+    top, bottom = jnp.split(share, 2, axis=0)
+    top_one = send(top, [(0, 1), (1, 0), (2, 3), (3, 2)])
     bottom_two = send(bottom, [(0, 2)])
-    bottom_one = send(bottom, [(0, 1)])
-    top_one, bottom_two = lax.optimization_barrier((top_one, bottom_two))
+    holds = jnp.where(place == 1, top_one, jnp.where(place == 2, bottom_two, bottom))
     top_three = send(top_one, [(1, 3)])
-    top_two = send(top_one, [(1, 2)])
-    bottom_three = send(bottom_two, [(2, 3)])
-    bottom_one, moved = lax.optimization_barrier((bottom_one, moved))
-    top = jnp.where(place == 0, top, jnp.where(place == 1, top_one, jnp.where(place == 2, top_two, top_three)))
-    bottom = jnp.where(
-        place == 0, bottom, jnp.where(place == 1, bottom_one, jnp.where(place == 2, bottom_two, bottom_three))
-    )
+    passed = send(holds, [(0, 1), (1, 2), (2, 3), (3, 0)])
+    top_three, moved = lax.optimization_barrier((top_three, moved))
+    top = jnp.where(place == 0, top, jnp.where(place == 1, top_one, jnp.where(place == 2, passed, top_three)))
+    bottom = jnp.where(place == 0, bottom, jnp.where(place == 2, bottom_two, passed))
     return jnp.concatenate([top, bottom], axis=0), moved
 
 

time: 41.1 us -> 39.9 us (0.971)
  the two profiles are of different devices: /device:TPU:19 before, /device:TPU:0 now
where the time goes in v6:
time: 39.9 us; the launch traced here: 39.7 us
  starting transfers between devices  17.5 us (44%)
  waiting for transfers between devices  13.6 us (34%)
  Pallas kernels  6.71 us (17%)
  other arithmetic  1.1 us (3%)
  between operations  0.73 us (2%)
    ppermute x4, starting transfers between devices, send(): return lax.ppermute(value, 'blk', pairs)  11 us
    ppermute x3, waiting for transfers between devices, exchange(): mine = lax.ppermute(share, ('blk', 'col'), sends) if flip or step else share  7.97 us
    pallas_call x1, Pallas kernels, step_call(): pl.pallas_call(functools.partial(step_kernel, groups), out_shape=(jax.Sha...  6.71 us
    ppermute x3, starting transfers between devices, exchange(): mine = lax.ppermute(share, ('blk', 'col'), sends) if flip or step else share  3.55 us
    ppermute x1, waiting for transfers between devices, shards(): lax.ppermute(upper, 'blk', [(source, source ^ 1) for source in range(bloc...  2.23 us
    ppermute x4, waiting for transfers between devices, send(): return lax.ppermute(value, 'blk', pairs)  2.04 us
    ppermute x1, starting transfers between devices, shards(): lax.ppermute(upper, 'blk', [(source, source ^ 1) for source in range(bloc...  1.56 us
    ppermute x4, waiting for transfers between devices, exchange(): shares += [mine, lax.ppermute(mine, 'col', swap)]  1.34 us
  transfers between devices with their start and end apart: 13, of which 8 were waited for; matrix products, arithmetic and copies ran while one was open for 0% of the time, Pallas kernels for 0%

profile of v6, /device:TPU:0, one launch (start us, length us, event | category | flops | bytes accessed | tf_op | source)
XLA Modules:
  0.0 39.7 jit_solution(1743659209166589472)
XLA Ops:
  0.6 1.0 %broadcast_select_fusion = f32[512,128]{1,0:T(8,128)S(1)} fusion(f32[512,128]{1,0:T(8,128)} %bitcast.10, f32[512,128]{1,0:T(8,128)} %bitcast.8, pred[]{:T(512)S(6)} %eq.23), kind=kLoop, calls=%fused_computation.5 | loop fusion | flops 65536 | bytes 786433 | tf_op jit(solution)/shard_map/jit(_where)/select_n | solution.py:174
  1.6 0.0 copy-start.1
  1.7 3.1 %collective-permute-start = (f32[256,128]{1,0:T(8,128)S(1)}, f32[256,128]{1,0:T(8,128)S(1)}, u32[]{:S(2)}, u32[]{:S(2)}) collective-permute-start(f32[256,128]{1,0:T(8,128)S(1)} %get-tuple-element.14), channel_id=1, source_target_pairs={{0,8},{4,12},{8,0},{12,4},{16,24},{20,28},{24,16},{28,20},{1,9},{5... | collective-permute-start | bytes 393224 | tf_op jit(solution)/shard_map/ppermute | solution.py:120
  4.8 4.5 %collective-permute-start.1 = (f32[256,128]{1,0:T(8,128)S(1)}, f32[256,128]{1,0:T(8,128)S(1)}, u32[]{:S(2)}, u32[]{:S(2)}) collective-permute-start(f32[256,128]{1,0:T(8,128)S(1)} %get-tuple-element.15), channel_id=1, source_target_pairs={{0,16},{4,20},{1,17},{5,21},{2,18},{6,22},{3,19},{7,23}} | collective-permute-start | bytes 393224 | tf_op jit(solution)/shard_map/ppermute | solution.py:120
  9.3 0.0 copy-done.1
  9.3 1.6 %collective-permute-start.4 = (f32[512,128]{1,0:T(8,128)S(1)}, f32[512,128]{1,0:T(8,128)S(1)}, u32[]{:S(2)}, u32[]{:S(2)}) collective-permute-start(f32[512,128]{1,0:T(8,128)S(1)} %bitcast.11), channel_id=1, source_target_pairs={{0,4},{4,0},{8,12},{12,8},{16,20},{20,16},{24,28},{28,24},{1,5},{5... | collective-permute-start | bytes 786440 | tf_op jit(solution)/shard_map/ppermute | solution.py:173
  10.8 0.0 collective-permute-done
  10.8 0.7 %collective-permute-start.3 = (f32[256,128]{1,0:T(8,128)S(1)}, f32[256,128]{1,0:T(8,128)S(1)}, u32[]{:S(2)}, u32[]{:S(2)}) collective-permute-start(f32[256,128]{1,0:T(8,128)S(1)} %collective-permute-done), channel_id=1, source_target_pairs={{8,24},{12,28},{9,25},{13,29},{10,26},{14,30},{11,27},{15,31}} | collective-permute-start | bytes 393224 | tf_op jit(solution)/shard_map/ppermute | solution.py:120
  11.5 0.3 collective-permute-done.1
  11.8 2.8 %collective-permute-start.2 = (f32[256,128]{1,0:T(8,128)S(1)}, f32[256,128]{1,0:T(8,128)S(1)}, u32[]{:S(2)}, u32[]{:S(2)}) collective-permute-start(f32[256,128]{1,0:T(8,128)S(1)} %select_select_fusion.3), channel_id=1, source_target_pairs={{0,8},{4,12},{8,16},{12,20},{16,24},{20,28},{24,0},{28,4},{1,9},{5... | collective-permute-start | bytes 393224 | tf_op jit(solution)/shard_map/ppermute | solution.py:120
  14.6 0.0 collective-permute-done.3
  14.6 2.2 %collective-permute-done.4 = f32[512,128]{1,0:T(8,128)S(1)} collective-permute-done((f32[512,128]{1,0:T(8,128)S(1)}, f32[512,128]{1,0:T(8,128)S(1)}, u32[]{:S(2)}, u32[]{:S(2)}) %collective-permute-start.4) | collective-permute-done | bytes 262176 | tf_op jit(solution)/shard_map/ppermute | solution.py:173
  16.8 1.8 %collective-permute-done.2 = f32[256,128]{1,0:T(8,128)S(1)} collective-permute-done((f32[256,128]{1,0:T(8,128)S(1)}, f32[256,128]{1,0:T(8,128)S(1)}, u32[]{:S(2)}, u32[]{:S(2)}) %collective-permute-start.2) | collective-permute-done | bytes 131104 | tf_op jit(solution)/shard_map/ppermute | solution.py:120
  18.7 2.5 %collective-permute-start.10 = (f32[512,128]{1,0:T(8,128)S(1)}, f32[512,128]{1,0:T(8,128)S(1)}, u32[]{:S(2)}, u32[]{:S(2)}) collective-permute-start(f32[512,128]{1,0:T(8,128)S(1)} %pad_maximum_fusion.refs_0_), channel_id=1, source_target_pairs={{6,0},{7,1},{4,2},{5,3},{2,4},{3,5},{0,6},{1,7},{14,8},{15,9},{12,... | collective-permute-start | bytes 786440 | tf_op jit(solution)/shard_map/ppermute | solution.py:160
  21.2 0.5 %collective-permute-start.6 = (f32[512,128]{1,0:T(8,128)S(1)}, f32[512,128]{1,0:T(8,128)S(1)}, u32[]{:S(2)}, u32[]{:S(2)}) collective-permute-start(f32[512,128]{1,0:T(8,128)S(1)} %pad_maximum_fusion.refs_0_), channel_id=1, source_target_pairs={{2,0},{3,1},{0,2},{1,3},{6,4},{7,5},{4,6},{5,7},{10,8},{11,9},{8,1... | collective-permute-start | bytes 786440 | tf_op jit(solution)/shard_map/ppermute | solution.py:160
  21.7 0.5 %collective-permute-start.8 = (f32[512,128]{1,0:T(8,128)S(1)}, f32[512,128]{1,0:T(8,128)S(1)}, u32[]{:S(2)}, u32[]{:S(2)}) collective-permute-start(f32[512,128]{1,0:T(8,128)S(1)} %pad_maximum_fusion.refs_0_), channel_id=1, source_target_pairs={{4,0},{5,1},{6,2},{7,3},{0,4},{1,5},{2,6},{3,7},{12,8},{13,9},{14,... | collective-permute-start | bytes 786440 | tf_op jit(solution)/shard_map/ppermute | solution.py:160
  22.2 1.0 %collective-permute-start.12 = (f32[512,128]{1,0:T(8,128)S(1)}, f32[512,128]{1,0:T(8,128)S(1)}, u32[]{:S(2)}, u32[]{:S(2)}) collective-permute-start(f32[512,128]{1,0:T(8,128)S(1)} %collective-permute-done.4), channel_id=1, source_target_pairs={{0,8},{4,12},{8,16},{12,20},{16,24},{20,28},{24,0},{28,4},{1,9},{5... | collective-permute-start | bytes 786440 | tf_op jit(solution)/shard_map/ppermute | solution.py:177
  23.2 0.0 collective-permute-start.5
  23.2 5.2 %collective-permute-done.10.refs_6_ = f32[512,128]{1,0:T(8,128)S(1)} collective-permute-done((f32[512,128]{1,0:T(8,128)S(1)}, f32[512,128]{1,0:T(8,128)S(1)}, u32[]{:S(2)}, u32[]{:S(2)}) %collective-permute-start.10) | collective-permute-done | bytes 262176 | tf_op jit(solution)/shard_map/ppermute | solution.py:160
  28.4 0.0 collective-permute-start.11
  28.4 2.7 %collective-permute-done.6.refs_2_ = f32[512,128]{1,0:T(8,128)S(1)} collective-permute-done((f32[512,128]{1,0:T(8,128)S(1)}, f32[512,128]{1,0:T(8,128)S(1)}, u32[]{:S(2)}, u32[]{:S(2)}) %collective-permute-start.6) | collective-permute-done | bytes 262176 | tf_op jit(solution)/shard_map/ppermute | solution.py:160
  31.1 0.0 collective-permute-start.7
  31.1 0.1 collective-permute-done.8.refs_4_
  31.2 0.4 %collective-permute-start.9 = (f32[512,128]{1,0:T(8,128)S(1)}, f32[512,128]{1,0:T(8,128)S(1)}, u32[]{:S(2)}, u32[]{:S(2)}) collective-permute-start(f32[512,128]{1,0:T(8,128)S(1)} %collective-permute-done.8.refs_4_), channel_id=1, source_target_pairs={{0,1},{1,0},{2,3},{3,2},{4,5},{5,4},{6,7},{7,6},{8,9},{9,8},{10,11... | collective-permute-start | bytes 786440 | tf_op jit(solution)/shard_map/ppermute | solution.py:162
  31.6 0.0 copy-start
  31.6 0.0 collective-permute-done.12
  31.6 0.0 collective-permute-done.5.refs_1_
  31.6 0.0 collective-permute-done.11.refs_7_
  31.6 1.0 %collective-permute-done.7.refs_3_ = f32[512,128]{1,0:T(8,128)S(1)} collective-permute-done((f32[512,128]{1,0:T(8,128)S(1)}, f32[512,128]{1,0:T(8,128)S(1)}, u32[]{:S(2)}, u32[]{:S(2)}) %collective-permute-start.7) | collective-permute-done | bytes 262176 | tf_op jit(solution)/shard_map/ppermute | solution.py:162
  32.6 0.4 collective-permute-done.9.refs_5_
  33.0 0.0 copy-done
  33.0 6.7 %shard_map.41 = (f32[512,128]{1,0:T(8,128)}, f32[512,128]{1,0:T(8,128)}) custom-call(f32[512,128]{1,0:T(8,128)S(1)} %pad_maximum_fusion.refs_0_, f32[512,128]{1,0:T(8,128)S(1)} %collective-permute-done.5.refs_1_, f32[512,128]{1,0:T(8,128)S(1)} %collective-permute-done.6.refs_2_, f32[512,128]{1,0:T(8,128)S(1)} %collective-permute-done.7.refs_3_, ...), custom_call_target="tpu_custom_call" | custom-call | tf_op jit(solution)/shard_map/pallas_call | solution.py:103
  (5 shorter events, 0.1 us)
Async XLA Ops:
  1.6 7.6 %copy-start.1 = (f32[512,1,128]{2,1,0:T(1,128)S(1)}, f32[512,1,128]{2,1,0:T(1,128)}, u32[]{:S(2)}) copy-start(f32[512,1,128]{2,1,0:T(1,128)} %param.2) | copy-start | bytes 786436
  1.7 9.2 %collective-permute-start = (f32[256,128]{1,0:T(8,128)S(1)}, f32[256,128]{1,0:T(8,128)S(1)}, u32[]{:S(2)}, u32[]{:S(2)}) collective-permute-start(f32[256,128]{1,0:T(8,128)S(1)} %get-tuple-element.14), channel_id=1, source_target_pairs={{0,8},{4,12},{8,0},{12,4},{16,24},{20,28},{24,16},{28,20},{1,9},{5... | collective-permute-start | bytes 393224 | tf_op jit(solution)/shard_map/ppermute | solution.py:120
  4.8 7.0 %collective-permute-start.1 = (f32[256,128]{1,0:T(8,128)S(1)}, f32[256,128]{1,0:T(8,128)S(1)}, u32[]{:S(2)}, u32[]{:S(2)}) collective-permute-start(f32[256,128]{1,0:T(8,128)S(1)} %get-tuple-element.15), channel_id=1, source_target_pairs={{0,16},{4,20},{1,17},{5,21},{2,18},{6,22},{3,19},{7,23}} | collective-permute-start | bytes 393224 | tf_op jit(solution)/shard_map/ppermute | solution.py:120
  9.3 7.6 %collective-permute-start.4 = (f32[512,128]{1,0:T(8,128)S(1)}, f32[512,128]{1,0:T(8,128)S(1)}, u32[]{:S(2)}, u32[]{:S(2)}) collective-permute-start(f32[512,128]{1,0:T(8,128)S(1)} %bitcast.11), channel_id=1, source_target_pairs={{0,4},{4,0},{8,12},{12,8},{16,20},{20,16},{24,28},{28,24},{1,5},{5... | collective-permute-start | bytes 786440 | tf_op jit(solution)/shard_map/ppermute | solution.py:173
  10.8 3.8 %collective-permute-start.3 = (f32[256,128]{1,0:T(8,128)S(1)}, f32[256,128]{1,0:T(8,128)S(1)}, u32[]{:S(2)}, u32[]{:S(2)}) collective-permute-start(f32[256,128]{1,0:T(8,128)S(1)} %collective-permute-done), channel_id=1, source_target_pairs={{8,24},{12,28},{9,25},{13,29},{10,26},{14,30},{11,27},{15,31}} | collective-permute-start | bytes 393224 | tf_op jit(solution)/shard_map/ppermute | solution.py:120
  11.8 6.8 %collective-permute-start.2 = (f32[256,128]{1,0:T(8,128)S(1)}, f32[256,128]{1,0:T(8,128)S(1)}, u32[]{:S(2)}, u32[]{:S(2)}) collective-permute-start(f32[256,128]{1,0:T(8,128)S(1)} %select_select_fusion.3), channel_id=1, source_target_pairs={{0,8},{4,12},{8,16},{12,20},{16,24},{20,28},{24,0},{28,4},{1,9},{5... | collective-permute-start | bytes 393224 | tf_op jit(solution)/shard_map/ppermute | solution.py:120
  18.7 9.7 %collective-permute-start.10 = (f32[512,128]{1,0:T(8,128)S(1)}, f32[512,128]{1,0:T(8,128)S(1)}, u32[]{:S(2)}, u32[]{:S(2)}) collective-permute-start(f32[512,128]{1,0:T(8,128)S(1)} %pad_maximum_fusion.refs_0_), channel_id=1, source_target_pairs={{6,0},{7,1},{4,2},{5,3},{2,4},{3,5},{0,6},{1,7},{14,8},{15,9},{12,... | collective-permute-start | bytes 786440 | tf_op jit(solution)/shard_map/ppermute | solution.py:160
  21.2 9.9 %collective-permute-start.6 = (f32[512,128]{1,0:T(8,128)S(1)}, f32[512,128]{1,0:T(8,128)S(1)}, u32[]{:S(2)}, u32[]{:S(2)}) collective-permute-start(f32[512,128]{1,0:T(8,128)S(1)} %pad_maximum_fusion.refs_0_), channel_id=1, source_target_pairs={{2,0},{3,1},{0,2},{1,3},{6,4},{7,5},{4,6},{5,7},{10,8},{11,9},{8,1... | collective-permute-start | bytes 786440 | tf_op jit(solution)/shard_map/ppermute | solution.py:160
  21.7 9.5 %collective-permute-start.8 = (f32[512,128]{1,0:T(8,128)S(1)}, f32[512,128]{1,0:T(8,128)S(1)}, u32[]{:S(2)}, u32[]{:S(2)}) collective-permute-start(f32[512,128]{1,0:T(8,128)S(1)} %pad_maximum_fusion.refs_0_), channel_id=1, source_target_pairs={{4,0},{5,1},{6,2},{7,3},{0,4},{1,5},{2,6},{3,7},{12,8},{13,9},{14,... | collective-permute-start | bytes 786440 | tf_op jit(solution)/shard_map/ppermute | solution.py:160
  22.2 9.4 %collective-permute-start.12 = (f32[512,128]{1,0:T(8,128)S(1)}, f32[512,128]{1,0:T(8,128)S(1)}, u32[]{:S(2)}, u32[]{:S(2)}) collective-permute-start(f32[512,128]{1,0:T(8,128)S(1)} %collective-permute-done.4), channel_id=1, source_target_pairs={{0,8},{4,12},{8,16},{12,20},{16,24},{20,28},{24,0},{28,4},{1,9},{5... | collective-permute-start | bytes 786440 | tf_op jit(solution)/shard_map/ppermute | solution.py:177
  23.2 8.4 %collective-permute-start.5 = (f32[512,128]{1,0:T(8,128)S(1)}, f32[512,128]{1,0:T(8,128)S(1)}, u32[]{:S(2)}, u32[]{:S(2)}) collective-permute-start(f32[512,128]{1,0:T(8,128)S(1)} %pad_maximum_fusion.refs_0_), channel_id=1, source_target_pairs={{0,1},{1,0},{2,3},{3,2},{4,5},{5,4},{6,7},{7,6},{8,9},{9,8},{10,11... | collective-permute-start | bytes 786440 | tf_op jit(solution)/shard_map/ppermute | solution.py:162
  28.4 3.3 %collective-permute-start.11 = (f32[512,128]{1,0:T(8,128)S(1)}, f32[512,128]{1,0:T(8,128)S(1)}, u32[]{:S(2)}, u32[]{:S(2)}) collective-permute-start(f32[512,128]{1,0:T(8,128)S(1)} %collective-permute-done.10.refs_6_), channel_id=1, source_target_pairs={{0,1},{1,0},{2,3},{3,2},{4,5},{5,4},{6,7},{7,6},{8,9},{9,8},{10,11... | collective-permute-start | bytes 786440 | tf_op jit(solution)/shard_map/ppermute | solution.py:162
  31.1 1.5 %collective-permute-start.7 = (f32[512,128]{1,0:T(8,128)S(1)}, f32[512,128]{1,0:T(8,128)S(1)}, u32[]{:S(2)}, u32[]{:S(2)}) collective-permute-start(f32[512,128]{1,0:T(8,128)S(1)} %collective-permute-done.6.refs_2_), channel_id=1, source_target_pairs={{0,1},{1,0},{2,3},{3,2},{4,5},{5,4},{6,7},{7,6},{8,9},{9,8},{10,11... | collective-permute-start | bytes 786440 | tf_op jit(solution)/shard_map/ppermute | solution.py:162
  31.2 1.8 %collective-permute-start.9 = (f32[512,128]{1,0:T(8,128)S(1)}, f32[512,128]{1,0:T(8,128)S(1)}, u32[]{:S(2)}, u32[]{:S(2)}) collective-permute-start(f32[512,128]{1,0:T(8,128)S(1)} %collective-permute-done.8.refs_4_), channel_id=1, source_target_pairs={{0,1},{1,0},{2,3},{3,2},{4,5},{5,4},{6,7},{7,6},{8,9},{9,8},{10,11... | collective-permute-start | bytes 786440 | tf_op jit(solution)/shard_map/ppermute | solution.py:162
  31.6 1.4 %copy-start = (f32[512,1,128]{2,1,0:T(1,128)S(1)}, f32[512,1,128]{2,1,0:T(1,128)}, u32[]{:S(2)}) copy-start(f32[512,1,128]{2,1,0:T(1,128)} %param.3) | copy-start | bytes 786436

commit v7 on v6

--- a/solution.py
+++ b/solution.py
@@ -173,9 +173,8 @@
     swapped = lax.ppermute(upper, "blk", [(source, source ^ 1) for source in range(blocks)])
     share = jnp.where(side == 0, upper, lower)
     share, swapped = spread(share, swapped, rows, block // PAIR)
-    forward = [(source, (source + PAIR) % blocks) for source in range(blocks)]
-    onward = lax.ppermute(swapped, "blk", forward)
-    shifted = jnp.where(side == 1, swapped, jnp.where(block == 0, 0.0, onward))
+    ahead = [(source, source + PAIR) for source in range(0, blocks - PAIR, PAIR)]
+    shifted = jnp.where(side == 1, swapped, lax.ppermute(swapped, "blk", ahead))
     shares = exchange(share, rows, groups)
     new_upper, new_lower = step_call(shares, shifted, lower, groups)
     return new_upper[:, None, :], new_lower[:, None, :]

time: 39.9 us -> 39.9 us (level)
  starting transfers between devices: 17.5 us -> 19.5 us
  waiting for transfers between devices: 13.6 us -> 11.6 us
    ppermute x3, waiting for transfers between devices: 7.97 us -> 5.98 us  [exchange(): mine = lax.ppermute(share, ('blk', 'col'), sends) if flip or step else share]
    ppermute x1, starting transfers between devices: 0.96 us -> 2.87 us  [shards(): shifted = jnp.where(side == 1, swapped, lax.ppermute(swapped, 'blk', ahead))]
where the time goes in v7:
time: 39.9 us; the launch traced here: 39.7 us
  starting transfers between devices  19.5 us (49%)
  waiting for transfers between devices  11.6 us (29%)
  Pallas kernels  6.71 us (17%)
  other arithmetic  1.1 us (3%)
  between operations  0.74 us (2%)
    ppermute x4, starting transfers between devices, send(): return lax.ppermute(value, 'blk', pairs)  11 us
    pallas_call x1, Pallas kernels, step_call(): pl.pallas_call(functools.partial(step_kernel, groups), out_shape=(jax.Sha...  6.71 us
    ppermute x3, waiting for transfers between devices, exchange(): mine = lax.ppermute(share, ('blk', 'col'), sends) if flip or step else share  5.98 us
    ppermute x3, starting transfers between devices, exchange(): mine = lax.ppermute(share, ('blk', 'col'), sends) if flip or step else share  3.55 us
    ppermute x1, starting transfers between devices, shards(): shifted = jnp.where(side == 1, swapped, lax.ppermute(swapped, 'blk', ahead))  2.87 us
    ppermute x1, waiting for transfers between devices, shards(): lax.ppermute(upper, 'blk', [(source, source ^ 1) for source in range(bloc...  2.23 us
    ppermute x4, waiting for transfers between devices, send(): return lax.ppermute(value, 'blk', pairs)  2.04 us
    ppermute x1, starting transfers between devices, shards(): lax.ppermute(upper, 'blk', [(source, source ^ 1) for source in range(bloc...  1.56 us
  transfers between devices with their start and end apart: 13, of which 8 were waited for; matrix products, arithmetic and copies ran while one was open for 0% of the time, Pallas kernels for 0%

profile of v7, /device:TPU:0, one launch (start us, length us, event | category | flops | bytes accessed | tf_op | source)
XLA Modules:
  0.0 39.7 jit_solution(10758230517550224348)
XLA Ops:
  0.6 1.0 %broadcast_select_fusion.1 = f32[512,128]{1,0:T(8,128)S(1)} fusion(f32[512,128]{1,0:T(8,128)} %bitcast.10, f32[512,128]{1,0:T(8,128)} %bitcast.8, pred[]{:T(512)S(6)} %eq.20), kind=kLoop, calls=%fused_computation.5 | loop fusion | flops 65536 | bytes 786433 | tf_op jit(solution)/shard_map/jit(_where)/select_n | solution.py:174
  1.6 0.0 copy-start.1
  1.7 3.1 %collective-permute-start = (f32[256,128]{1,0:T(8,128)S(1)}, f32[256,128]{1,0:T(8,128)S(1)}, u32[]{:S(2)}, u32[]{:S(2)}) collective-permute-start(f32[256,128]{1,0:T(8,128)S(1)} %get-tuple-element.14), channel_id=1, source_target_pairs={{0,8},{4,12},{8,0},{12,4},{16,24},{20,28},{24,16},{28,20},{1,9},{5... | collective-permute-start | bytes 393224 | tf_op jit(solution)/shard_map/ppermute | solution.py:120
  4.8 4.5 %collective-permute-start.1 = (f32[256,128]{1,0:T(8,128)S(1)}, f32[256,128]{1,0:T(8,128)S(1)}, u32[]{:S(2)}, u32[]{:S(2)}) collective-permute-start(f32[256,128]{1,0:T(8,128)S(1)} %get-tuple-element.15), channel_id=1, source_target_pairs={{0,16},{4,20},{1,17},{5,21},{2,18},{6,22},{3,19},{7,23}} | collective-permute-start | bytes 393224 | tf_op jit(solution)/shard_map/ppermute | solution.py:120
  9.3 0.0 copy-done.1
  9.3 1.6 %collective-permute-start.4 = (f32[512,128]{1,0:T(8,128)S(1)}, f32[512,128]{1,0:T(8,128)S(1)}, u32[]{:S(2)}, u32[]{:S(2)}) collective-permute-start(f32[512,128]{1,0:T(8,128)S(1)} %bitcast.11), channel_id=1, source_target_pairs={{0,4},{4,0},{8,12},{12,8},{16,20},{20,16},{24,28},{28,24},{1,5},{5... | collective-permute-start | bytes 786440 | tf_op jit(solution)/shard_map/ppermute | solution.py:173
  10.8 0.0 collective-permute-done
  10.8 0.7 %collective-permute-start.3 = (f32[256,128]{1,0:T(8,128)S(1)}, f32[256,128]{1,0:T(8,128)S(1)}, u32[]{:S(2)}, u32[]{:S(2)}) collective-permute-start(f32[256,128]{1,0:T(8,128)S(1)} %collective-permute-done), channel_id=1, source_target_pairs={{8,24},{12,28},{9,25},{13,29},{10,26},{14,30},{11,27},{15,31}} | collective-permute-start | bytes 393224 | tf_op jit(solution)/shard_map/ppermute | solution.py:120
  11.5 0.3 collective-permute-done.1
  11.8 2.8 %collective-permute-start.2 = (f32[256,128]{1,0:T(8,128)S(1)}, f32[256,128]{1,0:T(8,128)S(1)}, u32[]{:S(2)}, u32[]{:S(2)}) collective-permute-start(f32[256,128]{1,0:T(8,128)S(1)} %select_select_fusion.2), channel_id=1, source_target_pairs={{0,8},{4,12},{8,16},{12,20},{16,24},{20,28},{24,0},{28,4},{1,9},{5... | collective-permute-start | bytes 393224 | tf_op jit(solution)/shard_map/ppermute | solution.py:120
  14.6 0.0 collective-permute-done.3
  14.6 2.2 %collective-permute-done.4 = f32[512,128]{1,0:T(8,128)S(1)} collective-permute-done((f32[512,128]{1,0:T(8,128)S(1)}, f32[512,128]{1,0:T(8,128)S(1)}, u32[]{:S(2)}, u32[]{:S(2)}) %collective-permute-start.4) | collective-permute-done | bytes 262176 | tf_op jit(solution)/shard_map/ppermute | solution.py:173
  16.8 1.8 %collective-permute-done.2 = f32[256,128]{1,0:T(8,128)S(1)} collective-permute-done((f32[256,128]{1,0:T(8,128)S(1)}, f32[256,128]{1,0:T(8,128)S(1)}, u32[]{:S(2)}, u32[]{:S(2)}) %collective-permute-start.2) | collective-permute-done | bytes 131104 | tf_op jit(solution)/shard_map/ppermute | solution.py:120
  18.7 2.5 %collective-permute-start.10 = (f32[512,128]{1,0:T(8,128)S(1)}, f32[512,128]{1,0:T(8,128)S(1)}, u32[]{:S(2)}, u32[]{:S(2)}) collective-permute-start(f32[512,128]{1,0:T(8,128)S(1)} %pad_maximum_fusion.refs_0_), channel_id=1, source_target_pairs={{6,0},{7,1},{4,2},{5,3},{2,4},{3,5},{0,6},{1,7},{14,8},{15,9},{12,... | collective-permute-start | bytes 786440 | tf_op jit(solution)/shard_map/ppermute | solution.py:160
  21.2 0.5 %collective-permute-start.6 = (f32[512,128]{1,0:T(8,128)S(1)}, f32[512,128]{1,0:T(8,128)S(1)}, u32[]{:S(2)}, u32[]{:S(2)}) collective-permute-start(f32[512,128]{1,0:T(8,128)S(1)} %pad_maximum_fusion.refs_0_), channel_id=1, source_target_pairs={{2,0},{3,1},{0,2},{1,3},{6,4},{7,5},{4,6},{5,7},{10,8},{11,9},{8,1... | collective-permute-start | bytes 786440 | tf_op jit(solution)/shard_map/ppermute | solution.py:160
  21.7 0.5 %collective-permute-start.8 = (f32[512,128]{1,0:T(8,128)S(1)}, f32[512,128]{1,0:T(8,128)S(1)}, u32[]{:S(2)}, u32[]{:S(2)}) collective-permute-start(f32[512,128]{1,0:T(8,128)S(1)} %pad_maximum_fusion.refs_0_), channel_id=1, source_target_pairs={{4,0},{5,1},{6,2},{7,3},{0,4},{1,5},{2,6},{3,7},{12,8},{13,9},{14,... | collective-permute-start | bytes 786440 | tf_op jit(solution)/shard_map/ppermute | solution.py:160
  22.2 2.9 %collective-permute-start.12 = (f32[512,128]{1,0:T(8,128)S(1)}, f32[512,128]{1,0:T(8,128)S(1)}, u32[]{:S(2)}, u32[]{:S(2)}) collective-permute-start(f32[512,128]{1,0:T(8,128)S(1)} %collective-permute-done.4), channel_id=1, source_target_pairs={{0,8},{8,16},{16,24},{1,9},{9,17},{17,25},{2,10},{10,18},{18,26},{... | collective-permute-start | bytes 786440 | tf_op jit(solution)/shard_map/ppermute | solution.py:177
  25.1 0.1 collective-permute-start.5
  25.2 3.2 %collective-permute-done.10.refs_6_ = f32[512,128]{1,0:T(8,128)S(1)} collective-permute-done((f32[512,128]{1,0:T(8,128)S(1)}, f32[512,128]{1,0:T(8,128)S(1)}, u32[]{:S(2)}, u32[]{:S(2)}) %collective-permute-start.10) | collective-permute-done | bytes 262176 | tf_op jit(solution)/shard_map/ppermute | solution.py:160
  28.4 0.0 collective-permute-start.11
  28.4 2.7 %collective-permute-done.6.refs_2_ = f32[512,128]{1,0:T(8,128)S(1)} collective-permute-done((f32[512,128]{1,0:T(8,128)S(1)}, f32[512,128]{1,0:T(8,128)S(1)}, u32[]{:S(2)}, u32[]{:S(2)}) %collective-permute-start.6) | collective-permute-done | bytes 262176 | tf_op jit(solution)/shard_map/ppermute | solution.py:160
  31.1 0.0 collective-permute-start.7
  31.1 0.1 collective-permute-done.8.refs_4_
  31.2 0.4 %collective-permute-start.9 = (f32[512,128]{1,0:T(8,128)S(1)}, f32[512,128]{1,0:T(8,128)S(1)}, u32[]{:S(2)}, u32[]{:S(2)}) collective-permute-start(f32[512,128]{1,0:T(8,128)S(1)} %collective-permute-done.8.refs_4_), channel_id=1, source_target_pairs={{0,1},{1,0},{2,3},{3,2},{4,5},{5,4},{6,7},{7,6},{8,9},{9,8},{10,11... | collective-permute-start | bytes 786440 | tf_op jit(solution)/shard_map/ppermute | solution.py:162
  31.6 0.0 copy-start
  31.6 0.0 collective-permute-done.12
  31.6 0.0 collective-permute-done.5.refs_1_
  31.6 0.0 collective-permute-done.11.refs_7_
  31.6 1.0 %collective-permute-done.7.refs_3_ = f32[512,128]{1,0:T(8,128)S(1)} collective-permute-done((f32[512,128]{1,0:T(8,128)S(1)}, f32[512,128]{1,0:T(8,128)S(1)}, u32[]{:S(2)}, u32[]{:S(2)}) %collective-permute-start.7) | collective-permute-done | bytes 262176 | tf_op jit(solution)/shard_map/ppermute | solution.py:162
  32.6 0.4 collective-permute-done.9.refs_5_
  33.0 0.0 copy-done
  33.0 6.7 %shard_map.41 = (f32[512,128]{1,0:T(8,128)}, f32[512,128]{1,0:T(8,128)}) custom-call(f32[512,128]{1,0:T(8,128)S(1)} %pad_maximum_fusion.refs_0_, f32[512,128]{1,0:T(8,128)S(1)} %collective-permute-done.5.refs_1_, f32[512,128]{1,0:T(8,128)S(1)} %collective-permute-done.6.refs_2_, f32[512,128]{1,0:T(8,128)S(1)} %collective-permute-done.7.refs_3_, ...), custom_call_target="tpu_custom_call" | custom-call | tf_op jit(solution)/shard_map/pallas_call | solution.py:103
  (5 shorter events, 0.1 us)
Async XLA Ops:
  1.6 7.6 %copy-start.1 = (f32[512,1,128]{2,1,0:T(1,128)S(1)}, f32[512,1,128]{2,1,0:T(1,128)}, u32[]{:S(2)}) copy-start(f32[512,1,128]{2,1,0:T(1,128)} %param.2) | copy-start | bytes 786436
  1.7 9.2 %collective-permute-start = (f32[256,128]{1,0:T(8,128)S(1)}, f32[256,128]{1,0:T(8,128)S(1)}, u32[]{:S(2)}, u32[]{:S(2)}) collective-permute-start(f32[256,128]{1,0:T(8,128)S(1)} %get-tuple-element.14), channel_id=1, source_target_pairs={{0,8},{4,12},{8,0},{12,4},{16,24},{20,28},{24,16},{28,20},{1,9},{5... | collective-permute-start | bytes 393224 | tf_op jit(solution)/shard_map/ppermute | solution.py:120
  4.8 7.0 %collective-permute-start.1 = (f32[256,128]{1,0:T(8,128)S(1)}, f32[256,128]{1,0:T(8,128)S(1)}, u32[]{:S(2)}, u32[]{:S(2)}) collective-permute-start(f32[256,128]{1,0:T(8,128)S(1)} %get-tuple-element.15), channel_id=1, source_target_pairs={{0,16},{4,20},{1,17},{5,21},{2,18},{6,22},{3,19},{7,23}} | collective-permute-start | bytes 393224 | tf_op jit(solution)/shard_map/ppermute | solution.py:120
  9.3 7.6 %collective-permute-start.4 = (f32[512,128]{1,0:T(8,128)S(1)}, f32[512,128]{1,0:T(8,128)S(1)}, u32[]{:S(2)}, u32[]{:S(2)}) collective-permute-start(f32[512,128]{1,0:T(8,128)S(1)} %bitcast.11), channel_id=1, source_target_pairs={{0,4},{4,0},{8,12},{12,8},{16,20},{20,16},{24,28},{28,24},{1,5},{5... | collective-permute-start | bytes 786440 | tf_op jit(solution)/shard_map/ppermute | solution.py:173
  10.8 3.8 %collective-permute-start.3 = (f32[256,128]{1,0:T(8,128)S(1)}, f32[256,128]{1,0:T(8,128)S(1)}, u32[]{:S(2)}, u32[]{:S(2)}) collective-permute-start(f32[256,128]{1,0:T(8,128)S(1)} %collective-permute-done), channel_id=1, source_target_pairs={{8,24},{12,28},{9,25},{13,29},{10,26},{14,30},{11,27},{15,31}} | collective-permute-start | bytes 393224 | tf_op jit(solution)/shard_map/ppermute | solution.py:120
  11.8 6.8 %collective-permute-start.2 = (f32[256,128]{1,0:T(8,128)S(1)}, f32[256,128]{1,0:T(8,128)S(1)}, u32[]{:S(2)}, u32[]{:S(2)}) collective-permute-start(f32[256,128]{1,0:T(8,128)S(1)} %select_select_fusion.2), channel_id=1, source_target_pairs={{0,8},{4,12},{8,16},{12,20},{16,24},{20,28},{24,0},{28,4},{1,9},{5... | collective-permute-start | bytes 393224 | tf_op jit(solution)/shard_map/ppermute | solution.py:120
  18.7 9.7 %collective-permute-start.10 = (f32[512,128]{1,0:T(8,128)S(1)}, f32[512,128]{1,0:T(8,128)S(1)}, u32[]{:S(2)}, u32[]{:S(2)}) collective-permute-start(f32[512,128]{1,0:T(8,128)S(1)} %pad_maximum_fusion.refs_0_), channel_id=1, source_target_pairs={{6,0},{7,1},{4,2},{5,3},{2,4},{3,5},{0,6},{1,7},{14,8},{15,9},{12,... | collective-permute-start | bytes 786440 | tf_op jit(solution)/shard_map/ppermute | solution.py:160
  21.2 9.9 %collective-permute-start.6 = (f32[512,128]{1,0:T(8,128)S(1)}, f32[512,128]{1,0:T(8,128)S(1)}, u32[]{:S(2)}, u32[]{:S(2)}) collective-permute-start(f32[512,128]{1,0:T(8,128)S(1)} %pad_maximum_fusion.refs_0_), channel_id=1, source_target_pairs={{2,0},{3,1},{0,2},{1,3},{6,4},{7,5},{4,6},{5,7},{10,8},{11,9},{8,1... | collective-permute-start | bytes 786440 | tf_op jit(solution)/shard_map/ppermute | solution.py:160
  21.7 9.5 %collective-permute-start.8 = (f32[512,128]{1,0:T(8,128)S(1)}, f32[512,128]{1,0:T(8,128)S(1)}, u32[]{:S(2)}, u32[]{:S(2)}) collective-permute-start(f32[512,128]{1,0:T(8,128)S(1)} %pad_maximum_fusion.refs_0_), channel_id=1, source_target_pairs={{4,0},{5,1},{6,2},{7,3},{0,4},{1,5},{2,6},{3,7},{12,8},{13,9},{14,... | collective-permute-start | bytes 786440 | tf_op jit(solution)/shard_map/ppermute | solution.py:160
  22.2 9.4 %collective-permute-start.12 = (f32[512,128]{1,0:T(8,128)S(1)}, f32[512,128]{1,0:T(8,128)S(1)}, u32[]{:S(2)}, u32[]{:S(2)}) collective-permute-start(f32[512,128]{1,0:T(8,128)S(1)} %collective-permute-done.4), channel_id=1, source_target_pairs={{0,8},{8,16},{16,24},{1,9},{9,17},{17,25},{2,10},{10,18},{18,26},{... | collective-permute-start | bytes 786440 | tf_op jit(solution)/shard_map/ppermute | solution.py:177
  25.1 6.5 %collective-permute-start.5 = (f32[512,128]{1,0:T(8,128)S(1)}, f32[512,128]{1,0:T(8,128)S(1)}, u32[]{:S(2)}, u32[]{:S(2)}) collective-permute-start(f32[512,128]{1,0:T(8,128)S(1)} %pad_maximum_fusion.refs_0_), channel_id=1, source_target_pairs={{0,1},{1,0},{2,3},{3,2},{4,5},{5,4},{6,7},{7,6},{8,9},{9,8},{10,11... | collective-permute-start | bytes 786440 | tf_op jit(solution)/shard_map/ppermute | solution.py:162
  28.4 3.3 %collective-permute-start.11 = (f32[512,128]{1,0:T(8,128)S(1)}, f32[512,128]{1,0:T(8,128)S(1)}, u32[]{:S(2)}, u32[]{:S(2)}) collective-permute-start(f32[512,128]{1,0:T(8,128)S(1)} %collective-permute-done.10.refs_6_), channel_id=1, source_target_pairs={{0,1},{1,0},{2,3},{3,2},{4,5},{5,4},{6,7},{7,6},{8,9},{9,8},{10,11... | collective-permute-start | bytes 786440 | tf_op jit(solution)/shard_map/ppermute | solution.py:162
  31.1 1.5 %collective-permute-start.7 = (f32[512,128]{1,0:T(8,128)S(1)}, f32[512,128]{1,0:T(8,128)S(1)}, u32[]{:S(2)}, u32[]{:S(2)}) collective-permute-start(f32[512,128]{1,0:T(8,128)S(1)} %collective-permute-done.6.refs_2_), channel_id=1, source_target_pairs={{0,1},{1,0},{2,3},{3,2},{4,5},{5,4},{6,7},{7,6},{8,9},{9,8},{10,11... | collective-permute-start | bytes 786440 | tf_op jit(solution)/shard_map/ppermute | solution.py:162
  31.2 1.8 %collective-permute-start.9 = (f32[512,128]{1,0:T(8,128)S(1)}, f32[512,128]{1,0:T(8,128)S(1)}, u32[]{:S(2)}, u32[]{:S(2)}) collective-permute-start(f32[512,128]{1,0:T(8,128)S(1)} %collective-permute-done.8.refs_4_), channel_id=1, source_target_pairs={{0,1},{1,0},{2,3},{3,2},{4,5},{5,4},{6,7},{7,6},{8,9},{9,8},{10,11... | collective-permute-start | bytes 786440 | tf_op jit(solution)/shard_map/ppermute | solution.py:162
  31.6 1.4 %copy-start = (f32[512,1,128]{2,1,0:T(1,128)S(1)}, f32[512,1,128]{2,1,0:T(1,128)}, u32[]{:S(2)}) copy-start(f32[512,1,128]{2,1,0:T(1,128)} %param.3) | copy-start | bytes 786436

commit v8 on v7

--- a/solution.py
+++ b/solution.py
@@ -87,13 +87,15 @@
     made_lower[...] = (lower - bent + inner_lower).T
     lower_copy = pltpu.make_async_copy(made_lower, new_lower_ref, sent.at[0])
     lower_copy.start()
+    copies = [lower_copy]
     upper = upper - thin_product(lower - inner_upper, reflect)
     for i, part in enumerate(rows):
         made_upper[part, :] = upper[:, i * width : (i + 1) * width].T
-    upper_copy = pltpu.make_async_copy(made_upper, new_upper_ref, sent.at[1])
-    upper_copy.start()
-    lower_copy.wait()
-    upper_copy.wait()
+        copy = pltpu.make_async_copy(made_upper.at[part, :], new_upper_ref.at[part, :], sent.at[1 + i])
+        copy.start()
+        copies.append(copy)
+    for copy in copies:
+        copy.wait()
 
 
 def step_call(shares, upper, lower, groups):
@@ -107,7 +109,7 @@
         out_specs=(pl.BlockSpec(memory_space=pl.ANY),) * 2,
         scratch_shapes=[pltpu.VMEM((order, order), jnp.bfloat16)] * 2
         + [pltpu.VMEM((order, width), jnp.float32)] * 2
-        + [pltpu.SemaphoreType.DMA((2,))],
+        + [pltpu.SemaphoreType.DMA((1 + count,))],
         compiler_params=pltpu.CompilerParams(vmem_limit_bytes=48 * 1024 * 1024),
     )(*shares, upper, lower)
 

time: 39.9 us -> 39.9 us (level)
  no operation moved by 1% of the time
where the time goes in v8:
time: 39.9 us; the launch traced here: 39.7 us
  starting transfers between devices  19.5 us (49%)
  waiting for transfers between devices  11.6 us (29%)
  Pallas kernels  6.69 us (17%)
  other arithmetic  1.1 us (3%)
  between operations  0.74 us (2%)
    ppermute x4, starting transfers between devices, send(): return lax.ppermute(value, 'blk', pairs)  11 us
    pallas_call x1, Pallas kernels, step_call(): pl.pallas_call(functools.partial(step_kernel, groups), out_shape=(jax.Sha...  6.69 us
    ppermute x3, waiting for transfers between devices, exchange(): mine = lax.ppermute(share, ('blk', 'col'), sends) if flip or step else share  5.98 us
    ppermute x3, starting transfers between devices, exchange(): mine = lax.ppermute(share, ('blk', 'col'), sends) if flip or step else share  3.55 us
    ppermute x1, starting transfers between devices, shards(): shifted = jnp.where(side == 1, swapped, lax.ppermute(swapped, 'blk', ahead))  2.87 us
    ppermute x1, waiting for transfers between devices, shards(): lax.ppermute(upper, 'blk', [(source, source ^ 1) for source in range(bloc...  2.23 us
    ppermute x4, waiting for transfers between devices, send(): return lax.ppermute(value, 'blk', pairs)  2.04 us
    ppermute x1, starting transfers between devices, shards(): lax.ppermute(upper, 'blk', [(source, source ^ 1) for source in range(bloc...  1.56 us
  transfers between devices with their start and end apart: 13, of which 8 were waited for; matrix products, arithmetic and copies ran while one was open for 0% of the time, Pallas kernels for 0%

profile of v8, /device:TPU:0, one launch (start us, length us, event | category | flops | bytes accessed | tf_op | source)
XLA Modules:
  0.0 39.7 jit_solution(15098025271459083080)
XLA Ops:
  0.6 1.0 %broadcast_select_fusion.1 = f32[512,128]{1,0:T(8,128)S(1)} fusion(f32[512,128]{1,0:T(8,128)} %bitcast.10, f32[512,128]{1,0:T(8,128)} %bitcast.8, pred[]{:T(512)S(6)} %eq.20), kind=kLoop, calls=%fused_computation.5 | loop fusion | flops 65536 | bytes 786433 | tf_op jit(solution)/shard_map/jit(_where)/select_n | solution.py:176
  1.6 0.0 copy-start.1
  1.7 3.1 %collective-permute-start = (f32[256,128]{1,0:T(8,128)S(1)}, f32[256,128]{1,0:T(8,128)S(1)}, u32[]{:S(2)}, u32[]{:S(2)}) collective-permute-start(f32[256,128]{1,0:T(8,128)S(1)} %get-tuple-element.14), channel_id=1, source_target_pairs={{0,8},{4,12},{8,0},{12,4},{16,24},{20,28},{24,16},{28,20},{1,9},{5... | collective-permute-start | bytes 393224 | tf_op jit(solution)/shard_map/ppermute | solution.py:122
  4.8 4.5 %collective-permute-start.1 = (f32[256,128]{1,0:T(8,128)S(1)}, f32[256,128]{1,0:T(8,128)S(1)}, u32[]{:S(2)}, u32[]{:S(2)}) collective-permute-start(f32[256,128]{1,0:T(8,128)S(1)} %get-tuple-element.15), channel_id=1, source_target_pairs={{0,16},{4,20},{1,17},{5,21},{2,18},{6,22},{3,19},{7,23}} | collective-permute-start | bytes 393224 | tf_op jit(solution)/shard_map/ppermute | solution.py:122
  9.3 0.0 copy-done.1
  9.3 1.6 %collective-permute-start.4 = (f32[512,128]{1,0:T(8,128)S(1)}, f32[512,128]{1,0:T(8,128)S(1)}, u32[]{:S(2)}, u32[]{:S(2)}) collective-permute-start(f32[512,128]{1,0:T(8,128)S(1)} %bitcast.11), channel_id=1, source_target_pairs={{0,4},{4,0},{8,12},{12,8},{16,20},{20,16},{24,28},{28,24},{1,5},{5... | collective-permute-start | bytes 786440 | tf_op jit(solution)/shard_map/ppermute | solution.py:175
  10.8 0.0 collective-permute-done
  10.8 0.7 %collective-permute-start.3 = (f32[256,128]{1,0:T(8,128)S(1)}, f32[256,128]{1,0:T(8,128)S(1)}, u32[]{:S(2)}, u32[]{:S(2)}) collective-permute-start(f32[256,128]{1,0:T(8,128)S(1)} %collective-permute-done), channel_id=1, source_target_pairs={{8,24},{12,28},{9,25},{13,29},{10,26},{14,30},{11,27},{15,31}} | collective-permute-start | bytes 393224 | tf_op jit(solution)/shard_map/ppermute | solution.py:122
  11.5 0.3 collective-permute-done.1
  11.8 2.8 %collective-permute-start.2 = (f32[256,128]{1,0:T(8,128)S(1)}, f32[256,128]{1,0:T(8,128)S(1)}, u32[]{:S(2)}, u32[]{:S(2)}) collective-permute-start(f32[256,128]{1,0:T(8,128)S(1)} %select_select_fusion.2), channel_id=1, source_target_pairs={{0,8},{4,12},{8,16},{12,20},{16,24},{20,28},{24,0},{28,4},{1,9},{5... | collective-permute-start | bytes 393224 | tf_op jit(solution)/shard_map/ppermute | solution.py:122
  14.6 0.0 collective-permute-done.3
  14.6 2.2 %collective-permute-done.4 = f32[512,128]{1,0:T(8,128)S(1)} collective-permute-done((f32[512,128]{1,0:T(8,128)S(1)}, f32[512,128]{1,0:T(8,128)S(1)}, u32[]{:S(2)}, u32[]{:S(2)}) %collective-permute-start.4) | collective-permute-done | bytes 262176 | tf_op jit(solution)/shard_map/ppermute | solution.py:175
  16.8 1.8 %collective-permute-done.2 = f32[256,128]{1,0:T(8,128)S(1)} collective-permute-done((f32[256,128]{1,0:T(8,128)S(1)}, f32[256,128]{1,0:T(8,128)S(1)}, u32[]{:S(2)}, u32[]{:S(2)}) %collective-permute-start.2) | collective-permute-done | bytes 131104 | tf_op jit(solution)/shard_map/ppermute | solution.py:122
  18.7 2.5 %collective-permute-start.10 = (f32[512,128]{1,0:T(8,128)S(1)}, f32[512,128]{1,0:T(8,128)S(1)}, u32[]{:S(2)}, u32[]{:S(2)}) collective-permute-start(f32[512,128]{1,0:T(8,128)S(1)} %pad_maximum_fusion.refs_0_), channel_id=1, source_target_pairs={{6,0},{7,1},{4,2},{5,3},{2,4},{3,5},{0,6},{1,7},{14,8},{15,9},{12,... | collective-permute-start | bytes 786440 | tf_op jit(solution)/shard_map/ppermute | solution.py:162
  21.2 0.5 %collective-permute-start.6 = (f32[512,128]{1,0:T(8,128)S(1)}, f32[512,128]{1,0:T(8,128)S(1)}, u32[]{:S(2)}, u32[]{:S(2)}) collective-permute-start(f32[512,128]{1,0:T(8,128)S(1)} %pad_maximum_fusion.refs_0_), channel_id=1, source_target_pairs={{2,0},{3,1},{0,2},{1,3},{6,4},{7,5},{4,6},{5,7},{10,8},{11,9},{8,1... | collective-permute-start | bytes 786440 | tf_op jit(solution)/shard_map/ppermute | solution.py:162
  21.7 0.5 %collective-permute-start.8 = (f32[512,128]{1,0:T(8,128)S(1)}, f32[512,128]{1,0:T(8,128)S(1)}, u32[]{:S(2)}, u32[]{:S(2)}) collective-permute-start(f32[512,128]{1,0:T(8,128)S(1)} %pad_maximum_fusion.refs_0_), channel_id=1, source_target_pairs={{4,0},{5,1},{6,2},{7,3},{0,4},{1,5},{2,6},{3,7},{12,8},{13,9},{14,... | collective-permute-start | bytes 786440 | tf_op jit(solution)/shard_map/ppermute | solution.py:162
  22.2 2.9 %collective-permute-start.12 = (f32[512,128]{1,0:T(8,128)S(1)}, f32[512,128]{1,0:T(8,128)S(1)}, u32[]{:S(2)}, u32[]{:S(2)}) collective-permute-start(f32[512,128]{1,0:T(8,128)S(1)} %collective-permute-done.4), channel_id=1, source_target_pairs={{0,8},{8,16},{16,24},{1,9},{9,17},{17,25},{2,10},{10,18},{18,26},{... | collective-permute-start | bytes 786440 | tf_op jit(solution)/shard_map/ppermute | solution.py:179
  25.1 0.1 collective-permute-start.5
  25.2 3.2 %collective-permute-done.10.refs_6_ = f32[512,128]{1,0:T(8,128)S(1)} collective-permute-done((f32[512,128]{1,0:T(8,128)S(1)}, f32[512,128]{1,0:T(8,128)S(1)}, u32[]{:S(2)}, u32[]{:S(2)}) %collective-permute-start.10) | collective-permute-done | bytes 262176 | tf_op jit(solution)/shard_map/ppermute | solution.py:162
  28.4 0.0 collective-permute-start.11
  28.4 2.7 %collective-permute-done.6.refs_2_ = f32[512,128]{1,0:T(8,128)S(1)} collective-permute-done((f32[512,128]{1,0:T(8,128)S(1)}, f32[512,128]{1,0:T(8,128)S(1)}, u32[]{:S(2)}, u32[]{:S(2)}) %collective-permute-start.6) | collective-permute-done | bytes 262176 | tf_op jit(solution)/shard_map/ppermute | solution.py:162
  31.1 0.0 collective-permute-start.7
  31.1 0.1 collective-permute-done.8.refs_4_
  31.2 0.4 %collective-permute-start.9 = (f32[512,128]{1,0:T(8,128)S(1)}, f32[512,128]{1,0:T(8,128)S(1)}, u32[]{:S(2)}, u32[]{:S(2)}) collective-permute-start(f32[512,128]{1,0:T(8,128)S(1)} %collective-permute-done.8.refs_4_), channel_id=1, source_target_pairs={{0,1},{1,0},{2,3},{3,2},{4,5},{5,4},{6,7},{7,6},{8,9},{9,8},{10,11... | collective-permute-start | bytes 786440 | tf_op jit(solution)/shard_map/ppermute | solution.py:164
  31.6 0.0 copy-start
  31.6 0.0 collective-permute-done.12
  31.6 0.0 collective-permute-done.5.refs_1_
  31.6 0.0 collective-permute-done.11.refs_7_
  31.6 1.0 %collective-permute-done.7.refs_3_ = f32[512,128]{1,0:T(8,128)S(1)} collective-permute-done((f32[512,128]{1,0:T(8,128)S(1)}, f32[512,128]{1,0:T(8,128)S(1)}, u32[]{:S(2)}, u32[]{:S(2)}) %collective-permute-start.7) | collective-permute-done | bytes 262176 | tf_op jit(solution)/shard_map/ppermute | solution.py:164
  32.6 0.4 collective-permute-done.9.refs_5_
  33.0 0.0 copy-done
  33.0 6.7 %shard_map.41 = (f32[512,128]{1,0:T(8,128)}, f32[512,128]{1,0:T(8,128)}) custom-call(f32[512,128]{1,0:T(8,128)S(1)} %pad_maximum_fusion.refs_0_, f32[512,128]{1,0:T(8,128)S(1)} %collective-permute-done.5.refs_1_, f32[512,128]{1,0:T(8,128)S(1)} %collective-permute-done.6.refs_2_, f32[512,128]{1,0:T(8,128)S(1)} %collective-permute-done.7.refs_3_, ...), custom_call_target="tpu_custom_call" | custom-call | tf_op jit(solution)/shard_map/pallas_call | solution.py:105
  (5 shorter events, 0.1 us)
Async XLA Ops:
  1.6 7.6 %copy-start.1 = (f32[512,1,128]{2,1,0:T(1,128)S(1)}, f32[512,1,128]{2,1,0:T(1,128)}, u32[]{:S(2)}) copy-start(f32[512,1,128]{2,1,0:T(1,128)} %param.2) | copy-start | bytes 786436
  1.7 9.2 %collective-permute-start = (f32[256,128]{1,0:T(8,128)S(1)}, f32[256,128]{1,0:T(8,128)S(1)}, u32[]{:S(2)}, u32[]{:S(2)}) collective-permute-start(f32[256,128]{1,0:T(8,128)S(1)} %get-tuple-element.14), channel_id=1, source_target_pairs={{0,8},{4,12},{8,0},{12,4},{16,24},{20,28},{24,16},{28,20},{1,9},{5... | collective-permute-start | bytes 393224 | tf_op jit(solution)/shard_map/ppermute | solution.py:122
  4.8 7.0 %collective-permute-start.1 = (f32[256,128]{1,0:T(8,128)S(1)}, f32[256,128]{1,0:T(8,128)S(1)}, u32[]{:S(2)}, u32[]{:S(2)}) collective-permute-start(f32[256,128]{1,0:T(8,128)S(1)} %get-tuple-element.15), channel_id=1, source_target_pairs={{0,16},{4,20},{1,17},{5,21},{2,18},{6,22},{3,19},{7,23}} | collective-permute-start | bytes 393224 | tf_op jit(solution)/shard_map/ppermute | solution.py:122
  9.3 7.6 %collective-permute-start.4 = (f32[512,128]{1,0:T(8,128)S(1)}, f32[512,128]{1,0:T(8,128)S(1)}, u32[]{:S(2)}, u32[]{:S(2)}) collective-permute-start(f32[512,128]{1,0:T(8,128)S(1)} %bitcast.11), channel_id=1, source_target_pairs={{0,4},{4,0},{8,12},{12,8},{16,20},{20,16},{24,28},{28,24},{1,5},{5... | collective-permute-start | bytes 786440 | tf_op jit(solution)/shard_map/ppermute | solution.py:175
  10.8 3.8 %collective-permute-start.3 = (f32[256,128]{1,0:T(8,128)S(1)}, f32[256,128]{1,0:T(8,128)S(1)}, u32[]{:S(2)}, u32[]{:S(2)}) collective-permute-start(f32[256,128]{1,0:T(8,128)S(1)} %collective-permute-done), channel_id=1, source_target_pairs={{8,24},{12,28},{9,25},{13,29},{10,26},{14,30},{11,27},{15,31}} | collective-permute-start | bytes 393224 | tf_op jit(solution)/shard_map/ppermute | solution.py:122
  11.8 6.8 %collective-permute-start.2 = (f32[256,128]{1,0:T(8,128)S(1)}, f32[256,128]{1,0:T(8,128)S(1)}, u32[]{:S(2)}, u32[]{:S(2)}) collective-permute-start(f32[256,128]{1,0:T(8,128)S(1)} %select_select_fusion.2), channel_id=1, source_target_pairs={{0,8},{4,12},{8,16},{12,20},{16,24},{20,28},{24,0},{28,4},{1,9},{5... | collective-permute-start | bytes 393224 | tf_op jit(solution)/shard_map/ppermute | solution.py:122
  18.7 9.7 %collective-permute-start.10 = (f32[512,128]{1,0:T(8,128)S(1)}, f32[512,128]{1,0:T(8,128)S(1)}, u32[]{:S(2)}, u32[]{:S(2)}) collective-permute-start(f32[512,128]{1,0:T(8,128)S(1)} %pad_maximum_fusion.refs_0_), channel_id=1, source_target_pairs={{6,0},{7,1},{4,2},{5,3},{2,4},{3,5},{0,6},{1,7},{14,8},{15,9},{12,... | collective-permute-start | bytes 786440 | tf_op jit(solution)/shard_map/ppermute | solution.py:162
  21.2 9.9 %collective-permute-start.6 = (f32[512,128]{1,0:T(8,128)S(1)}, f32[512,128]{1,0:T(8,128)S(1)}, u32[]{:S(2)}, u32[]{:S(2)}) collective-permute-start(f32[512,128]{1,0:T(8,128)S(1)} %pad_maximum_fusion.refs_0_), channel_id=1, source_target_pairs={{2,0},{3,1},{0,2},{1,3},{6,4},{7,5},{4,6},{5,7},{10,8},{11,9},{8,1... | collective-permute-start | bytes 786440 | tf_op jit(solution)/shard_map/ppermute | solution.py:162
  21.7 9.5 %collective-permute-start.8 = (f32[512,128]{1,0:T(8,128)S(1)}, f32[512,128]{1,0:T(8,128)S(1)}, u32[]{:S(2)}, u32[]{:S(2)}) collective-permute-start(f32[512,128]{1,0:T(8,128)S(1)} %pad_maximum_fusion.refs_0_), channel_id=1, source_target_pairs={{4,0},{5,1},{6,2},{7,3},{0,4},{1,5},{2,6},{3,7},{12,8},{13,9},{14,... | collective-permute-start | bytes 786440 | tf_op jit(solution)/shard_map/ppermute | solution.py:162
  22.2 9.4 %collective-permute-start.12 = (f32[512,128]{1,0:T(8,128)S(1)}, f32[512,128]{1,0:T(8,128)S(1)}, u32[]{:S(2)}, u32[]{:S(2)}) collective-permute-start(f32[512,128]{1,0:T(8,128)S(1)} %collective-permute-done.4), channel_id=1, source_target_pairs={{0,8},{8,16},{16,24},{1,9},{9,17},{17,25},{2,10},{10,18},{18,26},{... | collective-permute-start | bytes 786440 | tf_op jit(solution)/shard_map/ppermute | solution.py:179
  25.1 6.5 %collective-permute-start.5 = (f32[512,128]{1,0:T(8,128)S(1)}, f32[512,128]{1,0:T(8,128)S(1)}, u32[]{:S(2)}, u32[]{:S(2)}) collective-permute-start(f32[512,128]{1,0:T(8,128)S(1)} %pad_maximum_fusion.refs_0_), channel_id=1, source_target_pairs={{0,1},{1,0},{2,3},{3,2},{4,5},{5,4},{6,7},{7,6},{8,9},{9,8},{10,11... | collective-permute-start | bytes 786440 | tf_op jit(solution)/shard_map/ppermute | solution.py:164
  28.4 3.3 %collective-permute-start.11 = (f32[512,128]{1,0:T(8,128)S(1)}, f32[512,128]{1,0:T(8,128)S(1)}, u32[]{:S(2)}, u32[]{:S(2)}) collective-permute-start(f32[512,128]{1,0:T(8,128)S(1)} %collective-permute-done.10.refs_6_), channel_id=1, source_target_pairs={{0,1},{1,0},{2,3},{3,2},{4,5},{5,4},{6,7},{7,6},{8,9},{9,8},{10,11... | collective-permute-start | bytes 786440 | tf_op jit(solution)/shard_map/ppermute | solution.py:164
  31.1 1.5 %collective-permute-start.7 = (f32[512,128]{1,0:T(8,128)S(1)}, f32[512,128]{1,0:T(8,128)S(1)}, u32[]{:S(2)}, u32[]{:S(2)}) collective-permute-start(f32[512,128]{1,0:T(8,128)S(1)} %collective-permute-done.6.refs_2_), channel_id=1, source_target_pairs={{0,1},{1,0},{2,3},{3,2},{4,5},{5,4},{6,7},{7,6},{8,9},{9,8},{10,11... | collective-permute-start | bytes 786440 | tf_op jit(solution)/shard_map/ppermute | solution.py:164
  31.2 1.8 %collective-permute-start.9 = (f32[512,128]{1,0:T(8,128)S(1)}, f32[512,128]{1,0:T(8,128)S(1)}, u32[]{:S(2)}, u32[]{:S(2)}) collective-permute-start(f32[512,128]{1,0:T(8,128)S(1)} %collective-permute-done.8.refs_4_), channel_id=1, source_target_pairs={{0,1},{1,0},{2,3},{3,2},{4,5},{5,4},{6,7},{7,6},{8,9},{9,8},{10,11... | collective-permute-start | bytes 786440 | tf_op jit(solution)/shard_map/ppermute | solution.py:164
  31.6 1.4 %copy-start = (f32[512,1,128]{2,1,0:T(1,128)S(1)}, f32[512,1,128]{2,1,0:T(1,128)}, u32[]{:S(2)}) copy-start(f32[512,1,128]{2,1,0:T(1,128)} %param.3) | copy-start | bytes 786436
